TPU v7x, 512 devices: a whole 4x4x16 slice. The times are simulated.
512 devices in a mesh: gx: 32 (over x, y, core), gy: 4 (over z_hi), gz: 4 (over z_lo).
Axes of the slice: x: 4, y: 4, z: 16 (z_hi: 4, z_lo: 4; z = z_hi * 4 + z_lo), core: 2. Of those that a mesh axis runs over, the one named last changes fastest.
Arguments:
- feats: bfloat16 [65536, 128], P(('gx', 'gy', 'gz')), may hold values from -6 to 6
- coords: float32 [3, 65536], P(None, ('gx', 'gy', 'gz')), may hold values from 0 to 1, as said below
- pair_dist: float32 [65536, 64], P(('gx', 'gy', 'gz')), may hold values from 0.9 to 5
- nbr_index: int32 [65536, 64], P(('gx', 'gy', 'gz')), may hold values from 0 to 703, as said below
- nbr_count: int32 [65536], P(('gx', 'gy', 'gz')), may hold values from 8 to 64
- send_x: int32 [2, 32768], P(None, ('gx', 'gy', 'gz')), may hold values from 0 to 127, as said below
- send_y: int32 [2, 49152], P(None, ('gx', 'gy', 'gz')), may hold values from 0 to 255, as said below
- send_z: int32 [2, 65536], P(None, ('gx', 'gy', 'gz')), may hold values from 0 to 447, as said below
- w_one: bfloat16 [128, 128], replicated, may hold values from -0.5 to 0.5
- w_two: bfloat16 [128, 128], replicated, may hold values from -0.5 to 0.5
- w_radial: bfloat16 [20, 128], replicated, may hold values from -1.25 to 1.25
- w_charge: bfloat16 [128, 32], replicated, may hold values from -0.5 to 0.5
- k_kernel: float32 [1024, 32], replicated, may hold values from 0.2 to 2
- w_ewald: bfloat16 [32, 128], replicated, may hold values from -1 to 1
Outputs:
- update: bfloat16 [65536, 128], P(('gx', 'gy', 'gz'))
Inputs may be any that keep to these rules, and one draw needn't show every extreme that they name: Each subdomain's atoms lie in its box: coords[0] of subdomain (a, b, c) is within a / 32 and (a + 1) / 32, likewise for the other two. `nbr_index`: entries are rows of the atom's subdomain table; entries at slots nbr_count[i] and beyond are padding. `send_x`: within one row of a subdomain's columns no entry repeats. `send_y`: within one row of a subdomain's columns no entry repeats. `send_z`: within one row of a subdomain's columns no entry repeats.
All inputs are finite; a program needn't handle non-finite values.
Results may differ from a plain program's by a relative error of at most 0.009.
Values may be sent and summed in bfloat16 or wider, within the bound.
No kernel may reach another device: no remote copies, remote signals or barrier semaphores. Data moves between devices by JAX's collectives and lax.ppermute only.
A program may use at most 64 MiB of HBM per device.

v0:
```python
import math

import jax
import jax.numpy as jnp
from jax import lax
from jax.sharding import PartitionSpec as P

cutoff = 5.0
pair_scale = 0.25


def with_halo(block, sides, width):
    for axis, dim in sides:
        count = lax.axis_size(axis)
        forward = [(i, i + 1) for i in range(count - 1)]
        forward.append((count - 1, 0))
        backward = [(target, source) for source, target in forward]
        low = lax.ppermute(
            lax.slice_in_dim(block, block.shape[dim] - width, None, axis=dim), axis, forward
        )
        high = lax.ppermute(lax.slice_in_dim(block, 0, width, axis=dim), axis, backward)
        block = jnp.concatenate([low, block, high], axis=dim)
    return block


def wave_numbers(total):
    k_index = jnp.arange(total, dtype=jnp.int32)
    along_third = (k_index % 8 + 1).astype(jnp.float32)
    along_second = (k_index // 8 % 8 - 4).astype(jnp.float32)
    along_first = (k_index // 64 - total // 64 // 2).astype(jnp.float32)
    return (along_first, along_second, along_third)


def trig_tables(coords, total):
    along_first, along_second, along_third = wave_numbers(total)
    phase = (
        along_first[:, None] * coords[0][None, :]
        + along_second[:, None] * coords[1][None, :]
        + along_third[:, None] * coords[2][None, :]
    )
    angle = 2.0 * math.pi * phase
    return (jnp.cos(angle).astype(jnp.bfloat16), jnp.sin(angle).astype(jnp.bfloat16))


def pair_filter(distance, w_radial):
    orders = jnp.arange(1, w_radial.shape[0] + 1, dtype=jnp.int32).astype(jnp.float32)
    radial_basis = (
        jnp.sin(orders[:, None] * (math.pi / cutoff) * distance[None, :]) / distance[None, :]
    ).astype(jnp.bfloat16)
    radial = lax.dot_general(
        radial_basis, w_radial, (((0,), (0,)), ((), ())), preferred_element_type=jnp.float32
    )
    envelope = 0.5 * (jnp.cos(math.pi / cutoff * distance) + 1.0)
    return (radial * envelope[:, None]).astype(jnp.bfloat16)


def message_base(feats, w_one, w_two):
    hidden = jax.nn.silu(jnp.dot(feats, w_one, preferred_element_type=jnp.float32)).astype(
        jnp.bfloat16
    )
    return jnp.dot(hidden, w_two, preferred_element_type=jnp.float32).astype(jnp.bfloat16)


def charges_of(feats, w_charge):
    return lax.dot_general(
        w_charge, feats, (((0,), (1,)), ((), ())), preferred_element_type=jnp.float32
    ).astype(jnp.bfloat16)


def structure_terms(cos_table, sin_table, charge_t):
    real_part = lax.dot_general(
        cos_table, charge_t, (((1,), (1,)), ((), ())), preferred_element_type=jnp.float32
    )
    imag_part = lax.dot_general(
        sin_table, charge_t, (((1,), (1,)), ((), ())), preferred_element_type=jnp.float32
    )
    return jnp.concatenate([real_part, imag_part], axis=1)


def potential(factors, cos_table, sin_table, total):
    channels = factors.shape[1] // 2
    real_part = lax.dot_general(
        factors[:, :channels],
        cos_table,
        (((0,), (0,)), ((), ())),
        preferred_element_type=jnp.float32,
    )
    imag_part = lax.dot_general(
        factors[:, channels:],
        sin_table,
        (((0,), (0,)), ((), ())),
        preferred_element_type=jnp.float32,
    )
    return ((real_part + imag_part) * (1.0 / math.sqrt(total))).astype(jnp.bfloat16)


def selector(indices, width):
    return (indices[:, None] == lax.broadcasted_iota(jnp.int32, (1, width), 1)).astype(jnp.bfloat16)


def trade_first(packet):
    return with_halo(packet, (("gx", 0),), packet.shape[0] // 2)


def trade_second(packet):
    return with_halo(packet, (("gy", 0),), packet.shape[0] // 2)


def trade_third(packet):
    return with_halo(packet, (("gz", 0),), packet.shape[0] // 2)


def extend(ext_table, trader, send_rows):
    rim_rows = send_rows.shape[1]
    picker = selector(send_rows.reshape(-1), ext_table.shape[0])
    packet = jnp.dot(picker, ext_table, preferred_element_type=jnp.float32).astype(ext_table.dtype)
    arrived = trader(packet)
    return jnp.concatenate([ext_table, arrived[:rim_rows], arrived[3 * rim_rows :]], axis=0)


def on_device(
    feats,
    coords,
    pair_dist,
    nbr_index,
    nbr_count,
    send_x,
    send_y,
    send_z,
    w_one,
    w_two,
    w_radial,
    w_charge,
    k_kernel,
    w_ewald,
):
    atom_count, feature_count = feats.shape
    slot_count = pair_dist.shape[1]
    sections = (
        (trade_first, send_x, atom_count),
        (trade_second, send_y, atom_count + 2 * send_x.shape[1]),
        (trade_third, send_z, atom_count + 2 * send_x.shape[1] + 2 * send_y.shape[1]),
    )
    base_ext = message_base(feats, w_one, w_two)
    for trader, send_rows, offset in sections:
        base_ext = extend(base_ext, trader, send_rows)
    ext_rows = base_ext.shape[0]
    block_atoms = math.gcd(atom_count, 16)
    block_count = atom_count // block_atoms
    block_pairs = block_atoms * slot_count
    filled_all = lax.broadcasted_iota(jnp.int32, (atom_count, slot_count), 1) < nbr_count[:, None]
    column_ids = lax.broadcasted_iota(jnp.int32, (1, ext_rows), 1)

    def pair_block(block_step, loop_state):
        gathered, spread = loop_state
        first_row = block_step * block_atoms
        distance = lax.dynamic_slice_in_dim(pair_dist, first_row, block_atoms, 0).reshape(-1)
        partner = lax.dynamic_slice_in_dim(nbr_index, first_row, block_atoms, 0).reshape(-1)
        filled = lax.dynamic_slice_in_dim(filled_all, first_row, block_atoms, 0).reshape(-1)
        picker = ((partner[:, None] == column_ids) & filled[:, None]).astype(jnp.bfloat16)
        radial_terms = pair_filter(distance, w_radial).astype(jnp.float32)
        partner_rows = jnp.dot(picker, base_ext, preferred_element_type=jnp.float32)
        inward = partner_rows * radial_terms
        block_total = jnp.sum(inward.reshape(block_atoms, slot_count, feature_count), axis=1)
        gathered = lax.dynamic_update_slice_in_dim(gathered, block_total, first_row, 0)
        own_rows = lax.dynamic_slice_in_dim(base_ext, first_row, block_atoms, 0).astype(jnp.float32)
        outward = (
            radial_terms.reshape(block_atoms, slot_count, feature_count) * own_rows[:, None, :]
        ).reshape(block_pairs, feature_count)
        spread = spread + lax.dot_general(
            picker.astype(jnp.float32),
            outward,
            (((0,), (0,)), ((), ())),
            precision=lax.Precision.HIGHEST,
            preferred_element_type=jnp.float32,
        )
        return (gathered, spread)

    start_state = (
        jnp.zeros((atom_count, feature_count), jnp.float32),
        jnp.zeros((ext_rows, feature_count), jnp.float32),
    )
    gathered, spread = lax.fori_loop(0, block_count, pair_block, start_state)
    for trader, send_rows, offset in reversed(sections):
        rim_rows = send_rows.shape[1]
        back_rows = trader(spread[offset : offset + 2 * rim_rows].astype(jnp.bfloat16))
        incoming = jnp.concatenate([back_rows[:rim_rows], back_rows[3 * rim_rows :]], axis=0)
        targets = jnp.concatenate([send_rows[1], send_rows[0]], axis=0)
        placer = selector(targets, offset)
        spread = spread[:offset] + lax.dot_general(
            placer, incoming, (((0,), (0,)), ((), ())), preferred_element_type=jnp.float32
        )
    pair_update = (gathered + spread) * pair_scale
    total_vectors = k_kernel.shape[0]
    cos_table, sin_table = trig_tables(coords, total_vectors)
    charge_t = charges_of(feats, w_charge)
    subdomain_count = lax.axis_size("gx") * lax.axis_size("gy") * lax.axis_size("gz")
    norm_factor = 1.0 / math.sqrt(atom_count * subdomain_count)
    doubled = jnp.concatenate([k_kernel, k_kernel], axis=1)
    structure = lax.psum(structure_terms(cos_table, sin_table, charge_t), ("gx", "gy", "gz"))
    factors = (structure * doubled * norm_factor).astype(jnp.bfloat16)
    field = potential(factors, cos_table, sin_table, total_vectors)
    ewald_update = lax.dot_general(
        field, w_ewald, (((0,), (0,)), ((), ())), preferred_element_type=jnp.float32
    )
    return (pair_update + ewald_update).astype(jnp.bfloat16)


def solution(mesh):
    in_specs = (
        P(("gx", "gy", "gz"), None),
        P(None, ("gx", "gy", "gz")),
        P(("gx", "gy", "gz"), None),
        P(("gx", "gy", "gz"), None),
        P(("gx", "gy", "gz")),
        P(None, ("gx", "gy", "gz")),
        P(None, ("gx", "gy", "gz")),
        P(None, ("gx", "gy", "gz")),
        P(),
        P(),
        P(),
        P(),
        P(),
        P(),
    )
    out_specs = P(("gx", "gy", "gz"), None)
    return jax.shard_map(
        on_device, mesh=mesh, in_specs=in_specs, out_specs=out_specs, check_vma=False
    )
```

profile of v0, /device:TPU:1, one launch (start us, length us, event | category | flops | bytes accessed | tf_op | source)
XLA Modules:
  0.0 495.3 jit_solution(5071212108506247247)
XLA Ops:
  6.6 0.8 slice_bitcast_fusion.2
  7.4 0.8 convolution_convert_fusion.4
  8.2 2.1 fusion.30
  10.3 2.0 fusion.32
  12.3 0.7 pad_maximum_fusion
  13.7 4.6 collective-permute-start
  18.3 6.1 %collective-permute-start.1 = (bf16[64,128]{1,0:T(8,128)(2,1)S(1)}, bf16[64,128]{1,0:T(8,128)(2,1)S(1)}, u32[]{:S(2)}, u32[]{:S(2)}) collective-permute-start(bf16[64,128]{1,0:T(8,128)(2,1)S(1)} %get-tuple-element.229), channel_id=1, source_target_pairs={{16,0},{32,16},{48,32},{64,48},{80,64},{96,80},{112,96},{128,112},... | collective-permute-start | bytes 49160 | tf_op jit(solution)/shard_map/ppermute | solution.py:21
  25.4 6.9 %collective-permute-start.2 = (bf16[96,128]{1,0:T(8,128)(2,1)S(1)}, bf16[96,128]{1,0:T(8,128)(2,1)S(1)}, u32[]{:S(2)}, u32[]{:S(2)}) collective-permute-start(bf16[96,128]{1,0:T(8,128)(2,1)S(1)} %get-tuple-element.226), channel_id=1, source_target_pairs={{0,4},{4,8},{8,12},{12,0},{1,5},{5,9},{9,13},{13,1},{2,6},{6,10},{... | collective-permute-start | bytes 73736 | tf_op jit(solution)/shard_map/ppermute | solution.py:18
  32.4 5.6 %collective-permute-start.3 = (bf16[96,128]{1,0:T(8,128)(2,1)S(1)}, bf16[96,128]{1,0:T(8,128)(2,1)S(1)}, u32[]{:S(2)}, u32[]{:S(2)}) collective-permute-start(bf16[96,128]{1,0:T(8,128)(2,1)S(1)} %get-tuple-element.225), channel_id=1, source_target_pairs={{4,0},{8,4},{12,8},{0,12},{5,1},{9,5},{13,9},{1,13},{6,2},{10,6},{... | collective-permute-start | bytes 73736 | tf_op jit(solution)/shard_map/ppermute | solution.py:21
  38.0 4.4 collective-permute-done.3
  42.7 2.6 collective-permute-start.4
  45.7 4.4 collective-permute-start.5
  50.1 1.0 collective-permute-done.5
  51.1 42.2 %while.16 = (s32[]{:T(128)}, f32[128,128]{1,0:T(8,128)S(1)}, f32[704,128]{1,0:T(8,128)S(1)}, s32[128,64]{1,0:T(8,128)S(1)}, pred[128,64]{1,0:T(8,128)(4,1)S(1)},...) while((s32[]{:T(128)}, f32[128,128]{1,0:T(8,128)S(1)}, ...), condition=%wide.region_2.3_spmd.clone, body=%wide.region_0.2_spmd.clone.sunk | while | flops 1301003264 | bytes 3112330 | solution.py:183
  51.3 0.7 bitcast_multiply_fusion.2
  52.2 1.2 bitcast_reduce_fusion.2
  53.4 3.0 fusion.118
  56.6 0.7 bitcast_multiply_fusion.2
  57.5 1.2 bitcast_reduce_fusion.2
  58.7 3.0 fusion.118
  61.9 0.7 bitcast_multiply_fusion.2
  62.7 1.2 bitcast_reduce_fusion.2
  63.9 3.0 fusion.118
  67.2 0.7 bitcast_multiply_fusion.2
  68.0 1.2 bitcast_reduce_fusion.2
  69.2 3.0 fusion.118
  72.4 0.7 bitcast_multiply_fusion.2
  73.3 1.2 bitcast_reduce_fusion.2
  74.5 3.0 fusion.118
  77.7 0.7 bitcast_multiply_fusion.2
  78.6 1.2 bitcast_reduce_fusion.2
  79.8 3.0 fusion.118
  83.0 0.7 bitcast_multiply_fusion.2
  83.9 1.2 bitcast_reduce_fusion.2
  85.0 3.0 fusion.118
  89.1 1.2 bitcast_reduce_fusion.2
  90.3 3.0 fusion.118
  93.4 5.7 %collective-permute-start.7 = (bf16[128,128]{1,0:T(8,128)(2,1)S(1)}, bf16[128,128]{1,0:T(8,128)(2,1)S(1)}, u32[]{:S(2)}, u32[]{:S(2)}) collective-permute-start(bf16[128,128]{1,0:T(8,128)(2,1)S(1)} %get-tuple-element.218), channel_id=1, source_target_pairs={{1,0},{2,1},{3,2},{0,3},{5,4},{6,5},{7,6},{4,7},{9,8},{10,9},{11,1... | collective-permute-start | bytes 98312 | tf_op jit(solution)/shard_map/ppermute | solution.py:21
  99.1 1.9 collective-permute-start.6
  101.1 4.6 collective-permute-done.6
  106.2 3.8 collective-permute-start.9
  110.0 5.5 %collective-permute-start.8 = (bf16[96,128]{1,0:T(8,128)(2,1)S(1)}, bf16[96,128]{1,0:T(8,128)(2,1)S(1)}, u32[]{:S(2)}, u32[]{:S(2)}) collective-permute-start(bf16[96,128]{1,0:T(8,128)(2,1)S(1)} %get-tuple-element.219), channel_id=1, source_target_pairs={{0,4},{4,8},{8,12},{12,0},{1,5},{5,9},{9,13},{13,1},{2,6},{6,10},{... | collective-permute-start | bytes 73736 | tf_op jit(solution)/shard_map/ppermute | solution.py:18
  115.5 359.3 %all-reduce.2.cloned.1.call-done = f32[1024,64]{0,1:T(8,128)} async-done(((f32[1024,64]{0,1:T(8,128)}), f32[1024,64]{0,1:T(8,128)}) %all-reduce.2.cloned.1.call-update) | async-done | bytes 262160 | tf_op jit(solution)/shard_map/psum | solution.py:200
  474.8 1.0 fusion.26
  476.1 3.8 collective-permute-start.11
  480.0 3.2 collective-permute-start.10
  483.2 2.0 fusion.31
  485.5 2.9 fusion.21
  (151 shorter events, 6.6 us)
Async XLA Ops:
  6.5 0.8 copy-start
  6.5 468.2 %all-reduce.2.cloned.1.call-start = ((), (), s32[]{:S(2)}) async-start(), calls=%async_computation | async-start | bytes 524288 | tf_op jit(solution)/shard_map/psum | solution.py:200
  12.3 0.8 copy-start.6
  12.3 0.9 copy-start.9
  12.3 0.9 copy-start.10
  13.0 11.4 %copy-start.8 = (s32[128]{0:T(128)S(1)}, s32[128]{0:T(128)}, u32[]{:S(2)}) copy-start(s32[128]{0:T(128)} %param.20) | copy-start | bytes 1540
  13.1 11.5 %copy-start.7 = (s32[2,128]{1,0:T(2,128)S(1)}, s32[2,128]{1,0:T(2,128)}, u32[]{:S(2)}) copy-start(s32[2,128]{1,0:T(2,128)} %param.23) | copy-start | bytes 3076
  13.1 11.5 %copy-start.5 = (s32[2,96]{1,0:T(2,128)S(1)}, s32[2,96]{1,0:T(2,128)}, u32[]{:S(2)}) copy-start(s32[2,96]{1,0:T(2,128)} %param.22) | copy-start | bytes 2308
  13.7 11.0 %collective-permute-start = (bf16[64,128]{1,0:T(8,128)(2,1)S(1)}, bf16[64,128]{1,0:T(8,128)(2,1)S(1)}, u32[]{:S(2)}, u32[]{:S(2)}) collective-permute-start(bf16[64,128]{1,0:T(8,128)(2,1)S(1)} %get-tuple-element.230), channel_id=1, source_target_pairs={{0,16},{16,32},{32,48},{48,64},{64,80},{80,96},{96,112},{112,128},... | collective-permute-start | bytes 49160 | tf_op jit(solution)/shard_map/ppermute | solution.py:18
  18.3 6.9 %collective-permute-start.1 = (bf16[64,128]{1,0:T(8,128)(2,1)S(1)}, bf16[64,128]{1,0:T(8,128)(2,1)S(1)}, u32[]{:S(2)}, u32[]{:S(2)}) collective-permute-start(bf16[64,128]{1,0:T(8,128)(2,1)S(1)} %get-tuple-element.229), channel_id=1, source_target_pairs={{16,0},{32,16},{48,32},{64,48},{80,64},{96,80},{112,96},{128,112},... | collective-permute-start | bytes 49160 | tf_op jit(solution)/shard_map/ppermute | solution.py:21
  24.7 20.8 %copy-start.3 = (s32[128,64]{0,1:T(8,128)S(1)}, s32[128,64]{0,1:T(8,128)}, u32[]{:S(2)}) copy-start(s32[128,64]{0,1:T(8,128)} %param.19) | copy-start | bytes 98308
  24.7 20.9 %copy-start.4 = (f32[128,64]{0,1:T(8,128)S(1)}, f32[128,64]{0,1:T(8,128)}, u32[]{:S(2)}) copy-start(f32[128,64]{0,1:T(8,128)} %param.18) | copy-start | bytes 98308
  25.4 12.6 %collective-permute-start.2 = (bf16[96,128]{1,0:T(8,128)(2,1)S(1)}, bf16[96,128]{1,0:T(8,128)(2,1)S(1)}, u32[]{:S(2)}, u32[]{:S(2)}) collective-permute-start(bf16[96,128]{1,0:T(8,128)(2,1)S(1)} %get-tuple-element.226), channel_id=1, source_target_pairs={{0,4},{4,8},{8,12},{12,0},{1,5},{5,9},{9,13},{13,1},{2,6},{6,10},{... | collective-permute-start | bytes 73736 | tf_op jit(solution)/shard_map/ppermute | solution.py:18
  32.4 10.0 %collective-permute-start.3 = (bf16[96,128]{1,0:T(8,128)(2,1)S(1)}, bf16[96,128]{1,0:T(8,128)(2,1)S(1)}, u32[]{:S(2)}, u32[]{:S(2)}) collective-permute-start(bf16[96,128]{1,0:T(8,128)(2,1)S(1)} %get-tuple-element.225), channel_id=1, source_target_pairs={{4,0},{8,4},{12,8},{0,12},{5,1},{9,5},{13,9},{1,13},{6,2},{10,6},{... | collective-permute-start | bytes 73736 | tf_op jit(solution)/shard_map/ppermute | solution.py:21
  38.0 13.2 %copy-start.1 = (bf16[20,128]{1,0:T(8,128)(2,1)S(1)}, bf16[20,128]{1,0:T(8,128)(2,1)}, u32[]{:S(2)}) copy-start(bf16[20,128]{1,0:T(8,128)(2,1)} %param.26) | copy-start | bytes 15364
  42.7 7.4 %collective-permute-start.4 = (bf16[128,128]{1,0:T(8,128)(2,1)S(1)}, bf16[128,128]{1,0:T(8,128)(2,1)S(1)}, u32[]{:S(2)}, u32[]{:S(2)}) collective-permute-start(bf16[128,128]{1,0:T(8,128)(2,1)S(1)} %get-tuple-element.224), channel_id=1, source_target_pairs={{0,1},{1,2},{2,3},{3,0},{4,5},{5,6},{6,7},{7,4},{8,9},{9,10},{10,1... | collective-permute-start | bytes 98312 | tf_op jit(solution)/shard_map/ppermute | solution.py:18
  45.7 5.4 %collective-permute-start.5 = (bf16[128,128]{1,0:T(8,128)(2,1)S(1)}, bf16[128,128]{1,0:T(8,128)(2,1)S(1)}, u32[]{:S(2)}, u32[]{:S(2)}) collective-permute-start(bf16[128,128]{1,0:T(8,128)(2,1)S(1)} %get-tuple-element.223), channel_id=1, source_target_pairs={{1,0},{2,1},{3,2},{0,3},{5,4},{6,5},{7,6},{4,7},{9,8},{10,9},{11,1... | collective-permute-start | bytes 98312 | tf_op jit(solution)/shard_map/ppermute | solution.py:21
  93.4 381.4 %copy-start.2 = (f32[1024,32]{0,1:T(8,128)S(1)}, f32[1024,32]{0,1:T(8,128)}, u32[]{:S(2)}) copy-start(f32[1024,32]{0,1:T(8,128)} %param.28) | copy-start | bytes 393220
  93.4 7.7 %collective-permute-start.7 = (bf16[128,128]{1,0:T(8,128)(2,1)S(1)}, bf16[128,128]{1,0:T(8,128)(2,1)S(1)}, u32[]{:S(2)}, u32[]{:S(2)}) collective-permute-start(bf16[128,128]{1,0:T(8,128)(2,1)S(1)} %get-tuple-element.218), channel_id=1, source_target_pairs={{1,0},{2,1},{3,2},{0,3},{5,4},{6,5},{7,6},{4,7},{9,8},{10,9},{11,1... | collective-permute-start | bytes 98312 | tf_op jit(solution)/shard_map/ppermute | solution.py:21
  99.1 6.6 %collective-permute-start.6 = (bf16[128,128]{1,0:T(8,128)(2,1)S(1)}, bf16[128,128]{1,0:T(8,128)(2,1)S(1)}, u32[]{:S(2)}, u32[]{:S(2)}) collective-permute-start(bf16[128,128]{1,0:T(8,128)(2,1)S(1)} %get-tuple-element.217), channel_id=1, source_target_pairs={{0,1},{1,2},{2,3},{3,0},{4,5},{5,6},{6,7},{7,4},{8,9},{9,10},{10,1... | collective-permute-start | bytes 98312 | tf_op jit(solution)/shard_map/ppermute | solution.py:18
  106.2 369.6 %collective-permute-start.9 = (bf16[96,128]{1,0:T(8,128)(2,1)S(1)}, bf16[96,128]{1,0:T(8,128)(2,1)S(1)}, u32[]{:S(2)}, u32[]{:S(2)}) collective-permute-start(bf16[96,128]{1,0:T(8,128)(2,1)S(1)} %get-tuple-element.220), channel_id=1, source_target_pairs={{4,0},{8,4},{12,8},{0,12},{5,1},{9,5},{13,9},{1,13},{6,2},{10,6},{... | collective-permute-start | bytes 73736 | tf_op jit(solution)/shard_map/ppermute | solution.py:21
  110.0 365.8 %collective-permute-start.8 = (bf16[96,128]{1,0:T(8,128)(2,1)S(1)}, bf16[96,128]{1,0:T(8,128)(2,1)S(1)}, u32[]{:S(2)}, u32[]{:S(2)}) collective-permute-start(bf16[96,128]{1,0:T(8,128)(2,1)S(1)} %get-tuple-element.219), channel_id=1, source_target_pairs={{0,4},{4,8},{8,12},{12,0},{1,5},{5,9},{9,13},{13,1},{2,6},{6,10},{... | collective-permute-start | bytes 73736 | tf_op jit(solution)/shard_map/ppermute | solution.py:18
  476.1 9.1 %collective-permute-start.11 = (bf16[64,128]{1,0:T(8,128)(2,1)S(1)}, bf16[64,128]{1,0:T(8,128)(2,1)S(1)}, u32[]{:S(2)}, u32[]{:S(2)}) collective-permute-start(bf16[64,128]{1,0:T(8,128)(2,1)S(1)} %get-tuple-element.222), channel_id=1, source_target_pairs={{16,0},{32,16},{48,32},{64,48},{80,64},{96,80},{112,96},{128,112},... | collective-permute-start | bytes 49160 | tf_op jit(solution)/shard_map/ppermute | solution.py:21
  480.0 5.6 %copy-start.11 = (bf16[32,128]{1,0:T(8,128)(2,1)S(1)}, bf16[32,128]{1,0:T(8,128)(2,1)}, u32[]{:S(2)}) copy-start(bf16[32,128]{1,0:T(8,128)(2,1)} %param.29) | copy-start | bytes 24580
  480.0 5.3 %collective-permute-start.10 = (bf16[64,128]{1,0:T(8,128)(2,1)S(1)}, bf16[64,128]{1,0:T(8,128)(2,1)S(1)}, u32[]{:S(2)}, u32[]{:S(2)}) collective-permute-start(bf16[64,128]{1,0:T(8,128)(2,1)S(1)} %get-tuple-element.221), channel_id=1, source_target_pairs={{0,16},{16,32},{32,48},{48,64},{64,80},{80,96},{96,112},{112,128},... | collective-permute-start | bytes 49160 | tf_op jit(solution)/shard_map/ppermute | solution.py:18
Sparse Core Ops, SparseCore 0:
  13.2 461.5 all-reduce.1
where the time goes:
time: 498 us; the launch traced here: 495 us
  waiting for transfers between devices  370 us (74%)
  starting transfers between devices  54.2 us (11%)
  matrix products  50.7 us (10%)
  between operations  13.8 us (3%)
    psum x1, waiting for transfers between devices, on_device(): lax.psum(structure_terms(cos_table, sin_table, charge_t), ('gx', 'gy', 'g...  359 us
    ppermute x6, starting transfers between devices, with_halo(): lax.ppermute(lax.slice_in_dim(block, 0, width, axis=dim), axis, backward)  29.5 us
    ppermute x6, starting transfers between devices, with_halo(): lax.ppermute(lax.slice_in_dim(block, block.shape[dim] - width, None, axis...  24.8 us
    dot_general x8, matrix products, pair_block(): lax.dot_general(picker.astype(jnp.float32), outward, (((0,), (0,)), ((),...  24.2 us
  transfers between devices with their start and end apart: 13, of which 5 were waited for; matrix products, arithmetic and copies ran while one was open for 9% of the time, Pallas kernels for 0%

commit v1 on v0

v1 whole, which is shorter than its diff:
```python
import math

import jax
import jax.numpy as jnp
from jax import lax
from jax.experimental import pallas as pl
from jax.experimental.pallas import tpu as pltpu
from jax.sharding import PartitionSpec as P

cutoff = 5.0
pair_scale = 0.25
basis_rows = 32
slot_group = 4
gather_group = 8
mebi = 1024 * 1024


def kernel_call(body, outs, operands, flops, limit, scratch=(), scalars=0):
    specs = [pl.BlockSpec(memory_space=pltpu.SMEM)] * scalars
    specs += [pl.BlockSpec(memory_space=pltpu.VMEM)] * (len(operands) - scalars)
    moved = sum(math.prod(v.shape) * v.dtype.itemsize for v in (*operands, *outs))
    return pl.pallas_call(
        body,
        out_shape=tuple(outs),
        in_specs=specs,
        out_specs=(pl.BlockSpec(memory_space=pltpu.VMEM),) * len(outs),
        scratch_shapes=list(scratch),
        compiler_params=pltpu.CompilerParams(vmem_limit_bytes=limit * mebi),
        cost_estimate=pl.CostEstimate(flops=flops, bytes_accessed=moved, transcendentals=0),
    )(*operands)


def like(shape, dtype):
    return jax.ShapeDtypeStruct(shape, dtype)


def dot32(left, right):
    return jnp.dot(left, right, preferred_element_type=jnp.float32)


def picked(send, side, table):
    columns = jnp.concatenate([send] * 4, axis=0).T[:, side : side + 1]
    lanes = lax.broadcasted_iota(jnp.int32, (send.shape[1], table.shape[0]), 1)
    return dot32((columns == lanes).astype(jnp.bfloat16), table).astype(jnp.bfloat16)


def placed(send, below, above, rows):
    iota = lax.broadcasted_iota(jnp.int32, (rows, send.shape[1]), 0)
    low = dot32((iota == send[1:2]).astype(jnp.bfloat16), below)
    return low + dot32((iota == send[0:1]).astype(jnp.bfloat16), above)


def base_body(feats_ref, one_ref, two_ref, send_ref, base_ref, low_ref, high_ref):
    raw = dot32(feats_ref[...], one_ref[...])
    hidden = (raw / (1.0 + jnp.exp(-raw))).astype(jnp.bfloat16)
    base = dot32(hidden, two_ref[...]).astype(jnp.bfloat16)
    base_ref[...] = base
    low_ref[...] = picked(send_ref[...], 0, base)
    high_ref[...] = picked(send_ref[...], 1, base)


def extend_body(*refs):
    *parts, send_ref, low_ref, high_ref = refs
    table = jnp.concatenate([part[...] for part in parts], axis=0)
    low_ref[...] = picked(send_ref[...], 0, table)
    high_ref[...] = picked(send_ref[...], 1, table)


def fold_body(spread_ref, below_ref, above_ref, send_ref, core_ref, low_ref, high_ref):
    rows = spread_ref.shape[0]
    keep = core_ref.shape[0]
    half = low_ref.shape[0]
    total = spread_ref[...] + placed(send_ref[...], below_ref[...], above_ref[...], rows)
    core_ref[...] = total[:keep]
    low_ref[...] = total[keep : keep + half].astype(jnp.bfloat16)
    high_ref[...] = total[keep + half :].astype(jnp.bfloat16)


def unit_waves(coord, first, count):
    orders = (lax.broadcasted_iota(jnp.int32, (count, coord.shape[1]), 0) + first).astype(jnp.float32)
    turns = orders * coord
    angle = (2.0 * math.pi) * (turns - jnp.round(turns))
    return jnp.cos(angle), jnp.sin(angle)


def outer_waves(left, right):
    left_cos, left_sin = (v[:, None, :] for v in left)
    right_cos, right_sin = (v[None, :, :] for v in right)
    shape = (left_cos.shape[0] * right_cos.shape[1], left_cos.shape[2])
    cos_part = (left_cos * right_cos - left_sin * right_sin).reshape(shape)
    return cos_part, (left_sin * right_cos + left_cos * right_sin).reshape(shape)


def wave_body(coords_ref, feats_ref, charge_ref, blocks_ref, cos_ref, sin_ref):
    total, atoms = cos_ref.shape
    firsts = total // 64
    coords = coords_ref[...]
    along_first = unit_waves(coords[0:1], -(firsts // 2), firsts)
    along_second = unit_waves(coords[1:2], -4, 8)
    along_third = unit_waves(coords[2:3], 1, 8)
    cos_part, sin_part = outer_waves(outer_waves(along_first, along_second), along_third)
    cos_table = cos_part.astype(jnp.bfloat16)
    sin_table = sin_part.astype(jnp.bfloat16)
    cos_ref[...] = cos_table
    sin_ref[...] = sin_table
    charge_t = dot32(feats_ref[...], charge_ref[...]).T.astype(jnp.bfloat16)
    over_atoms = (((1,), (1,)), ((), ()))
    real = lax.dot_general(charge_t, cos_table, over_atoms, preferred_element_type=jnp.float32)
    imag = lax.dot_general(charge_t, sin_table, over_atoms, preferred_element_type=jnp.float32)
    blocks, height, width = blocks_ref.shape
    both = jnp.concatenate([real, imag], axis=0).astype(blocks_ref.dtype)
    across = total // width
    for block in range(blocks):
        down, along = block // across * height, block % across * width
        blocks_ref[block] = both[down : down + height, along : along + width]


def merge_body(parts_ref, copies_ref):
    total = jnp.sum(parts_ref[...].astype(jnp.float32), axis=0)
    copies_ref[...] = jnp.broadcast_to(total.astype(copies_ref.dtype)[None], copies_ref.shape)


def factor_body(where_ref, parts_ref, kernel_ref, copies_ref, norm_factor):
    blocks, height, width = copies_ref.shape
    across = kernel_ref.shape[0] // width
    down, along = where_ref[0] // across, where_ref[0] % across
    start = pl.multiple_of(along * width, width)
    weights = kernel_ref[pl.ds(start, width), :].T
    weights = jnp.where(down % 2 == 0, weights[:height], weights[height:])
    total = jnp.sum(parts_ref[...].astype(jnp.float32), axis=0)
    factors = (total * weights * norm_factor).astype(copies_ref.dtype)
    copies_ref[...] = jnp.broadcast_to(factors[None], copies_ref.shape)


def spread_body(
    dist_ref, nbr_ref, count_ref, base_ref, wide_ref,
    core_ref, low_ref, high_ref, radial_ref, basis_ref, partner_ref, total_ref,
):
    atoms, slots = dist_ref.shape
    feat = base_ref.shape[1]
    core, half = core_ref.shape[0], low_ref.shape[0]
    distance = dist_ref[...].T
    partner_ref[...] = nbr_ref[...].T
    angle = (math.pi / cutoff) * distance
    turn = jnp.cos(angle)
    listed = lax.broadcasted_iota(jnp.int32, (slots, atoms), 0) < count_ref[...]
    fade = jnp.where(listed, 0.5 * (turn + 1.0), 0.0) / distance
    turn = turn + turn
    basis_ref[...] = jnp.zeros_like(basis_ref)
    before, now = jnp.zeros_like(angle), jnp.sin(angle)
    for order in range(20):
        term = now * fade
        for row in range(0, slots, 8):
            place = pl.ds(row * basis_rows + order, 8, stride=basis_rows)
            basis_ref[place, :] = term[row : row + 8]
        before, now = now, turn * now - before
    total_ref[...] = jnp.zeros_like(total_ref)
    base = base_ref[...]
    iota = lax.broadcasted_iota(jnp.int32, (total_ref.shape[0], atoms), 0)
    group_rows = slot_group * basis_rows

    def step(index, carry):
        start = pl.multiple_of(index * group_rows, group_rows)
        block = basis_ref[pl.ds(start, group_rows), :].T.astype(jnp.bfloat16)
        wide = dot32(block, wide_ref[...]).astype(jnp.bfloat16)
        pickers, outward = [], []
        for offset in range(slot_group):
            slot = index * slot_group + offset
            radial = wide[:, offset * feat : (offset + 1) * feat]
            radial_ref[slot] = radial
            outward.append(radial * base)
            pickers.append((iota == partner_ref[pl.ds(slot, 1), :]).astype(jnp.bfloat16))
        picker = jnp.concatenate(pickers, axis=1)
        total_ref[...] += dot32(picker, jnp.concatenate(outward, axis=0))
        return carry

    lax.fori_loop(0, slots // slot_group, step, 0)
    core_ref[...] = total_ref[:core]
    low_ref[...] = total_ref[core : core + half].astype(jnp.bfloat16)
    high_ref[...] = total_ref[core + half :].astype(jnp.bfloat16)


def gather_body(nbr_ref, radial_ref, *refs):
    *parts, gathered_ref = refs
    atoms, slots = nbr_ref.shape
    table = jnp.concatenate([part[...] for part in parts], axis=0)
    lanes = lax.broadcasted_iota(jnp.int32, (atoms, table.shape[0]), 1)
    spare = jnp.zeros((atoms, 128 - slots), jnp.int32)

    def step(index, state):
        partner, total = state
        for offset in range(gather_group):
            picker = (partner[:, offset : offset + 1] == lanes).astype(jnp.bfloat16)
            rows = dot32(picker, table)
            radial = radial_ref[index * gather_group + offset].astype(jnp.float32)
            total = total + rows * radial
        return pltpu.roll(partner, 128 - gather_group, 1), total

    start = (jnp.concatenate([nbr_ref[...], spare], axis=1), jnp.zeros(gathered_ref.shape, jnp.float32))
    gathered_ref[...] = lax.fori_loop(0, slots // gather_group, step, start)[1]


def update_body(
    spread_ref, below_ref, above_ref, send_ref, gathered_ref, factor_ref, cos_ref, sin_ref, ewald_ref, out_ref
):
    atoms = spread_ref.shape[0]
    returned = spread_ref[...] + placed(send_ref[...], below_ref[...], above_ref[...], atoms)
    pair_update = (gathered_ref[...] + returned) * pair_scale
    total = cos_ref.shape[0]
    blocks, height, width = factor_ref.shape
    across = total // width
    lines = []
    for down in range(blocks // across):
        lines.append(jnp.concatenate([factor_ref[down * across + i] for i in range(across)], axis=1))
    real = dot32(jnp.concatenate(lines[: len(lines) // 2], axis=0), cos_ref[...])
    imag = dot32(jnp.concatenate(lines[len(lines) // 2 :], axis=0), sin_ref[...])
    field = ((real + imag) * (1.0 / math.sqrt(total))).T.astype(jnp.bfloat16)
    out_ref[...] = (pair_update + dot32(field, ewald_ref[...])).astype(out_ref.dtype)


def swap(low, high, axis):
    count = lax.axis_size(axis)
    forward = [(i, (i + 1) % count) for i in range(count)]
    backward = [(target, source) for source, target in forward]
    return lax.ppermute(high, axis, forward), lax.ppermute(low, axis, backward)


def on_device(
    feats,
    coords,
    pair_dist,
    nbr_index,
    nbr_count,
    send_x,
    send_y,
    send_z,
    w_one,
    w_two,
    w_radial,
    w_charge,
    k_kernel,
    w_ewald,
):
    atoms, feat = feats.shape
    slots = pair_dist.shape[1]
    charges = w_charge.shape[1]
    total = k_kernel.shape[0]
    rim_x, rim_y, rim_z = send_x.shape[1], send_y.shape[1], send_z.shape[1]
    with_x = atoms + 2 * rim_x
    with_y = with_x + 2 * rim_y
    with_z = with_y + 2 * rim_z
    half, full = jnp.bfloat16, jnp.float32
    count_x = lax.axis_size("gx")
    count_yz = lax.axis_size("gy") * lax.axis_size("gz")
    across = total // 128
    height = 2 * charges * across // count_x

    base, low, high = kernel_call(
        base_body,
        (like((atoms, feat), half), like((rim_x, feat), half), like((rim_x, feat), half)),
        (feats, w_one, w_two, send_x), 10**7, 8,
    )
    below_x, above_x = swap(low, high, "gx")
    blocks, cos_table, sin_table = kernel_call(
        wave_body,
        (like((count_x, height, 128), half), like((total, atoms), half), like((total, atoms), half)),
        (coords, feats, w_charge), 10**8, 16,
    )
    parts = lax.all_to_all(blocks, "gx", split_axis=0, concat_axis=0)

    padded = jnp.pad(w_radial, ((0, basis_rows - w_radial.shape[0]), (0, 0)))
    wide = jnp.kron(jnp.eye(slot_group, dtype=half), padded)
    core, low, high, radial = kernel_call(
        spread_body,
        (
            like((with_y, feat), full), like((rim_z, feat), half), like((rim_z, feat), half),
            like((slots, atoms, feat), half),
        ),
        (pair_dist, nbr_index, nbr_count[None, :], base, wide), 3 * 10**9, 24,
        (
            pltpu.VMEM((slots * basis_rows, atoms), full), pltpu.VMEM((slots, atoms), jnp.int32),
            pltpu.VMEM((with_z, feat), full),
        ),
    )
    below, above = swap(low, high, "gz")

    low, high = kernel_call(
        extend_body, (like((rim_y, feat), half),) * 2, (base, below_x, above_x, send_y), 10**7, 8
    )
    below_y, above_y = swap(low, high, "gy")
    (copies,) = kernel_call(
        merge_body, (like((count_yz, height, 128), half),), (parts,), 10**6, 8
    )
    parts = lax.all_to_all(copies, ("gy", "gz"), split_axis=0, concat_axis=0)

    core, low, high = kernel_call(
        fold_body,
        (like((with_x, feat), full), like((rim_y, feat), half), like((rim_y, feat), half)),
        (core, below, above, send_z), 10**7, 8,
    )
    below, above = swap(low, high, "gy")
    low, high = kernel_call(
        extend_body, (like((rim_z, feat), half),) * 2, (base, below_x, above_x, below_y, above_y, send_z), 10**7, 8
    )
    below_z, above_z = swap(low, high, "gz")

    norm_factor = 1.0 / math.sqrt(atoms * count_x * count_yz)
    where = lax.axis_index("gx").astype(jnp.int32)[None]
    (copies,) = kernel_call(
        lambda *refs: factor_body(*refs, norm_factor),
        (like((count_x, height, 128), half),), (where, parts, k_kernel), 10**6, 8, scalars=1,
    )
    factors = lax.all_to_all(copies, "gx", split_axis=0, concat_axis=0)

    core, low, high = kernel_call(
        fold_body,
        (like((atoms, feat), full), like((rim_x, feat), half), like((rim_x, feat), half)),
        (core, below, above, send_y), 10**7, 8,
    )
    below, above = swap(low, high, "gx")
    (gathered,) = kernel_call(
        gather_body, (like((atoms, feat), full),),
        (nbr_index, radial, base, below_x, above_x, below_y, above_y, below_z, above_z), 15 * 10**8, 24,
    )
    (update,) = kernel_call(
        update_body, (like((atoms, feat), half),),
        (core, below, above, send_x, gathered, factors, cos_table, sin_table, w_ewald), 10**8, 16,
    )
    return update


def solution(mesh):
    in_specs = (
        P(("gx", "gy", "gz"), None),
        P(None, ("gx", "gy", "gz")),
        P(("gx", "gy", "gz"), None),
        P(("gx", "gy", "gz"), None),
        P(("gx", "gy", "gz")),
        P(None, ("gx", "gy", "gz")),
        P(None, ("gx", "gy", "gz")),
        P(None, ("gx", "gy", "gz")),
        P(),
        P(),
        P(),
        P(),
        P(),
        P(),
    )
    out_specs = P(("gx", "gy", "gz"), None)
    return jax.shard_map(
        on_device, mesh=mesh, in_specs=in_specs, out_specs=out_specs, check_vma=False
    )
```

time: 498 us -> 131 us (0.26)
  waiting for transfers between devices: 370 us -> 18.6 us
  matrix products: 50.7 us -> 0 us
  starting transfers between devices: 54.2 us -> 78.8 us
  Pallas kernels: 0 us -> 20.5 us
  between operations: 13.8 us -> 0.35 us
  local copies, waits for them, and re-layouts: 3.37 us -> 11.4 us
    psum x1 -> x0, waiting for transfers between devices: 359 us -> none  [on_device(): lax.psum(structure_terms(cos_table, sin_table, charge_t), ('gx', 'gy', 'g...]
    dot_general x36 -> x0, matrix products: 50.7 us -> none  [the longest x8 24.2 us: pair_block(): lax.dot_general(picker.astype(jnp.float32), outward, (((0,), (0,)), ((),...]
    all_to_all x0 -> x3, starting transfers between devices: none -> 26.7 us  [the longest x1 9.7 us: on_device(): parts = lax.all_to_all(copies, ('gy', 'gz'), split_axis=0, concat_axis=0)]
    pallas_call x0 -> x11, Pallas kernels: none -> 20.5 us  [kernel_call(): pl.pallas_call(body, out_shape=tuple(outs), in_specs=specs, out_specs=(pl...]
    unnamed x30 -> x33, local copies, waits for them, and re-layouts: 0.29 us -> 10.7 us
    all_to_all x0 -> x3, waiting for transfers between devices: none -> 6.12 us  [the longest x1 5.23 us: on_device(): parts = lax.all_to_all(blocks, 'gx', split_axis=0, concat_axis=0)]
  transfers between devices with their start and end apart: 13 -> 15, of which waited for: 5 -> 4; matrix products, arithmetic and copies ran while one was open for 9% -> 3% of each run, Pallas kernels for 0% -> 15%
where the time goes in v1:
time: 131 us; the launch traced here: 130 us
  starting transfers between devices  78.8 us (60%)
  Pallas kernels  20.5 us (16%)
  waiting for transfers between devices  18.6 us (14%)
  local copies, waits for them, and re-layouts  11.4 us (9%)
    ppermute x6, starting transfers between devices, swap(): lax.ppermute(high, axis, forward)  30.7 us
    ppermute x6, starting transfers between devices, swap(): lax.ppermute(low, axis, backward)  21.5 us
    pallas_call x11, Pallas kernels, kernel_call(): pl.pallas_call(body, out_shape=tuple(outs), in_specs=specs, out_specs=(pl...  20.5 us
    ppermute x6, waiting for transfers between devices, swap(): lax.ppermute(low, axis, backward)  12.5 us
    unnamed x33, local copies, waits for them, and re-layouts  10.7 us
    all_to_all x1, starting transfers between devices, on_device(): parts = lax.all_to_all(copies, ('gy', 'gz'), split_axis=0, concat_axis=0)  9.7 us
    all_to_all x1, starting transfers between devices, on_device(): parts = lax.all_to_all(blocks, 'gx', split_axis=0, concat_axis=0)  8.55 us
    all_to_all x1, starting transfers between devices, on_device(): factors = lax.all_to_all(copies, 'gx', split_axis=0, concat_axis=0)  8.41 us
  transfers between devices with their start and end apart: 15, of which 4 were waited for; matrix products, arithmetic and copies ran while one was open for 3% of the time, Pallas kernels for 15%

profile of v1, /device:TPU:1, one launch (start us, length us, event | category | flops | bytes accessed | tf_op | source)
XLA Modules:
  0.0 129.8 jit_solution(9624015885323802210)
XLA Ops:
  0.0 0.8 copy-done
  0.8 0.8 copy-done.1
  1.5 0.8 copy-done.2
  2.3 0.7 copy-done.7
  3.0 0.4 shard_map.136
  3.3 4.6 %collective-permute-start.6 = (bf16[64,128]{1,0:T(8,128)(2,1)S(1)}, bf16[64,128]{1,0:T(8,128)(2,1)S(1)}, u32[]{:S(2)}, u32[]{:S(2)}) collective-permute-start(bf16[64,128]{1,0:T(8,128)(2,1)S(1)} %get-tuple-element.36), channel_id=1, source_target_pairs={{0,16},{16,32},{32,48},{48,64},{64,80},{80,96},{96,112},{112,128},... | collective-permute-start | bytes 49160 | tf_op jit(solution)/shard_map/ppermute | solution.py:225
  8.0 6.1 %collective-permute-start.7 = (bf16[64,128]{1,0:T(8,128)(2,1)S(1)}, bf16[64,128]{1,0:T(8,128)(2,1)S(1)}, u32[]{:S(2)}, u32[]{:S(2)}) collective-permute-start(bf16[64,128]{1,0:T(8,128)(2,1)S(1)} %get-tuple-element.37), channel_id=1, source_target_pairs={{16,0},{32,16},{48,32},{64,48},{80,64},{96,80},{112,96},{128,112},... | collective-permute-start | bytes 49160 | tf_op jit(solution)/shard_map/ppermute | solution.py:225
  14.1 0.8 copy.18.charge_ref
  14.9 0.8 copy-done.3
  15.7 0.7 copy-done.9
  16.3 1.2 shard_map.143
  17.5 8.6 %all-to-all-start = ((bf16[32,16,128]{2,1,0:T(8,128)(2,1)}), bf16[32,16,128]{2,1,0:T(8,128)(2,1)S(1)}, u32[]{:S(2)}, u32[]{:S(2)}) async-start(bf16[32,16,128]{2,1,0:T(8,128)(2,1)} %get-tuple-element.42), calls=%async_computation | async-start | bytes 262144 | tf_op jit(solution)/shard_map/all_to_all | solution.py:269
  26.1 0.8 copy.15.dist_ref
  27.0 0.9 copy.16.nbr_ref
  27.8 0.7 pad.4
  28.5 0.1 broadcast_multiply_fusion
  28.7 5.2 %all-to-all-done.parts_ref = bf16[32,16,128]{2,1,0:T(8,128)(2,1)S(1)} async-done(((bf16[32,16,128]{2,1,0:T(8,128)(2,1)}), bf16[32,16,128]{2,1,0:T(8,128)(2,1)S(1)}, u32[]{:S(2)}, u32[]{:S(2)}) %all-to-all-start) | async-done | bytes 131104 | tf_op jit(solution)/shard_map/all_to_all | solution.py:269
  33.9 0.7 shard_map.144
  34.6 9.7 %all-to-all-start.1 = ((bf16[16,16,128]{2,1,0:T(8,128)(2,1)}), bf16[16,16,128]{2,1,0:T(8,128)(2,1)S(1)}, u32[]{:S(2)}, u32[]{:S(2)}) async-start(bf16[16,16,128]{2,1,0:T(8,128)(2,1)} %shard_map.144), calls=%async_computation.1 | async-start | bytes 131072 | tf_op jit(solution)/shard_map/all_to_all | solution.py:294
  44.3 0.0 copy-start.10
  44.3 0.6 copy-done.10
  44.9 10.0 %shard_map.137 = (f32[448,128]{1,0:T(8,128)S(1)}, bf16[128,128]{1,0:T(8,128)(2,1)S(1)}, bf16[128,128]{1,0:T(8,128)(2,1)S(1)}, bf16[64,128,128]{2,1,0:T(8,128)(2,1)S(1)}) custom-call(f32[128,64]{1,0:T(8,128)S(1)} %copy.15.dist_ref, s32[128,64]{1,0:T(8,128)S(1)} %copy.16.nbr_ref, s32[1,128]{1,0:T(1,128)S(1)} %bitcast.8, ...), custom_call_target="tpu_custom_call" | custom-call | flops 3000000000 | bytes 2621952 | tf_op jit(solution)/shard_map/pallas_call | solution.py:22
  54.9 1.4 %copy-done.11 = bf16[64,128,128]{2,1,0:T(8,128)(2,1)} copy-done((bf16[64,128,128]{2,1,0:T(8,128)(2,1)}, bf16[64,128,128]{2,1,0:T(8,128)(2,1)S(1)}, u32[]{:S(2)}) %copy-start.11) | copy-done | bytes 2097176
  56.3 3.3 %collective-permute-start = (bf16[128,128]{1,0:T(8,128)(2,1)S(1)}, bf16[128,128]{1,0:T(8,128)(2,1)S(1)}, u32[]{:S(2)}, u32[]{:S(2)}) collective-permute-start(bf16[128,128]{1,0:T(8,128)(2,1)S(1)} %get-tuple-element.27), channel_id=1, source_target_pairs={{0,1},{1,2},{2,3},{3,0},{4,5},{5,6},{6,7},{7,4},{8,9},{9,10},{10,1... | collective-permute-start | bytes 98312 | tf_op jit(solution)/shard_map/ppermute | solution.py:225
  59.6 3.8 %collective-permute-start.1 = (bf16[128,128]{1,0:T(8,128)(2,1)S(1)}, bf16[128,128]{1,0:T(8,128)(2,1)S(1)}, u32[]{:S(2)}, u32[]{:S(2)}) collective-permute-start(bf16[128,128]{1,0:T(8,128)(2,1)S(1)} %get-tuple-element.28), channel_id=1, source_target_pairs={{1,0},{2,1},{3,2},{0,3},{5,4},{6,5},{7,6},{4,7},{9,8},{10,9},{11,1... | collective-permute-start | bytes 98312 | tf_op jit(solution)/shard_map/ppermute | solution.py:225
  63.4 0.0 collective-permute-done.6.refs_1_
  63.4 0.3 shard_map.140
  63.8 7.2 %collective-permute-start.8 = (bf16[96,128]{1,0:T(8,128)(2,1)S(1)}, bf16[96,128]{1,0:T(8,128)(2,1)S(1)}, u32[]{:S(2)}, u32[]{:S(2)}) collective-permute-start(bf16[96,128]{1,0:T(8,128)(2,1)S(1)} %get-tuple-element.38), channel_id=1, source_target_pairs={{0,4},{4,8},{8,12},{12,0},{1,5},{5,9},{9,13},{13,1},{2,6},{6,10},{... | collective-permute-start | bytes 73736 | tf_op jit(solution)/shard_map/ppermute | solution.py:225
  70.9 2.0 %collective-permute-start.9 = (bf16[96,128]{1,0:T(8,128)(2,1)S(1)}, bf16[96,128]{1,0:T(8,128)(2,1)S(1)}, u32[]{:S(2)}, u32[]{:S(2)}) collective-permute-start(bf16[96,128]{1,0:T(8,128)(2,1)S(1)} %get-tuple-element.39), channel_id=1, source_target_pairs={{4,0},{8,4},{12,8},{0,12},{5,1},{9,5},{13,9},{1,13},{6,2},{10,6},{... | collective-permute-start | bytes 73736 | tf_op jit(solution)/shard_map/ppermute | solution.py:225
  73.0 0.0 collective-permute-done.8.refs_3_
  73.0 6.7 %collective-permute-done.9.refs_4_ = bf16[96,128]{1,0:T(8,128)(2,1)S(1)} collective-permute-done((bf16[96,128]{1,0:T(8,128)(2,1)S(1)}, bf16[96,128]{1,0:T(8,128)(2,1)S(1)}, u32[]{:S(2)}, u32[]{:S(2)}) %collective-permute-start.9) | collective-permute-done | bytes 24608 | tf_op jit(solution)/shard_map/ppermute | solution.py:225
  79.7 0.4 shard_map.141
  80.1 1.9 %collective-permute-start.10 = (bf16[128,128]{1,0:T(8,128)(2,1)S(1)}, bf16[128,128]{1,0:T(8,128)(2,1)S(1)}, u32[]{:S(2)}, u32[]{:S(2)}) collective-permute-start(bf16[128,128]{1,0:T(8,128)(2,1)S(1)} %get-tuple-element.40), channel_id=1, source_target_pairs={{0,1},{1,2},{2,3},{3,0},{4,5},{5,6},{6,7},{7,4},{8,9},{9,10},{10,1... | collective-permute-start | bytes 98312 | tf_op jit(solution)/shard_map/ppermute | solution.py:225
  82.0 5.2 %collective-permute-start.11 = (bf16[128,128]{1,0:T(8,128)(2,1)S(1)}, bf16[128,128]{1,0:T(8,128)(2,1)S(1)}, u32[]{:S(2)}, u32[]{:S(2)}) collective-permute-start(bf16[128,128]{1,0:T(8,128)(2,1)S(1)} %get-tuple-element.41), channel_id=1, source_target_pairs={{1,0},{2,1},{3,2},{0,3},{5,4},{6,5},{7,6},{4,7},{9,8},{10,9},{11,1... | collective-permute-start | bytes 98312 | tf_op jit(solution)/shard_map/ppermute | solution.py:225
  87.2 0.2 shard_map.138
  87.4 6.7 %collective-permute-start.2 = (bf16[96,128]{1,0:T(8,128)(2,1)S(1)}, bf16[96,128]{1,0:T(8,128)(2,1)S(1)}, u32[]{:S(2)}, u32[]{:S(2)}) collective-permute-start(bf16[96,128]{1,0:T(8,128)(2,1)S(1)} %get-tuple-element.30), channel_id=1, source_target_pairs={{0,4},{4,8},{8,12},{12,0},{1,5},{5,9},{9,13},{13,1},{2,6},{6,10},{... | collective-permute-start | bytes 73736 | tf_op jit(solution)/shard_map/ppermute | solution.py:225
  94.2 2.5 %collective-permute-start.3 = (bf16[96,128]{1,0:T(8,128)(2,1)S(1)}, bf16[96,128]{1,0:T(8,128)(2,1)S(1)}, u32[]{:S(2)}, u32[]{:S(2)}) collective-permute-start(bf16[96,128]{1,0:T(8,128)(2,1)S(1)} %get-tuple-element.31), channel_id=1, source_target_pairs={{4,0},{8,4},{12,8},{0,12},{5,1},{9,5},{13,9},{1,13},{6,2},{10,6},{... | collective-permute-start | bytes 73736 | tf_op jit(solution)/shard_map/ppermute | solution.py:225
  96.7 0.2 copy.19.refs_2_
  96.9 5.8 %collective-permute-done.3.above_ref = bf16[96,128]{1,0:T(8,128)(2,1)S(1)} collective-permute-done((bf16[96,128]{1,0:T(8,128)(2,1)S(1)}, bf16[96,128]{1,0:T(8,128)(2,1)S(1)}, u32[]{:S(2)}, u32[]{:S(2)}) %collective-permute-start.3) | collective-permute-done | bytes 24608 | tf_op jit(solution)/shard_map/ppermute | solution.py:225
  102.7 0.2 shard_map.139
  102.8 7.0 %collective-permute-start.4 = (bf16[64,128]{1,0:T(8,128)(2,1)S(1)}, bf16[64,128]{1,0:T(8,128)(2,1)S(1)}, u32[]{:S(2)}, u32[]{:S(2)}) collective-permute-start(bf16[64,128]{1,0:T(8,128)(2,1)S(1)} %get-tuple-element.33), channel_id=1, source_target_pairs={{0,16},{16,32},{32,48},{48,64},{64,80},{80,96},{96,112},{112,128},... | collective-permute-start | bytes 49160 | tf_op jit(solution)/shard_map/ppermute | solution.py:225
  109.8 1.9 %collective-permute-start.5 = (bf16[64,128]{1,0:T(8,128)(2,1)S(1)}, bf16[64,128]{1,0:T(8,128)(2,1)S(1)}, u32[]{:S(2)}, u32[]{:S(2)}) collective-permute-start(bf16[64,128]{1,0:T(8,128)(2,1)S(1)} %get-tuple-element.34), channel_id=1, source_target_pairs={{16,0},{32,16},{48,32},{64,48},{80,64},{96,80},{112,96},{128,112},... | collective-permute-start | bytes 49160 | tf_op jit(solution)/shard_map/ppermute | solution.py:225
  111.8 0.8 shard_map.145
  112.5 8.4 %all-to-all-start.2 = ((bf16[32,16,128]{2,1,0:T(8,128)(2,1)}), bf16[32,16,128]{2,1,0:T(8,128)(2,1)S(1)}, u32[]{:S(2)}, u32[]{:S(2)}) async-start(bf16[32,16,128]{2,1,0:T(8,128)(2,1)} %shard_map.145), calls=%async_computation.2 | async-start | bytes 262144 | tf_op jit(solution)/shard_map/all_to_all | solution.py:313
  121.0 1.6 %copy-done.12 = bf16[64,128,128]{2,1,0:T(8,128)(2,1)S(1)} copy-done((bf16[64,128,128]{2,1,0:T(8,128)(2,1)S(1)}, bf16[64,128,128]{2,1,0:T(8,128)(2,1)}, u32[]{:S(2)}) %copy-start.12) | copy-done | bytes 2097176
  122.6 5.3 %shard_map.142.gathered_ref = f32[128,128]{1,0:T(8,128)S(1)} custom-call(s32[128,64]{1,0:T(8,128)S(1)} %copy.16.nbr_ref, bf16[64,128,128]{2,1,0:T(8,128)(2,1)S(1)} %copy-done.12, bf16[128,128]{1,0:T(8,128)(2,1)S(1)} %get-tuple-element.25.base_ref.refs_0_, bf16[64,128]{1,0:T(8,128)(2,1)S(1)} %collective-permute-done.6.refs_1_, ...), custom_call_target="tpu_custom_call" | custom-call | flops 1500000000 | bytes 2375680 | tf_op jit(solution)/shard_map/pallas_call | solution.py:22
  127.9 0.9 all-to-all-done.2.factor_ref
  128.8 1.1 shard_map.146
  (29 shorter events, 0.1 us)
Async XLA Ops:
  0.0 0.8 copy-start
  0.8 0.8 copy-start.1
  1.5 0.8 copy-start.2
  2.3 0.7 copy-start.7
  3.3 60.0 %collective-permute-start.6 = (bf16[64,128]{1,0:T(8,128)(2,1)S(1)}, bf16[64,128]{1,0:T(8,128)(2,1)S(1)}, u32[]{:S(2)}, u32[]{:S(2)}) collective-permute-start(bf16[64,128]{1,0:T(8,128)(2,1)S(1)} %get-tuple-element.36), channel_id=1, source_target_pairs={{0,16},{16,32},{32,48},{48,64},{64,80},{80,96},{96,112},{112,128},... | collective-permute-start | bytes 49160 | tf_op jit(solution)/shard_map/ppermute | solution.py:225
  8.0 55.4 %collective-permute-start.7 = (bf16[64,128]{1,0:T(8,128)(2,1)S(1)}, bf16[64,128]{1,0:T(8,128)(2,1)S(1)}, u32[]{:S(2)}, u32[]{:S(2)}) collective-permute-start(bf16[64,128]{1,0:T(8,128)(2,1)S(1)} %get-tuple-element.37), channel_id=1, source_target_pairs={{16,0},{32,16},{48,32},{64,48},{80,64},{96,80},{112,96},{128,112},... | collective-permute-start | bytes 49160 | tf_op jit(solution)/shard_map/ppermute | solution.py:225
  14.9 0.8 copy-start.3
  15.6 0.7 copy-start.9
  17.5 16.4 %all-to-all-start = ((bf16[32,16,128]{2,1,0:T(8,128)(2,1)}), bf16[32,16,128]{2,1,0:T(8,128)(2,1)S(1)}, u32[]{:S(2)}, u32[]{:S(2)}) async-start(bf16[32,16,128]{2,1,0:T(8,128)(2,1)} %get-tuple-element.42), calls=%async_computation | async-start | bytes 262144 | tf_op jit(solution)/shard_map/all_to_all | solution.py:269
  34.6 77.2 %all-to-all-start.1 = ((bf16[16,16,128]{2,1,0:T(8,128)(2,1)}), bf16[16,16,128]{2,1,0:T(8,128)(2,1)S(1)}, u32[]{:S(2)}, u32[]{:S(2)}) async-start(bf16[16,16,128]{2,1,0:T(8,128)(2,1)} %shard_map.144), calls=%async_computation.1 | async-start | bytes 131072 | tf_op jit(solution)/shard_map/all_to_all | solution.py:294
  44.3 0.7 copy-start.10
  44.9 18.5 %copy-start.6 = (s32[2,96]{1,0:T(2,128)S(1)}, s32[2,96]{1,0:T(2,128)}, u32[]{:S(2)}) copy-start(s32[2,96]{1,0:T(2,128)} %refs_3_.1) | copy-start | bytes 2308
  44.9 34.7 %copy-start.5 = (s32[2,128]{1,0:T(2,128)S(1)}, s32[2,128]{1,0:T(2,128)}, u32[]{:S(2)}) copy-start(s32[2,128]{1,0:T(2,128)} %refs_5_.1) | copy-start | bytes 3076
  44.9 51.7 %copy-start.13 = (f32[1024,32]{0,1:T(8,128)S(1)}, f32[1024,32]{0,1:T(8,128)}, u32[]{:S(2)}) copy-start(f32[1024,32]{0,1:T(8,128)} %param.26) | copy-start | bytes 393220
  54.9 1.4 %copy-start.11 = (bf16[64,128,128]{2,1,0:T(8,128)(2,1)}, bf16[64,128,128]{2,1,0:T(8,128)(2,1)S(1)}, u32[]{:S(2)}) copy-start(bf16[64,128,128]{2,1,0:T(8,128)(2,1)S(1)} %get-tuple-element.35.radial_ref) | copy-start | bytes 6291460
  56.3 30.9 %collective-permute-start = (bf16[128,128]{1,0:T(8,128)(2,1)S(1)}, bf16[128,128]{1,0:T(8,128)(2,1)S(1)}, u32[]{:S(2)}, u32[]{:S(2)}) collective-permute-start(bf16[128,128]{1,0:T(8,128)(2,1)S(1)} %get-tuple-element.27), channel_id=1, source_target_pairs={{0,1},{1,2},{2,3},{3,0},{4,5},{5,6},{6,7},{7,4},{8,9},{9,10},{10,1... | collective-permute-start | bytes 98312 | tf_op jit(solution)/shard_map/ppermute | solution.py:225
  59.6 27.6 %collective-permute-start.1 = (bf16[128,128]{1,0:T(8,128)(2,1)S(1)}, bf16[128,128]{1,0:T(8,128)(2,1)S(1)}, u32[]{:S(2)}, u32[]{:S(2)}) collective-permute-start(bf16[128,128]{1,0:T(8,128)(2,1)S(1)} %get-tuple-element.28), channel_id=1, source_target_pairs={{1,0},{2,1},{3,2},{0,3},{5,4},{6,5},{7,6},{4,7},{9,8},{10,9},{11,1... | collective-permute-start | bytes 98312 | tf_op jit(solution)/shard_map/ppermute | solution.py:225
  63.8 9.2 %collective-permute-start.8 = (bf16[96,128]{1,0:T(8,128)(2,1)S(1)}, bf16[96,128]{1,0:T(8,128)(2,1)S(1)}, u32[]{:S(2)}, u32[]{:S(2)}) collective-permute-start(bf16[96,128]{1,0:T(8,128)(2,1)S(1)} %get-tuple-element.38), channel_id=1, source_target_pairs={{0,4},{4,8},{8,12},{12,0},{1,5},{5,9},{9,13},{13,1},{2,6},{6,10},{... | collective-permute-start | bytes 73736 | tf_op jit(solution)/shard_map/ppermute | solution.py:225
  70.9 8.7 %collective-permute-start.9 = (bf16[96,128]{1,0:T(8,128)(2,1)S(1)}, bf16[96,128]{1,0:T(8,128)(2,1)S(1)}, u32[]{:S(2)}, u32[]{:S(2)}) collective-permute-start(bf16[96,128]{1,0:T(8,128)(2,1)S(1)} %get-tuple-element.39), channel_id=1, source_target_pairs={{4,0},{8,4},{12,8},{0,12},{5,1},{9,5},{13,9},{1,13},{6,2},{10,6},{... | collective-permute-start | bytes 73736 | tf_op jit(solution)/shard_map/ppermute | solution.py:225
  80.1 40.9 %collective-permute-start.10 = (bf16[128,128]{1,0:T(8,128)(2,1)S(1)}, bf16[128,128]{1,0:T(8,128)(2,1)S(1)}, u32[]{:S(2)}, u32[]{:S(2)}) collective-permute-start(bf16[128,128]{1,0:T(8,128)(2,1)S(1)} %get-tuple-element.40), channel_id=1, source_target_pairs={{0,1},{1,2},{2,3},{3,0},{4,5},{5,6},{6,7},{7,4},{8,9},{9,10},{10,1... | collective-permute-start | bytes 98312 | tf_op jit(solution)/shard_map/ppermute | solution.py:225
  82.0 38.9 %collective-permute-start.11 = (bf16[128,128]{1,0:T(8,128)(2,1)S(1)}, bf16[128,128]{1,0:T(8,128)(2,1)S(1)}, u32[]{:S(2)}, u32[]{:S(2)}) collective-permute-start(bf16[128,128]{1,0:T(8,128)(2,1)S(1)} %get-tuple-element.41), channel_id=1, source_target_pairs={{1,0},{2,1},{3,2},{0,3},{5,4},{6,5},{7,6},{4,7},{9,8},{10,9},{11,1... | collective-permute-start | bytes 98312 | tf_op jit(solution)/shard_map/ppermute | solution.py:225
  87.4 9.4 %collective-permute-start.2 = (bf16[96,128]{1,0:T(8,128)(2,1)S(1)}, bf16[96,128]{1,0:T(8,128)(2,1)S(1)}, u32[]{:S(2)}, u32[]{:S(2)}) collective-permute-start(bf16[96,128]{1,0:T(8,128)(2,1)S(1)} %get-tuple-element.30), channel_id=1, source_target_pairs={{0,4},{4,8},{8,12},{12,0},{1,5},{5,9},{9,13},{13,1},{2,6},{6,10},{... | collective-permute-start | bytes 73736 | tf_op jit(solution)/shard_map/ppermute | solution.py:225
  94.2 8.5 %collective-permute-start.3 = (bf16[96,128]{1,0:T(8,128)(2,1)S(1)}, bf16[96,128]{1,0:T(8,128)(2,1)S(1)}, u32[]{:S(2)}, u32[]{:S(2)}) collective-permute-start(bf16[96,128]{1,0:T(8,128)(2,1)S(1)} %get-tuple-element.31), channel_id=1, source_target_pairs={{4,0},{8,4},{12,8},{0,12},{5,1},{9,5},{13,9},{1,13},{6,2},{10,6},{... | collective-permute-start | bytes 73736 | tf_op jit(solution)/shard_map/ppermute | solution.py:225
  102.8 25.0 %collective-permute-start.4 = (bf16[64,128]{1,0:T(8,128)(2,1)S(1)}, bf16[64,128]{1,0:T(8,128)(2,1)S(1)}, u32[]{:S(2)}, u32[]{:S(2)}) collective-permute-start(bf16[64,128]{1,0:T(8,128)(2,1)S(1)} %get-tuple-element.33), channel_id=1, source_target_pairs={{0,16},{16,32},{32,48},{48,64},{64,80},{80,96},{96,112},{112,128},... | collective-permute-start | bytes 49160 | tf_op jit(solution)/shard_map/ppermute | solution.py:225
  109.8 18.0 %collective-permute-start.5 = (bf16[64,128]{1,0:T(8,128)(2,1)S(1)}, bf16[64,128]{1,0:T(8,128)(2,1)S(1)}, u32[]{:S(2)}, u32[]{:S(2)}) collective-permute-start(bf16[64,128]{1,0:T(8,128)(2,1)S(1)} %get-tuple-element.34), channel_id=1, source_target_pairs={{16,0},{32,16},{48,32},{64,48},{80,64},{96,80},{112,96},{128,112},... | collective-permute-start | bytes 49160 | tf_op jit(solution)/shard_map/ppermute | solution.py:225
  112.5 16.2 %all-to-all-start.2 = ((bf16[32,16,128]{2,1,0:T(8,128)(2,1)}), bf16[32,16,128]{2,1,0:T(8,128)(2,1)S(1)}, u32[]{:S(2)}, u32[]{:S(2)}) async-start(bf16[32,16,128]{2,1,0:T(8,128)(2,1)} %shard_map.145), calls=%async_computation.2 | async-start | bytes 262144 | tf_op jit(solution)/shard_map/all_to_all | solution.py:313
  121.0 1.6 %copy-start.12 = (bf16[64,128,128]{2,1,0:T(8,128)(2,1)S(1)}, bf16[64,128,128]{2,1,0:T(8,128)(2,1)}, u32[]{:S(2)}) copy-start(bf16[64,128,128]{2,1,0:T(8,128)(2,1)} %copy-done.11) | copy-start | bytes 6291460
  122.6 6.2 %copy-start.4 = (bf16[32,128]{1,0:T(8,128)(2,1)S(1)}, bf16[32,128]{1,0:T(8,128)(2,1)}, u32[]{:S(2)}) copy-start(bf16[32,128]{1,0:T(8,128)(2,1)} %ewald_ref.1) | copy-start | bytes 24580
  122.6 6.2 %copy-start.8 = (s32[2,64]{1,0:T(2,128)S(1)}, s32[2,64]{1,0:T(2,128)}, u32[]{:S(2)}) copy-start(s32[2,64]{1,0:T(2,128)} %send_ref.7) | copy-start | bytes 1540

commit v2 on v1

v2 whole, which is shorter than its diff:
```python
import math

import jax
import jax.numpy as jnp
from jax import lax
from jax.experimental import pallas as pl
from jax.experimental.pallas import tpu as pltpu
from jax.sharding import PartitionSpec as P

cutoff = 5.0
pair_scale = 0.25
basis_rows = 32
slot_group = 4
mebi = 1024 * 1024


def kernel_call(body, outs, operands, flops, limit, scratch=(), far=0):
    specs = [pl.BlockSpec(memory_space=pl.ANY)] * far
    specs += [pl.BlockSpec(memory_space=pltpu.VMEM)] * (len(operands) - far)
    moved = sum(math.prod(v.shape) * v.dtype.itemsize for v in (*operands, *outs))
    return pl.pallas_call(
        body,
        out_shape=tuple(outs),
        in_specs=specs,
        out_specs=(pl.BlockSpec(memory_space=pltpu.VMEM),) * len(outs),
        scratch_shapes=list(scratch),
        compiler_params=pltpu.CompilerParams(vmem_limit_bytes=limit * mebi),
        cost_estimate=pl.CostEstimate(flops=flops, bytes_accessed=moved, transcendentals=0),
    )(*operands)


def like(shape, dtype):
    return jax.ShapeDtypeStruct(shape, dtype)


def dot32(left, right):
    return jnp.dot(left, right, preferred_element_type=jnp.float32)


def picked(send, side, table):
    columns = jnp.concatenate([send] * 4, axis=0).T[:, side : side + 1]
    lanes = lax.broadcasted_iota(jnp.int32, (send.shape[1], table.shape[0]), 1)
    return dot32((columns == lanes).astype(jnp.bfloat16), table).astype(jnp.bfloat16)


def placed(send, below, above, rows):
    iota = lax.broadcasted_iota(jnp.int32, (rows, send.shape[1]), 0)
    low = dot32((iota == send[1:2]).astype(jnp.bfloat16), below)
    return low + dot32((iota == send[0:1]).astype(jnp.bfloat16), above)


def sides(axis):
    count = lax.axis_size(axis)
    here = lax.axis_index(axis).astype(jnp.int32)
    return lax.rem(here + count - 1, count), lax.rem(here + 1, count)


def unit_waves(coord, first, count):
    orders = (lax.broadcasted_iota(jnp.int32, (count, coord.shape[1]), 0) + first).astype(jnp.float32)
    turns = orders * coord
    angle = (2.0 * math.pi) * (turns - jnp.round(turns))
    return jnp.cos(angle), jnp.sin(angle)


def outer_waves(left, right):
    left_cos, left_sin = (v[:, None, :] for v in left)
    right_cos, right_sin = (v[None, :, :] for v in right)
    shape = (left_cos.shape[0] * right_cos.shape[1], left_cos.shape[2])
    cos_part = (left_cos * right_cos - left_sin * right_sin).reshape(shape)
    return cos_part, (left_sin * right_cos + left_cos * right_sin).reshape(shape)


def opening_body(*refs):
    far, (base_ref, blocks_ref, cos_ref, sin_ref), near, sems = refs[:6], refs[6:10], refs[10:16], refs[16]
    copies = [pltpu.make_async_copy(far[i], near[i], sems.at[i]) for i in range(6)]
    for copy in copies:
        copy.start()
    for copy in copies:
        copy.wait()
    feats_ref, one_ref, two_ref, send_ref, coords_ref, charge_ref = near
    feats = feats_ref[...]
    raw = dot32(feats, one_ref[...])
    hidden = (raw / (1.0 + jnp.exp(-raw))).astype(jnp.bfloat16)
    base = dot32(hidden, two_ref[...]).astype(jnp.bfloat16)
    base_ref[...] = base
    total, atoms = cos_ref.shape
    blocks, tall, width = blocks_ref.shape
    height = tall - send_ref.shape[1]
    lower, upper = sides("gx")
    blocks_ref[lower, height:] = picked(send_ref[...], 0, base)
    blocks_ref[upper, height:] = picked(send_ref[...], 1, base)

    firsts = total // 64
    coords = coords_ref[...]
    along_first = unit_waves(coords[0:1], -(firsts // 2), firsts)
    along_second = unit_waves(coords[1:2], -4, 8)
    along_third = unit_waves(coords[2:3], 1, 8)
    cos_part, sin_part = outer_waves(outer_waves(along_first, along_second), along_third)
    cos_table = cos_part.astype(jnp.bfloat16)
    sin_table = sin_part.astype(jnp.bfloat16)
    cos_ref[...] = cos_table
    sin_ref[...] = sin_table
    over_last = (((1,), (1,)), ((), ()))
    charge_t = lax.dot_general(charge_ref[...], feats, over_last, preferred_element_type=jnp.float32).astype(jnp.bfloat16)
    real = lax.dot_general(charge_t, cos_table, over_last, preferred_element_type=jnp.float32)
    imag = lax.dot_general(charge_t, sin_table, over_last, preferred_element_type=jnp.float32)
    both = jnp.concatenate([real, imag], axis=0).astype(blocks_ref.dtype)
    across = total // width
    for block in range(blocks):
        down, along = block // across * height, block % across * width
        blocks_ref[block, :height] = both[down : down + height, along : along + width]


def spread_body(
    dist_ref, nbr_ref, count_ref, base_ref, wide_ref, core_ref, blocks_ref, radial_ref, basis_ref
):
    slots, atoms = dist_ref.shape
    feat = base_ref.shape[1]
    core, half = core_ref.shape[0], blocks_ref.shape[1]
    distance = dist_ref[...]
    angle = (math.pi / cutoff) * distance
    turn = jnp.cos(angle)
    listed = lax.broadcasted_iota(jnp.int32, (slots, atoms), 0) < count_ref[...]
    fade = jnp.where(listed, 0.5 * (turn + 1.0), 0.0) / distance
    turn = turn + turn
    basis_ref[...] = jnp.zeros_like(basis_ref)
    before, now = jnp.zeros_like(angle), jnp.sin(angle)
    for order in range(20):
        term = now * fade
        for row in range(0, slots, 8):
            place = pl.ds(row * basis_rows + order, 8, stride=basis_rows)
            basis_ref[place, :] = term[row : row + 8]
        before, now = now, turn * now - before
    base = base_ref[...]
    iota = lax.broadcasted_iota(jnp.int32, (core + 2 * half, atoms), 0)
    group_rows = slot_group * basis_rows
    pickers, outward = [], []
    for group in range(slots // slot_group):
        block = basis_ref[group * group_rows : (group + 1) * group_rows, :].T.astype(jnp.bfloat16)
        wide = dot32(block, wide_ref[...]).astype(jnp.bfloat16)
        for offset in range(slot_group):
            slot = group * slot_group + offset
            radial = wide[:, offset * feat : (offset + 1) * feat]
            radial_ref[slot] = radial
            outward.append(radial * base)
            pickers.append((iota == nbr_ref[slot : slot + 1, :]).astype(jnp.bfloat16))
    total = dot32(jnp.concatenate(pickers, axis=1), jnp.concatenate(outward, axis=0))
    core_ref[...] = total[:core]
    lower, upper = sides("gz")
    blocks_ref[lower] = total[core : core + half].astype(jnp.bfloat16)
    blocks_ref[upper] = total[core + half :].astype(jnp.bfloat16)


def second_body(
    first_ref, third_ref, base_ref, core_ref, send_y_ref, send_z_ref,
    table_ref, keep_ref, low_ref, high_ref, copies_ref,
):
    height = copies_ref.shape[1]
    lower, upper = sides("gx")
    table = jnp.concatenate([base_ref[...], first_ref[lower, height:], first_ref[upper, height:]], axis=0)
    table_ref[...] = table
    total = jnp.sum(first_ref[:, :height].astype(jnp.float32), axis=0)
    copies_ref[...] = jnp.broadcast_to(total.astype(copies_ref.dtype)[None], copies_ref.shape)
    below, above = sides("gz")
    spread = core_ref[...] + placed(send_z_ref[...], third_ref[below], third_ref[above], core_ref.shape[0])
    keep, half = keep_ref.shape[0], send_y_ref.shape[1]
    keep_ref[...] = spread[:keep]
    low_ref[:half] = picked(send_y_ref[...], 0, table)
    high_ref[:half] = picked(send_y_ref[...], 1, table)
    low_ref[half:] = spread[keep : keep + half].astype(jnp.bfloat16)
    high_ref[half:] = spread[keep + half :].astype(jnp.bfloat16)


def third_body(
    below_ref, above_ref, table_ref, core_ref, send_y_ref, send_z_ref, longer_ref, keep_ref, low_ref, high_ref, blocks_ref
):
    half = send_y_ref.shape[1]
    table = jnp.concatenate([table_ref[...], below_ref[:half], above_ref[:half]], axis=0)
    longer_ref[...] = table
    lower, upper = sides("gz")
    blocks_ref[lower] = picked(send_z_ref[...], 0, table)
    blocks_ref[upper] = picked(send_z_ref[...], 1, table)
    spread = core_ref[...] + placed(send_y_ref[...], below_ref[half:], above_ref[half:], core_ref.shape[0])
    keep, rim = keep_ref.shape[0], low_ref.shape[0]
    keep_ref[...] = spread[:keep]
    low_ref[...] = spread[keep : keep + rim].astype(jnp.bfloat16)
    high_ref[...] = spread[keep + rim :].astype(jnp.bfloat16)


def factor_body(parts_ref, kernel_ref, low_ref, high_ref, blocks_ref, norm_factor):
    blocks, tall, width = blocks_ref.shape
    height = parts_ref.shape[1]
    across = kernel_ref.shape[1] // width
    here = lax.axis_index("gx").astype(jnp.int32)
    down, along = lax.div(here, across), lax.rem(here, across)
    weights = kernel_ref[:, pl.ds(pl.multiple_of(along * width, width), width)]
    weights = jnp.where(lax.rem(down, 2) == 0, weights[:height], weights[height:])
    total = jnp.sum(parts_ref[...].astype(jnp.float32), axis=0)
    factors = (total * weights * norm_factor).astype(blocks_ref.dtype)
    blocks_ref[:, :height] = jnp.broadcast_to(factors[None], (blocks, height, width))
    lower, upper = sides("gx")
    blocks_ref[lower, height:] = low_ref[...]
    blocks_ref[upper, height:] = high_ref[...]


def gather_body(nbr_ref, radial_ref, table_ref, third_ref, gathered_ref):
    slots, atoms = nbr_ref.shape
    lower, upper = sides("gz")
    table = jnp.concatenate([table_ref[...], third_ref[lower], third_ref[upper]], axis=0)
    lanes = lax.broadcasted_iota(jnp.int32, (atoms, table.shape[0]), 1)
    partner = nbr_ref[...].T
    total = jnp.zeros(gathered_ref.shape, jnp.float32)
    for slot in range(slots):
        picker = (partner[:, slot : slot + 1] == lanes).astype(jnp.bfloat16)
        total = total + dot32(picker, table) * radial_ref[slot].astype(jnp.float32)
    gathered_ref[...] = total


def update_body(first_ref, core_ref, send_ref, gathered_ref, cos_ref, sin_ref, ewald_ref, out_ref):
    blocks, tall, width = first_ref.shape
    height = tall - send_ref.shape[1]
    lower, upper = sides("gx")
    returned = core_ref[...] + placed(
        send_ref[...], first_ref[lower, height:], first_ref[upper, height:], core_ref.shape[0]
    )
    pair_update = (gathered_ref[...] + returned) * pair_scale
    total = cos_ref.shape[0]
    across = total // width
    lines = []
    for down in range(blocks // across):
        lines.append(jnp.concatenate([first_ref[down * across + i, :height] for i in range(across)], axis=1))
    real = dot32(jnp.concatenate(lines[: len(lines) // 2], axis=0), cos_ref[...])
    imag = dot32(jnp.concatenate(lines[len(lines) // 2 :], axis=0), sin_ref[...])
    field = ((real + imag) * (1.0 / math.sqrt(total))).T.astype(jnp.bfloat16)
    out_ref[...] = (pair_update + dot32(field, ewald_ref[...])).astype(out_ref.dtype)


def swap(low, high, axis):
    count = lax.axis_size(axis)
    forward = [(i, (i + 1) % count) for i in range(count)]
    backward = [(target, source) for source, target in forward]
    return lax.ppermute(high, axis, forward), lax.ppermute(low, axis, backward)


def exchange(blocks, axes):
    return lax.all_to_all(blocks, axes, split_axis=0, concat_axis=0)


def on_device(
    feats,
    coords,
    pair_dist,
    nbr_index,
    nbr_count,
    send_x,
    send_y,
    send_z,
    w_one,
    w_two,
    w_radial,
    w_charge,
    k_kernel,
    w_ewald,
):
    atoms, feat = feats.shape
    slots = pair_dist.shape[1]
    charges = w_charge.shape[1]
    total = k_kernel.shape[0]
    rim_x, rim_y, rim_z = send_x.shape[1], send_y.shape[1], send_z.shape[1]
    with_x = atoms + 2 * rim_x
    with_y = with_x + 2 * rim_y
    half, full = jnp.bfloat16, jnp.float32
    count_x, count_z = lax.axis_size("gx"), lax.axis_size("gz")
    count_yz = lax.axis_size("gy") * count_z
    height = 2 * charges * (total // 128) // count_x
    tall = height + rim_x

    far = (feats, w_one, w_two, send_x, coords, w_charge.T)
    base, blocks, cos_table, sin_table = kernel_call(
        opening_body,
        (
            like((atoms, feat), half), like((count_x, tall, feat), half),
            like((total, atoms), half), like((total, atoms), half),
        ),
        far, 10**8, 16,
        (*(pltpu.VMEM(v.shape, v.dtype) for v in far), pltpu.SemaphoreType.DMA((len(far),))), far=len(far),
    )
    first = exchange(blocks, "gx")

    padded = jnp.pad(w_radial, ((0, basis_rows - w_radial.shape[0]), (0, 0)))
    wide = jnp.concatenate(
        [jnp.pad(padded, ((0, 0), (i * feat, (slot_group - 1 - i) * feat))) for i in range(slot_group)], axis=0
    )
    core, blocks, radial = kernel_call(
        spread_body,
        (like((with_y, feat), full), like((count_z, rim_z, feat), half), like((slots, atoms, feat), half)),
        (pair_dist.T, nbr_index.T, nbr_count[None, :], base, wide), 6 * 10**9, 32,
        (pltpu.VMEM((slots * basis_rows, atoms), full),),
    )
    third = exchange(blocks, "gz")

    table, core, low, high, copies = kernel_call(
        second_body,
        (
            like((with_x, feat), half), like((with_x, feat), full), like((2 * rim_y, feat), half),
            like((2 * rim_y, feat), half), like((count_yz, height, feat), half),
        ),
        (first, third, base, core, send_y, send_z), 10**8, 8,
    )
    below, above = swap(low, high, "gy")
    parts = exchange(copies, ("gy", "gz"))
    table, core, low, high, blocks = kernel_call(
        third_body,
        (
            like((with_y, feat), half), like((atoms, feat), full), like((rim_x, feat), half),
            like((rim_x, feat), half), like((count_z, rim_z, feat), half),
        ),
        (below, above, table, core, send_y, send_z), 10**8, 8,
    )
    third = exchange(blocks, "gz")

    norm_factor = 1.0 / math.sqrt(atoms * count_x * count_yz)
    (blocks,) = kernel_call(
        lambda *refs: factor_body(*refs, norm_factor),
        (like((count_x, tall, feat), half),), (parts, k_kernel.T, low, high), 10**6, 8,
    )
    first = exchange(blocks, "gx")
    (gathered,) = kernel_call(
        gather_body, (like((atoms, feat), full),), (nbr_index.T, radial, table, third), 6 * 10**9, 32
    )
    (update,) = kernel_call(
        update_body, (like((atoms, feat), half),),
        (first, core, send_x, gathered, cos_table, sin_table, w_ewald), 10**8, 16,
    )
    return update


def solution(mesh):
    in_specs = (
        P(("gx", "gy", "gz"), None),
        P(None, ("gx", "gy", "gz")),
        P(("gx", "gy", "gz"), None),
        P(("gx", "gy", "gz"), None),
        P(("gx", "gy", "gz")),
        P(None, ("gx", "gy", "gz")),
        P(None, ("gx", "gy", "gz")),
        P(None, ("gx", "gy", "gz")),
        P(),
        P(),
        P(),
        P(),
        P(),
        P(),
    )
    out_specs = P(("gx", "gy", "gz"), None)
    return jax.shard_map(
        on_device, mesh=mesh, in_specs=in_specs, out_specs=out_specs, check_vma=False
    )
```

time: 131 us -> 109 us (0.83)
  starting transfers between devices: 78.8 us -> 34.2 us
  blocking collectives: 0 us -> 33.2 us
  Pallas kernels: 20.5 us -> 12.8 us
  local copies, waits for them, and re-layouts: 11.4 us -> 8.8 us
    all_to_all x0 -> x2, blocking collectives: none -> 33.2 us  [exchange(): return lax.all_to_all(blocks, axes, split_axis=0, concat_axis=0)]
    ppermute x6 -> x1, starting transfers between devices: 30.7 us -> 7.2 us  [swap(): lax.ppermute(high, axis, forward)]
    ppermute x6 -> x1, starting transfers between devices: 21.5 us -> 2.02 us  [swap(): lax.ppermute(low, axis, backward)]
    pallas_call x11 -> x7, Pallas kernels: 20.5 us -> 12.8 us  [kernel_call(): pl.pallas_call(body, out_shape=tuple(outs), in_specs=specs, out_specs=(pl...]
    ppermute x6 -> x1, waiting for transfers between devices: 12.5 us -> 6.19 us  [swap(): lax.ppermute(low, axis, backward)]
    all_to_all x3, waiting for transfers between devices: 6.12 us -> 11.7 us  [exchange(): return lax.all_to_all(blocks, axes, split_axis=0, concat_axis=0)]
    unnamed x33 -> x34, local copies, waits for them, and re-layouts: 10.7 us -> 8.1 us
    all_to_all x3, starting transfers between devices: 26.7 us -> 25 us  [exchange(): return lax.all_to_all(blocks, axes, split_axis=0, concat_axis=0)]
  transfers between devices with their start and end apart: 15 -> 5, of which waited for: 4 -> 4; matrix products, arithmetic and copies ran while one was open for 3% -> 0% of each run, Pallas kernels for 15% -> 5%
where the time goes in v2:
time: 109 us; the launch traced here: 108 us
  starting transfers between devices  34.2 us (31%)
  blocking collectives  33.2 us (30%)
  waiting for transfers between devices  18.4 us (17%)
  Pallas kernels  12.8 us (12%)
  local copies, waits for them, and re-layouts  8.8 us (8%)
    all_to_all x2, blocking collectives, exchange(): return lax.all_to_all(blocks, axes, split_axis=0, concat_axis=0)  33.2 us
    all_to_all x3, starting transfers between devices, exchange(): return lax.all_to_all(blocks, axes, split_axis=0, concat_axis=0)  25 us
    pallas_call x7, Pallas kernels, kernel_call(): pl.pallas_call(body, out_shape=tuple(outs), in_specs=specs, out_specs=(pl...  12.8 us
    all_to_all x3, waiting for transfers between devices, exchange(): return lax.all_to_all(blocks, axes, split_axis=0, concat_axis=0)  11.7 us
    unnamed x34, local copies, waits for them, and re-layouts  8.1 us
    ppermute x1, starting transfers between devices, swap(): lax.ppermute(high, axis, forward)  7.2 us
    ppermute x1, waiting for transfers between devices, swap(): lax.ppermute(low, axis, backward)  6.19 us
  transfers between devices with their start and end apart: 5, of which 4 were waited for; matrix products, arithmetic and copies ran while one was open for 0% of the time, Pallas kernels for 5%

profile of v2, /device:TPU:1, one launch (start us, length us, event | category | flops | bytes accessed | tf_op | source)
XLA Modules:
  0.0 107.6 jit_solution(14850010979247057428)
XLA Ops:
  0.0 0.7 pad.20
  0.7 0.0 copy-start.2
  0.7 0.7 copy-done.2
  1.4 0.0 copy-start.6
  1.4 0.8 copy-done.6
  2.2 0.0 copy-start.7
  2.2 0.8 copy-done.7
  2.9 0.0 copy-start.8
  2.9 0.8 copy-done.8
  3.7 0.0 copy-start.12
  3.7 0.7 copy-done.12
  4.4 0.0 copy-start.13
  4.4 0.7 copy-done.13
  5.0 1.0 shard_map.136
  6.0 0.0 copy-start.9
  6.0 0.7 copy-done.9
  6.8 0.0 copy-start.10
  6.8 0.8 copy-done.10
  7.5 0.7 copy-done.14
  8.2 4.2 %shard_map.137 = (f32[448,128]{1,0:T(8,128)S(1)}, bf16[4,128,128]{2,1,0:T(8,128)(2,1)S(1)}, bf16[64,128,128]{2,1,0:T(8,128)(2,1)S(1)}) custom-call(f32[64,128]{1,0:T(8,128)S(1)} %bitcast.6, s32[64,128]{1,0:T(8,128)S(1)} %bitcast.7, s32[1,128]{1,0:T(1,128)S(1)} %bitcast.10, bf16[128,128]{1,0:T(8,128)(2,1)S(1)} %get-tuple-element.23.base_ref, ...), custom_call_target="tpu_custom_call" | custom-call | flops 6000000000 | bytes 2687488 | tf_op jit(solution)/shard_map/pallas_call | solution.py:21
  12.4 0.0 copy-start.15
  12.4 0.0 copy-start
  12.5 11.1 %all_to_all.25.third_ref = bf16[4,128,128]{2,1,0:T(8,128)(2,1)S(1)} all-to-all(bf16[4,128,128]{2,1,0:T(8,128)(2,1)S(1)} %get-tuple-element.24), channel_id=1, replica_groups=mesh['gx'=32,'gy'=4,'gz'=4] {'gz'}, dimensions={0} | all-to-all | bytes 262144 | tf_op jit(solution)/shard_map/all_to_all | solution.py:246
  23.6 22.1 %all_to_all.26.first_ref = bf16[32,80,128]{2,1,0:T(8,128)(2,1)S(1)} all-to-all(bf16[32,80,128]{2,1,0:T(8,128)(2,1)S(1)} %get-tuple-element.22), channel_id=1, replica_groups=mesh['gx'=32,'gy'=4,'gz'=4] {'gx'}, dimensions={0} | all-to-all | bytes 1310720 | tf_op jit(solution)/shard_map/all_to_all | solution.py:246
  45.7 0.0 copy-done.4
  45.7 0.0 copy-done.5
  45.7 1.0 shard_map.138
  46.6 0.0 copy-done.15
  46.7 12.2 %all-to-all-start.2 = ((bf16[16,16,128]{2,1,0:T(8,128)(2,1)}), bf16[16,16,128]{2,1,0:T(8,128)(2,1)S(1)}, u32[]{:S(2)}, u32[]{:S(2)}) async-start(bf16[16,16,128]{2,1,0:T(8,128)(2,1)} %get-tuple-element.26), calls=%async_computation.2 | async-start | bytes 131072 | tf_op jit(solution)/shard_map/all_to_all | solution.py:246
  58.9 7.2 %collective-permute-start = (bf16[192,128]{1,0:T(8,128)(2,1)S(1)}, bf16[192,128]{1,0:T(8,128)(2,1)S(1)}, u32[]{:S(2)}, u32[]{:S(2)}) collective-permute-start(bf16[192,128]{1,0:T(8,128)(2,1)S(1)} %get-tuple-element.27), channel_id=1, source_target_pairs={{0,4},{4,8},{8,12},{12,0},{1,5},{5,9},{9,13},{13,1},{2,6},{6,10},{... | collective-permute-start | bytes 147464 | tf_op jit(solution)/shard_map/ppermute | solution.py:242
  66.1 2.0 %collective-permute-start.1 = (bf16[192,128]{1,0:T(8,128)(2,1)S(1)}, bf16[192,128]{1,0:T(8,128)(2,1)S(1)}, u32[]{:S(2)}, u32[]{:S(2)}) collective-permute-start(bf16[192,128]{1,0:T(8,128)(2,1)S(1)} %get-tuple-element.28), channel_id=1, source_target_pairs={{4,0},{8,4},{12,8},{0,12},{5,1},{9,5},{13,9},{1,13},{6,2},{10,6},{... | collective-permute-start | bytes 147464 | tf_op jit(solution)/shard_map/ppermute | solution.py:242
  68.1 0.5 collective-permute-done.below_ref
  68.6 6.2 %collective-permute-done.1.above_ref = bf16[192,128]{1,0:T(8,128)(2,1)S(1)} collective-permute-done((bf16[192,128]{1,0:T(8,128)(2,1)S(1)}, bf16[192,128]{1,0:T(8,128)(2,1)S(1)}, u32[]{:S(2)}, u32[]{:S(2)}) %collective-permute-start.1) | collective-permute-done | bytes 49184 | tf_op jit(solution)/shard_map/ppermute | solution.py:242
  74.8 1.1 %shard_map.139 = (bf16[448,128]{1,0:T(8,128)(2,1)S(1)}, f32[128,128]{1,0:T(8,128)S(1)}, bf16[64,128]{1,0:T(8,128)(2,1)S(1)}, bf16[64,128]{1,0:T(8,128)(2,1)S(1)}, bf16[4,128,128]{2,1,0:T(8,128)(2,1)}) custom-call(bf16[192,128]{1,0:T(8,128)(2,1)S(1)} %collective-permute-done.below_ref, bf16[192,128]{1,0:T(8,128)(2,1)S(1)} %collective-permute-done.1.above_ref, ...), custom_call_target="tpu_custom_call" | custom-call | flops 100000000 | bytes 640768 | tf_op jit(solution)/shard_map/pallas_call | solution.py:21
  75.9 0.0 all-to-all-done.2.refs_0_
  75.9 4.3 %all-to-all-start.4 = ((bf16[4,128,128]{2,1,0:T(8,128)(2,1)}), bf16[4,128,128]{2,1,0:T(8,128)(2,1)S(1)}, u32[]{:S(2)}, u32[]{:S(2)}) async-start(bf16[4,128,128]{2,1,0:T(8,128)(2,1)} %get-tuple-element.36), calls=%async_computation.4 | async-start | bytes 262144 | tf_op jit(solution)/shard_map/all_to_all | solution.py:246
  80.2 0.0 copy-done
  80.2 0.9 shard_map.140
  81.1 3.9 %all-to-all-done.4.third_ref = bf16[4,128,128]{2,1,0:T(8,128)(2,1)S(1)} async-done(((bf16[4,128,128]{2,1,0:T(8,128)(2,1)}), bf16[4,128,128]{2,1,0:T(8,128)(2,1)S(1)}, u32[]{:S(2)}, u32[]{:S(2)}) %all-to-all-start.4) | async-done | bytes 131104 | tf_op jit(solution)/shard_map/all_to_all | solution.py:246
  85.0 8.5 %all-to-all-start.3 = ((bf16[32,80,128]{2,1,0:T(8,128)(2,1)}), bf16[32,80,128]{2,1,0:T(8,128)(2,1)S(1)}, u32[]{:S(2)}, u32[]{:S(2)}) async-start(bf16[32,80,128]{2,1,0:T(8,128)(2,1)} %shard_map.140), calls=%async_computation.3 | async-start | bytes 1310720 | tf_op jit(solution)/shard_map/all_to_all | solution.py:246
  93.5 0.0 copy-done.11
  93.5 0.0 copy-start.16
  93.5 1.6 %copy-done.16 = bf16[64,128,128]{2,1,0:T(8,128)(2,1)S(1)} copy-done((bf16[64,128,128]{2,1,0:T(8,128)(2,1)S(1)}, bf16[64,128,128]{2,1,0:T(8,128)(2,1)}, u32[]{:S(2)}) %copy-start.16) | copy-done | bytes 2097176
  95.1 3.6 %shard_map.141.gathered_ref = f32[128,128]{1,0:T(8,128)S(1)} custom-call(s32[64,128]{1,0:T(8,128)S(1)} %bitcast.8, bf16[64,128,128]{2,1,0:T(8,128)(2,1)S(1)} %copy-done.16, bf16[448,128]{1,0:T(8,128)(2,1)S(1)} %get-tuple-element.35.table_ref, bf16[4,128,128]{2,1,0:T(8,128)(2,1)S(1)} %all-to-all-done.4.third_ref), custom_call_target="tpu_custom_call" | custom-call | flops 6000000000 | bytes 2441216 | tf_op jit(solution)/shard_map/pallas_call | solution.py:21
  98.7 7.8 %all-to-all-done.3.first_ref = bf16[32,80,128]{2,1,0:T(8,128)(2,1)S(1)} async-done(((bf16[32,80,128]{2,1,0:T(8,128)(2,1)}), bf16[32,80,128]{2,1,0:T(8,128)(2,1)S(1)}, u32[]{:S(2)}, u32[]{:S(2)}) %all-to-all-start.3) | async-done | bytes 655392 | tf_op jit(solution)/shard_map/all_to_all | solution.py:246
  106.5 0.0 copy-done.1
  106.5 0.0 copy-done.3
  106.5 1.1 shard_map.142
  (7 shorter events, 0.0 us)
Async XLA Ops:
  0.7 0.7 copy-start.2
  1.4 0.8 copy-start.6
  2.2 0.8 copy-start.7
  2.9 0.8 copy-start.8
  3.7 0.7 copy-start.12
  4.4 0.7 copy-start.13
  6.0 0.8 copy-start.9
  6.8 0.8 copy-start.10
  7.5 0.7 copy-start.14
  8.2 37.5 %copy-start.4 = (s32[2,96]{1,0:T(2,128)S(1)}, s32[2,96]{1,0:T(2,128)}, u32[]{:S(2)}) copy-start(s32[2,96]{1,0:T(2,128)} %send_y_ref.3) | copy-start | bytes 2308
  8.2 37.5 %copy-start.5 = (s32[2,128]{1,0:T(2,128)S(1)}, s32[2,128]{1,0:T(2,128)}, u32[]{:S(2)}) copy-start(s32[2,128]{1,0:T(2,128)} %send_z_ref.3) | copy-start | bytes 3076
  12.4 34.2 %copy-start.15 = (bf16[64,128,128]{2,1,0:T(8,128)(2,1)}, bf16[64,128,128]{2,1,0:T(8,128)(2,1)S(1)}, u32[]{:S(2)}) copy-start(bf16[64,128,128]{2,1,0:T(8,128)(2,1)S(1)} %get-tuple-element.34.radial_ref) | copy-start | bytes 6291460
  12.4 67.8 %copy-start = (f32[1024,32]{0,1:T(8,128)S(1)}, f32[1024,32]{0,1:T(8,128)}, u32[]{:S(2)}) copy-start(f32[1024,32]{0,1:T(8,128)} %param.26) | copy-start | bytes 393220
  45.7 47.8 %copy-start.11 = (s32[128,64]{0,1:T(8,128)S(1)}, s32[128,64]{0,1:T(8,128)}, u32[]{:S(2)}) copy-start(s32[128,64]{0,1:T(8,128)} %param.17) | copy-start | bytes 98308
  46.7 29.3 %all-to-all-start.2 = ((bf16[16,16,128]{2,1,0:T(8,128)(2,1)}), bf16[16,16,128]{2,1,0:T(8,128)(2,1)S(1)}, u32[]{:S(2)}, u32[]{:S(2)}) async-start(bf16[16,16,128]{2,1,0:T(8,128)(2,1)} %get-tuple-element.26), calls=%async_computation.2 | async-start | bytes 131072 | tf_op jit(solution)/shard_map/all_to_all | solution.py:246
  58.9 9.8 %collective-permute-start = (bf16[192,128]{1,0:T(8,128)(2,1)S(1)}, bf16[192,128]{1,0:T(8,128)(2,1)S(1)}, u32[]{:S(2)}, u32[]{:S(2)}) collective-permute-start(bf16[192,128]{1,0:T(8,128)(2,1)S(1)} %get-tuple-element.27), channel_id=1, source_target_pairs={{0,4},{4,8},{8,12},{12,0},{1,5},{5,9},{9,13},{13,1},{2,6},{6,10},{... | collective-permute-start | bytes 147464 | tf_op jit(solution)/shard_map/ppermute | solution.py:242
  66.1 8.7 %collective-permute-start.1 = (bf16[192,128]{1,0:T(8,128)(2,1)S(1)}, bf16[192,128]{1,0:T(8,128)(2,1)S(1)}, u32[]{:S(2)}, u32[]{:S(2)}) collective-permute-start(bf16[192,128]{1,0:T(8,128)(2,1)S(1)} %get-tuple-element.28), channel_id=1, source_target_pairs={{4,0},{8,4},{12,8},{0,12},{5,1},{9,5},{13,9},{1,13},{6,2},{10,6},{... | collective-permute-start | bytes 147464 | tf_op jit(solution)/shard_map/ppermute | solution.py:242
  75.9 9.1 %all-to-all-start.4 = ((bf16[4,128,128]{2,1,0:T(8,128)(2,1)}), bf16[4,128,128]{2,1,0:T(8,128)(2,1)S(1)}, u32[]{:S(2)}, u32[]{:S(2)}) async-start(bf16[4,128,128]{2,1,0:T(8,128)(2,1)} %get-tuple-element.36), calls=%async_computation.4 | async-start | bytes 262144 | tf_op jit(solution)/shard_map/all_to_all | solution.py:246
  85.0 21.5 %all-to-all-start.3 = ((bf16[32,80,128]{2,1,0:T(8,128)(2,1)}), bf16[32,80,128]{2,1,0:T(8,128)(2,1)S(1)}, u32[]{:S(2)}, u32[]{:S(2)}) async-start(bf16[32,80,128]{2,1,0:T(8,128)(2,1)} %shard_map.140), calls=%async_computation.3 | async-start | bytes 1310720 | tf_op jit(solution)/shard_map/all_to_all | solution.py:246
  93.5 1.6 %copy-start.16 = (bf16[64,128,128]{2,1,0:T(8,128)(2,1)S(1)}, bf16[64,128,128]{2,1,0:T(8,128)(2,1)}, u32[]{:S(2)}) copy-start(bf16[64,128,128]{2,1,0:T(8,128)(2,1)} %copy-done.15) | copy-start | bytes 6291460
  95.1 11.4 %copy-start.1 = (bf16[32,128]{1,0:T(8,128)(2,1)S(1)}, bf16[32,128]{1,0:T(8,128)(2,1)}, u32[]{:S(2)}) copy-start(bf16[32,128]{1,0:T(8,128)(2,1)} %ewald_ref.1) | copy-start | bytes 24580
  95.1 11.5 %copy-start.3 = (s32[2,64]{1,0:T(2,128)S(1)}, s32[2,64]{1,0:T(2,128)}, u32[]{:S(2)}) copy-start(s32[2,64]{1,0:T(2,128)} %send_ref.1) | copy-start | bytes 1540

commit v3 on v2

--- a/solution.py
+++ b/solution.py
@@ -15,7 +15,7 @@
 
 
 def kernel_call(body, outs, operands, flops, limit, scratch=(), far=0):
-    specs = [pl.BlockSpec(memory_space=pl.ANY)] * far
+    specs = [pl.BlockSpec(memory_space=pltpu.HBM)] * far
     specs += [pl.BlockSpec(memory_space=pltpu.VMEM)] * (len(operands) - far)
     moved = sum(math.prod(v.shape) * v.dtype.itemsize for v in (*operands, *outs))
     return pl.pallas_call(
@@ -49,6 +49,19 @@
     return low + dot32((iota == send[0:1]).astype(jnp.bfloat16), above)
 
 
+def fetched(far, near, sems):
+    copies = [pltpu.make_async_copy(far[i], near[i], sems.at[i]) for i in range(len(far))]
+    for copy in copies:
+        copy.start()
+    for copy in copies:
+        copy.wait()
+    return near
+
+
+def landing(far):
+    return (*(pltpu.VMEM(v.shape, v.dtype) for v in far), pltpu.SemaphoreType.DMA((len(far),)))
+
+
 def sides(axis):
     count = lax.axis_size(axis)
     here = lax.axis_index(axis).astype(jnp.int32)
@@ -72,12 +85,7 @@
 
 def opening_body(*refs):
     far, (base_ref, blocks_ref, cos_ref, sin_ref), near, sems = refs[:6], refs[6:10], refs[10:16], refs[16]
-    copies = [pltpu.make_async_copy(far[i], near[i], sems.at[i]) for i in range(6)]
-    for copy in copies:
-        copy.start()
-    for copy in copies:
-        copy.wait()
-    feats_ref, one_ref, two_ref, send_ref, coords_ref, charge_ref = near
+    feats_ref, one_ref, two_ref, send_ref, coords_ref, charge_ref = fetched(far, near, sems)
     feats = feats_ref[...]
     raw = dot32(feats, one_ref[...])
     hidden = (raw / (1.0 + jnp.exp(-raw))).astype(jnp.bfloat16)
@@ -111,12 +119,12 @@
         blocks_ref[block, :height] = both[down : down + height, along : along + width]
 
 
-def spread_body(
-    dist_ref, nbr_ref, count_ref, base_ref, wide_ref, core_ref, blocks_ref, radial_ref, basis_ref
-):
+def spread_body(*refs):
+    far, (base_ref, core_ref, low_ref, high_ref, radial_ref, basis_ref) = refs[:4], refs[4:10]
+    dist_ref, nbr_ref, count_ref, weight_ref = fetched(far, refs[10:14], refs[14])
     slots, atoms = dist_ref.shape
     feat = base_ref.shape[1]
-    core, half = core_ref.shape[0], blocks_ref.shape[1]
+    core, half = core_ref.shape[0], low_ref.shape[0]
     distance = dist_ref[...]
     angle = (math.pi / cutoff) * distance
     turn = jnp.cos(angle)
@@ -134,10 +142,17 @@
     base = base_ref[...]
     iota = lax.broadcasted_iota(jnp.int32, (core + 2 * half, atoms), 0)
     group_rows = slot_group * basis_rows
+    shape = (group_rows, weight_ref.shape[0])
+    down, along = (lax.broadcasted_iota(jnp.int32, shape, i) for i in range(2))
+    wide = []
+    for offset in range(slot_group):
+        mover = (down == along + offset * basis_rows).astype(jnp.bfloat16)
+        wide.append(dot32(mover, weight_ref[...]).astype(jnp.bfloat16))
+    weights = jnp.concatenate(wide, axis=1)
     pickers, outward = [], []
     for group in range(slots // slot_group):
         block = basis_ref[group * group_rows : (group + 1) * group_rows, :].T.astype(jnp.bfloat16)
-        wide = dot32(block, wide_ref[...]).astype(jnp.bfloat16)
+        wide = dot32(block, weights).astype(jnp.bfloat16)
         for offset in range(slot_group):
             slot = group * slot_group + offset
             radial = wide[:, offset * feat : (offset + 1) * feat]
@@ -146,67 +161,77 @@
             pickers.append((iota == nbr_ref[slot : slot + 1, :]).astype(jnp.bfloat16))
     total = dot32(jnp.concatenate(pickers, axis=1), jnp.concatenate(outward, axis=0))
     core_ref[...] = total[:core]
+    low_ref[...] = total[core : core + half].astype(jnp.bfloat16)
+    high_ref[...] = total[core + half :].astype(jnp.bfloat16)
+
+
+def second_body(first_ref, base_ref, low_ref, high_ref, table_ref, blocks_ref):
+    height = blocks_ref.shape[1] - low_ref.shape[0]
+    lower, upper = sides("gx")
+    table_ref[...] = jnp.concatenate(
+        [base_ref[...], first_ref[lower, height:], first_ref[upper, height:]], axis=0
+    )
+    total = jnp.sum(first_ref[:, :height].astype(jnp.float32), axis=0).astype(blocks_ref.dtype)
+    for peer in range(blocks_ref.shape[0]):
+        blocks_ref[peer, :height] = total
     lower, upper = sides("gz")
-    blocks_ref[lower] = total[core : core + half].astype(jnp.bfloat16)
-    blocks_ref[upper] = total[core + half :].astype(jnp.bfloat16)
-
-
-def second_body(
-    first_ref, third_ref, base_ref, core_ref, send_y_ref, send_z_ref,
-    table_ref, keep_ref, low_ref, high_ref, copies_ref,
+    blocks_ref[lower, height:] = low_ref[...]
+    blocks_ref[upper, height:] = high_ref[...]
+
+
+def third_body(
+    third_ref, table_ref, core_ref, send_y_ref, send_z_ref, keep_ref, low_ref, high_ref, share_ref
 ):
-    height = copies_ref.shape[1]
-    lower, upper = sides("gx")
-    table = jnp.concatenate([base_ref[...], first_ref[lower, height:], first_ref[upper, height:]], axis=0)
-    table_ref[...] = table
-    total = jnp.sum(first_ref[:, :height].astype(jnp.float32), axis=0)
-    copies_ref[...] = jnp.broadcast_to(total.astype(copies_ref.dtype)[None], copies_ref.shape)
+    height, half = share_ref.shape[0], send_y_ref.shape[1]
+    share = jnp.sum(third_ref[:, :height].astype(jnp.float32), axis=0).astype(share_ref.dtype)
+    share_ref[...] = share
     below, above = sides("gz")
-    spread = core_ref[...] + placed(send_z_ref[...], third_ref[below], third_ref[above], core_ref.shape[0])
-    keep, half = keep_ref.shape[0], send_y_ref.shape[1]
+    spread = core_ref[...] + placed(
+        send_z_ref[...], third_ref[below, height:], third_ref[above, height:], core_ref.shape[0]
+    )
+    keep = keep_ref.shape[0]
     keep_ref[...] = spread[:keep]
-    low_ref[:half] = picked(send_y_ref[...], 0, table)
-    high_ref[:half] = picked(send_y_ref[...], 1, table)
-    low_ref[half:] = spread[keep : keep + half].astype(jnp.bfloat16)
-    high_ref[half:] = spread[keep + half :].astype(jnp.bfloat16)
-
-
-def third_body(
-    below_ref, above_ref, table_ref, core_ref, send_y_ref, send_z_ref, longer_ref, keep_ref, low_ref, high_ref, blocks_ref
+    table = table_ref[...]
+    for side, packet_ref in enumerate((low_ref, high_ref)):
+        rows = slice(keep + side * half, keep + (side + 1) * half)
+        packet_ref[:height] = share
+        packet_ref[height : height + half] = picked(send_y_ref[...], side, table)
+        packet_ref[height + half :] = spread[rows].astype(jnp.bfloat16)
+
+
+def fourth_body(
+    below_ref, above_ref, share_ref, across_ref, table_ref, core_ref, send_y_ref, send_z_ref, kernel_ref,
+    longer_ref, keep_ref, low_ref, high_ref, blocks_ref, norm_factor,
 ):
-    half = send_y_ref.shape[1]
-    table = jnp.concatenate([table_ref[...], below_ref[:half], above_ref[:half]], axis=0)
+    height, half = share_ref.shape[0], send_y_ref.shape[1]
+    fresh, back = slice(height, height + half), slice(height + half, height + 2 * half)
+    table = jnp.concatenate([table_ref[...], below_ref[fresh], above_ref[fresh]], axis=0)
     longer_ref[...] = table
-    lower, upper = sides("gz")
-    blocks_ref[lower] = picked(send_z_ref[...], 0, table)
-    blocks_ref[upper] = picked(send_z_ref[...], 1, table)
-    spread = core_ref[...] + placed(send_y_ref[...], below_ref[half:], above_ref[half:], core_ref.shape[0])
-    keep, rim = keep_ref.shape[0], low_ref.shape[0]
+    low_ref[...] = picked(send_z_ref[...], 0, table)
+    high_ref[...] = picked(send_z_ref[...], 1, table)
+    spread = core_ref[...] + placed(send_y_ref[...], below_ref[back], above_ref[back], core_ref.shape[0])
+    keep = keep_ref.shape[0]
     keep_ref[...] = spread[:keep]
-    low_ref[...] = spread[keep : keep + rim].astype(jnp.bfloat16)
-    high_ref[...] = spread[keep + rim :].astype(jnp.bfloat16)
-
-
-def factor_body(parts_ref, kernel_ref, low_ref, high_ref, blocks_ref, norm_factor):
+
     blocks, tall, width = blocks_ref.shape
-    height = parts_ref.shape[1]
+    rim = tall - height
     across = kernel_ref.shape[1] // width
     here = lax.axis_index("gx").astype(jnp.int32)
     down, along = lax.div(here, across), lax.rem(here, across)
     weights = kernel_ref[:, pl.ds(pl.multiple_of(along * width, width), width)]
     weights = jnp.where(lax.rem(down, 2) == 0, weights[:height], weights[height:])
-    total = jnp.sum(parts_ref[...].astype(jnp.float32), axis=0)
+    parts = (share_ref[...], across_ref[...], below_ref[:height], above_ref[:height])
+    total = sum(part.astype(jnp.float32) for part in parts)
     factors = (total * weights * norm_factor).astype(blocks_ref.dtype)
     blocks_ref[:, :height] = jnp.broadcast_to(factors[None], (blocks, height, width))
     lower, upper = sides("gx")
-    blocks_ref[lower, height:] = low_ref[...]
-    blocks_ref[upper, height:] = high_ref[...]
-
-
-def gather_body(nbr_ref, radial_ref, table_ref, third_ref, gathered_ref):
+    blocks_ref[lower, height:] = spread[keep : keep + rim].astype(jnp.bfloat16)
+    blocks_ref[upper, height:] = spread[keep + rim :].astype(jnp.bfloat16)
+
+
+def gather_body(nbr_ref, radial_ref, table_ref, below_ref, above_ref, gathered_ref):
     slots, atoms = nbr_ref.shape
-    lower, upper = sides("gz")
-    table = jnp.concatenate([table_ref[...], third_ref[lower], third_ref[upper]], axis=0)
+    table = jnp.concatenate([table_ref[...], below_ref[...], above_ref[...]], axis=0)
     lanes = lax.broadcasted_iota(jnp.int32, (atoms, table.shape[0]), 1)
     partner = nbr_ref[...].T
     total = jnp.zeros(gathered_ref.shape, jnp.float32)
@@ -270,8 +295,7 @@
     with_x = atoms + 2 * rim_x
     with_y = with_x + 2 * rim_y
     half, full = jnp.bfloat16, jnp.float32
-    count_x, count_z = lax.axis_size("gx"), lax.axis_size("gz")
-    count_yz = lax.axis_size("gy") * count_z
+    count_x, count_y, count_z = (lax.axis_size(axis) for axis in ("gx", "gy", "gz"))
     height = 2 * charges * (total // 128) // count_x
     tall = height + rim_x
 
@@ -282,51 +306,48 @@
             like((atoms, feat), half), like((count_x, tall, feat), half),
             like((total, atoms), half), like((total, atoms), half),
         ),
-        far, 10**8, 16,
-        (*(pltpu.VMEM(v.shape, v.dtype) for v in far), pltpu.SemaphoreType.DMA((len(far),))), far=len(far),
+        far, 10**8, 60, landing(far), far=len(far),
     )
     first = exchange(blocks, "gx")
 
-    padded = jnp.pad(w_radial, ((0, basis_rows - w_radial.shape[0]), (0, 0)))
-    wide = jnp.concatenate(
-        [jnp.pad(padded, ((0, 0), (i * feat, (slot_group - 1 - i) * feat))) for i in range(slot_group)], axis=0
-    )
-    core, blocks, radial = kernel_call(
+    far = (pair_dist.T, nbr_index.T, nbr_count[None, :], w_radial)
+    core, low, high, radial = kernel_call(
         spread_body,
-        (like((with_y, feat), full), like((count_z, rim_z, feat), half), like((slots, atoms, feat), half)),
-        (pair_dist.T, nbr_index.T, nbr_count[None, :], base, wide), 6 * 10**9, 32,
-        (pltpu.VMEM((slots * basis_rows, atoms), full),),
+        (
+            like((with_y, feat), full), like((rim_z, feat), half), like((rim_z, feat), half),
+            like((slots, atoms, feat), half),
+        ),
+        (*far, base), 6 * 10**9, 60, (pltpu.VMEM((slots * basis_rows, atoms), full), *landing(far)), far=len(far),
+    )
+    table, blocks = kernel_call(
+        second_body,
+        (like((with_x, feat), half), like((count_z, height + rim_z, feat), half)),
+        (first, base, low, high), 10**8, 8,
     )
     third = exchange(blocks, "gz")
-
-    table, core, low, high, copies = kernel_call(
-        second_body,
-        (
-            like((with_x, feat), half), like((with_x, feat), full), like((2 * rim_y, feat), half),
-            like((2 * rim_y, feat), half), like((count_yz, height, feat), half),
-        ),
-        (first, third, base, core, send_y, send_z), 10**8, 8,
-    )
-    below, above = swap(low, high, "gy")
-    parts = exchange(copies, ("gy", "gz"))
-    table, core, low, high, blocks = kernel_call(
+    core, low, high, share = kernel_call(
         third_body,
         (
-            like((with_y, feat), half), like((atoms, feat), full), like((rim_x, feat), half),
-            like((rim_x, feat), half), like((count_z, rim_z, feat), half),
+            like((with_x, feat), full), like((height + 2 * rim_y, feat), half),
+            like((height + 2 * rim_y, feat), half), like((height, feat), half),
         ),
-        (below, above, table, core, send_y, send_z), 10**8, 8,
-    )
-    third = exchange(blocks, "gz")
-
-    norm_factor = 1.0 / math.sqrt(atoms * count_x * count_yz)
-    (blocks,) = kernel_call(
-        lambda *refs: factor_body(*refs, norm_factor),
-        (like((count_x, tall, feat), half),), (parts, k_kernel.T, low, high), 10**6, 8,
-    )
+        (third, table, core, send_y, send_z), 10**8, 8,
+    )
+    below, above = swap(low, high, "gy")
+    across = lax.ppermute(share, "gy", [(i, (i + 2) % count_y) for i in range(count_y)])
+    norm_factor = 1.0 / math.sqrt(atoms * count_x * count_y * count_z)
+    table, core, low, high, blocks = kernel_call(
+        lambda *refs: fourth_body(*refs, norm_factor),
+        (
+            like((with_y, feat), half), like((atoms, feat), full), like((rim_z, feat), half),
+            like((rim_z, feat), half), like((count_x, tall, feat), half),
+        ),
+        (below, above, share, across, table, core, send_y, send_z, k_kernel.T), 10**8, 8,
+    )
+    below, above = swap(low, high, "gz")
     first = exchange(blocks, "gx")
     (gathered,) = kernel_call(
-        gather_body, (like((atoms, feat), full),), (nbr_index.T, radial, table, third), 6 * 10**9, 32
+        gather_body, (like((atoms, feat), full),), (nbr_index.T, radial, table, below, above), 6 * 10**9, 32
     )
     (update,) = kernel_call(
         update_body, (like((atoms, feat), half),),

time: 109 us -> 86.4 us (0.79)
  blocking collectives: 33.2 us -> 9.62 us
  starting transfers between devices: 34.2 us -> 45.7 us
  waiting for transfers between devices: 18.4 us -> 10.3 us
  local copies, waits for them, and re-layouts: 8.8 us -> 4.09 us
  Pallas kernels: 12.8 us -> 15.5 us
    all_to_all x2 -> x1, blocking collectives: 33.2 us -> 9.62 us  [exchange(): return lax.all_to_all(blocks, axes, split_axis=0, concat_axis=0)]
    ppermute x0 -> x1, starting transfers between devices: none -> 10.3 us  [on_device(): lax.ppermute(share, 'gy', [(i, (i + 2) % count_y) for i in range(count_y)])]
    all_to_all x3 -> x2, starting transfers between devices: 25 us -> 16.7 us  [exchange(): return lax.all_to_all(blocks, axes, split_axis=0, concat_axis=0)]
    ppermute x1 -> x2, starting transfers between devices: 2.02 us -> 7.45 us  [swap(): lax.ppermute(low, axis, backward)]
    all_to_all x3 -> x2, waiting for transfers between devices: 11.7 us -> 6.47 us  [exchange(): return lax.all_to_all(blocks, axes, split_axis=0, concat_axis=0)]
    ppermute x1 -> x2, waiting for transfers between devices: 6.19 us -> 0.99 us  [swap(): lax.ppermute(low, axis, backward)]
    ppermute x1 -> x2, starting transfers between devices: 7.2 us -> 11.3 us  [swap(): lax.ppermute(high, axis, forward)]
    unnamed x34 -> x26, local copies, waits for them, and re-layouts: 8.1 us -> 4.09 us
  transfers between devices with their start and end apart: 5 -> 7, of which waited for: 4 -> 3; matrix products, arithmetic and copies ran while one was open for 0% -> 0% of each run, Pallas kernels for 5% -> 12%
where the time goes in v3:
time: 86.4 us; the launch traced here: 85.4 us
  starting transfers between devices  45.7 us (53%)
  Pallas kernels  15.5 us (18%)
  waiting for transfers between devices  10.3 us (12%)
  blocking collectives  9.62 us (11%)
  local copies, waits for them, and re-layouts  4.09 us (5%)
    all_to_all x2, starting transfers between devices, exchange(): return lax.all_to_all(blocks, axes, split_axis=0, concat_axis=0)  16.7 us
    pallas_call x7, Pallas kernels, kernel_call(): pl.pallas_call(body, out_shape=tuple(outs), in_specs=specs, out_specs=(pl...  15.5 us
    ppermute x2, starting transfers between devices, swap(): lax.ppermute(high, axis, forward)  11.3 us
    ppermute x1, starting transfers between devices, on_device(): lax.ppermute(share, 'gy', [(i, (i + 2) % count_y) for i in range(count_y)])  10.3 us
    all_to_all x1, blocking collectives, exchange(): return lax.all_to_all(blocks, axes, split_axis=0, concat_axis=0)  9.62 us
    ppermute x2, starting transfers between devices, swap(): lax.ppermute(low, axis, backward)  7.45 us
    all_to_all x2, waiting for transfers between devices, exchange(): return lax.all_to_all(blocks, axes, split_axis=0, concat_axis=0)  6.47 us
    unnamed x26, local copies, waits for them, and re-layouts  4.09 us
  transfers between devices with their start and end apart: 7, of which 3 were waited for; matrix products, arithmetic and copies ran while one was open for 0% of the time, Pallas kernels for 12%

profile of v3, /device:TPU:1, one launch (start us, length us, event | category | flops | bytes accessed | tf_op | source)
XLA Modules:
  0.0 85.4 jit_solution(17843500410743865590)
XLA Ops:
  0.0 2.6 %shard_map.136 = (bf16[128,128]{1,0:T(8,128)(2,1)}, bf16[32,80,128]{2,1,0:T(8,128)(2,1)}, bf16[1024,128]{1,0:T(8,128)(2,1)}, bf16[1024,128]{1,0:T(8,128)(2,1)}) custom-call(bf16[128,128]{1,0:T(8,128)(2,1)} %refs_0_.1, bf16[128,128]{1,0:T(8,128)(2,1)} %refs_1_.1, bf16[128,128]{1,0:T(8,128)(2,1)} %refs_2_.1, s32[2,64]{1,0:T(2,128)} %send_ref.1, ...), custom_call_target="tpu_custom_call" | custom-call | flops 100000000 | bytes 1320960 | tf_op jit(solution)/shard_map/pallas_call | solution.py:21
  2.6 10.4 %all-to-all-start = ((bf16[32,80,128]{2,1,0:T(8,128)(2,1)}), bf16[32,80,128]{2,1,0:T(8,128)(2,1)S(1)}, u32[]{:S(2)}, u32[]{:S(2)}) async-start(bf16[32,80,128]{2,1,0:T(8,128)(2,1)} %get-tuple-element.24), calls=%async_computation | async-start | bytes 1310720 | tf_op jit(solution)/shard_map/all_to_all | solution.py:271
  13.0 0.0 copy-start.4
  13.0 0.0 copy-start.8
  13.0 0.0 copy-start.9
  13.1 0.0 copy-start.3
  13.1 0.0 copy-start.11
  13.1 6.5 %shard_map.137 = (f32[448,128]{1,0:T(8,128)}, bf16[128,128]{1,0:T(8,128)(2,1)}, bf16[128,128]{1,0:T(8,128)(2,1)}, bf16[64,128,128]{2,1,0:T(8,128)(2,1)}) custom-call(f32[64,128]{1,0:T(8,128)} %bitcast.8, s32[64,128]{1,0:T(8,128)} %bitcast.6, s32[1,128]{1,0:T(1,128)} %bitcast.10, bf16[20,128]{1,0:T(8,128)(2,1)} %refs_3_.3, ...), custom_call_target="tpu_custom_call" | custom-call | flops 6000000000 | bytes 2496000 | tf_op jit(solution)/shard_map/pallas_call | solution.py:21
  19.6 6.5 %all-to-all-done.first_ref = bf16[32,80,128]{2,1,0:T(8,128)(2,1)S(1)} async-done(((bf16[32,80,128]{2,1,0:T(8,128)(2,1)}), bf16[32,80,128]{2,1,0:T(8,128)(2,1)S(1)}, u32[]{:S(2)}, u32[]{:S(2)}) %all-to-all-start) | async-done | bytes 655392 | tf_op jit(solution)/shard_map/all_to_all | solution.py:271
  26.1 0.0 copy-done.4
  26.1 0.0 copy-start.5
  26.1 0.8 copy-done.5
  26.8 0.0 copy-start.6
  26.8 0.8 copy-done.6
  27.6 9.6 %all_to_all.15.third_ref = bf16[4,144,128]{2,1,0:T(8,128)(2,1)S(1)} all-to-all(bf16[4,144,128]{2,1,0:T(8,128)(2,1)S(1)} %get-tuple-element.28), channel_id=1, replica_groups=mesh['gx'=32,'gy'=4,'gz'=4] {'gz'}, dimensions={0} | all-to-all | bytes 294912 | tf_op jit(solution)/shard_map/all_to_all | solution.py:271
  37.3 0.0 copy-done.8
  37.3 0.0 copy-done.9
  37.3 0.0 copy-start.2
  37.3 0.9 %copy-done.2 = f32[448,128]{1,0:T(8,128)S(1)} copy-done((f32[448,128]{1,0:T(8,128)S(1)}, f32[448,128]{1,0:T(8,128)}, u32[]{:S(2)}) %copy-start.2) | copy-done | bytes 229400
  38.2 0.4 shard_map.139
  38.6 8.8 %collective-permute-start = (bf16[208,128]{1,0:T(8,128)(2,1)S(1)}, bf16[208,128]{1,0:T(8,128)(2,1)S(1)}, u32[]{:S(2)}, u32[]{:S(2)}) collective-permute-start(bf16[208,128]{1,0:T(8,128)(2,1)S(1)} %get-tuple-element.31), channel_id=1, source_target_pairs={{0,4},{4,8},{8,12},{12,0},{1,5},{5,9},{9,13},{13,1},{2,6},{6,10},{... | collective-permute-start | bytes 159752 | tf_op jit(solution)/shard_map/ppermute | solution.py:267
  47.4 2.9 %collective-permute-start.1 = (bf16[208,128]{1,0:T(8,128)(2,1)S(1)}, bf16[208,128]{1,0:T(8,128)(2,1)S(1)}, u32[]{:S(2)}, u32[]{:S(2)}) collective-permute-start(bf16[208,128]{1,0:T(8,128)(2,1)S(1)} %get-tuple-element.32), channel_id=1, source_target_pairs={{4,0},{8,4},{12,8},{0,12},{5,1},{9,5},{13,9},{1,13},{6,2},{10,6},{... | collective-permute-start | bytes 159752 | tf_op jit(solution)/shard_map/ppermute | solution.py:267
  50.3 10.3 %collective-permute-start.2 = (bf16[16,128]{1,0:T(8,128)(2,1)S(1)}, bf16[16,128]{1,0:T(8,128)(2,1)S(1)}, u32[]{:S(2)}, u32[]{:S(2)}) collective-permute-start(bf16[16,128]{1,0:T(8,128)(2,1)S(1)} %get-tuple-element.33.refs_2_), channel_id=1, source_target_pairs={{0,8},{4,12},{8,0},{12,4},{1,9},{5,13},{9,1},{13,5},{2,10},{6,14},... | collective-permute-start | bytes 12296 | tf_op jit(solution)/shard_map/ppermute | solution.py:337
  60.6 2.8 %collective-permute-done.2.refs_3_ = bf16[16,128]{1,0:T(8,128)(2,1)S(1)} collective-permute-done((bf16[16,128]{1,0:T(8,128)(2,1)S(1)}, bf16[16,128]{1,0:T(8,128)(2,1)S(1)}, u32[]{:S(2)}, u32[]{:S(2)}) %collective-permute-start.2) | collective-permute-done | bytes 4128 | tf_op jit(solution)/shard_map/ppermute | solution.py:337
  63.4 0.0 collective-permute-done.refs_0_
  63.4 0.0 collective-permute-done.1.refs_1_
  63.4 0.0 copy-done.3
  63.4 1.3 %shard_map.140 = (bf16[448,128]{1,0:T(8,128)(2,1)S(1)}, f32[128,128]{1,0:T(8,128)S(1)}, bf16[128,128]{1,0:T(8,128)(2,1)S(1)}, bf16[128,128]{1,0:T(8,128)(2,1)S(1)}, bf16[32,80,128]{2,1,0:T(8,128)(2,1)}) custom-call(bf16[208,128]{1,0:T(8,128)(2,1)S(1)} %collective-permute-done.refs_0_, bf16[208,128]{1,0:T(8,128)(2,1)S(1)} %collective-permute-done.1.refs_1_, ...), custom_call_target="tpu_custom_call" | custom-call | flops 100000000 | bytes 1345280 | tf_op jit(solution)/shard_map/pallas_call | solution.py:21
  64.7 6.2 %all-to-all-start.2 = ((bf16[32,80,128]{2,1,0:T(8,128)(2,1)}), bf16[32,80,128]{2,1,0:T(8,128)(2,1)S(1)}, u32[]{:S(2)}, u32[]{:S(2)}) async-start(bf16[32,80,128]{2,1,0:T(8,128)(2,1)} %get-tuple-element.35), calls=%async_computation.2 | async-start | bytes 1310720 | tf_op jit(solution)/shard_map/all_to_all | solution.py:271
  70.9 2.5 %collective-permute-start.3 = (bf16[128,128]{1,0:T(8,128)(2,1)S(1)}, bf16[128,128]{1,0:T(8,128)(2,1)S(1)}, u32[]{:S(2)}, u32[]{:S(2)}) collective-permute-start(bf16[128,128]{1,0:T(8,128)(2,1)S(1)} %get-tuple-element.39), channel_id=1, source_target_pairs={{0,1},{1,2},{2,3},{3,0},{4,5},{5,6},{6,7},{7,4},{8,9},{9,10},{10,1... | collective-permute-start | bytes 98312 | tf_op jit(solution)/shard_map/ppermute | solution.py:267
  73.4 4.6 %collective-permute-start.4 = (bf16[128,128]{1,0:T(8,128)(2,1)S(1)}, bf16[128,128]{1,0:T(8,128)(2,1)S(1)}, u32[]{:S(2)}, u32[]{:S(2)}) collective-permute-start(bf16[128,128]{1,0:T(8,128)(2,1)S(1)} %get-tuple-element.40), channel_id=1, source_target_pairs={{1,0},{2,1},{3,2},{0,3},{5,4},{6,5},{7,6},{4,7},{9,8},{10,9},{11,1... | collective-permute-start | bytes 98312 | tf_op jit(solution)/shard_map/ppermute | solution.py:267
  78.0 0.0 collective-permute-done.3.below_ref
  78.0 1.0 %collective-permute-done.4.above_ref = bf16[128,128]{1,0:T(8,128)(2,1)S(1)} collective-permute-done((bf16[128,128]{1,0:T(8,128)(2,1)S(1)}, bf16[128,128]{1,0:T(8,128)(2,1)S(1)}, u32[]{:S(2)}, u32[]{:S(2)}) %collective-permute-start.4) | collective-permute-done | bytes 32800 | tf_op jit(solution)/shard_map/ppermute | solution.py:267
  79.0 0.0 copy-done.11
  79.0 0.0 copy-start.12
  79.0 1.6 %copy-done.12 = bf16[64,128,128]{2,1,0:T(8,128)(2,1)S(1)} copy-done((bf16[64,128,128]{2,1,0:T(8,128)(2,1)S(1)}, bf16[64,128,128]{2,1,0:T(8,128)(2,1)}, u32[]{:S(2)}) %copy-start.12) | copy-done | bytes 2097176
  80.6 0.0 copy-start
  80.6 0.0 copy-start.1
  80.6 0.0 copy-start.7
  80.6 0.0 copy-start.10
  80.6 3.6 %shard_map.141.gathered_ref = f32[128,128]{1,0:T(8,128)S(1)} custom-call(s32[64,128]{1,0:T(8,128)S(1)} %bitcast.7, bf16[64,128,128]{2,1,0:T(8,128)(2,1)S(1)} %copy-done.12, bf16[448,128]{1,0:T(8,128)(2,1)S(1)} %get-tuple-element.38.table_ref, bf16[128,128]{1,0:T(8,128)(2,1)S(1)} %collective-permute-done.3.below_ref, ...), custom_call_target="tpu_custom_call" | custom-call | flops 6000000000 | bytes 2375680 | tf_op jit(solution)/shard_map/pallas_call | solution.py:21
  84.3 0.0 all-to-all-done.2.first_ref
  84.3 0.0 copy-done
  84.3 0.0 copy-done.1
  84.3 0.0 copy-done.7
  84.3 0.0 copy-done.10
  84.3 1.1 %shard_map.142 = bf16[128,128]{1,0:T(8,128)(2,1)} custom-call(bf16[32,80,128]{2,1,0:T(8,128)(2,1)S(1)} %all-to-all-done.2.first_ref, f32[128,128]{1,0:T(8,128)S(1)} %get-tuple-element.36.core_ref, s32[2,64]{1,0:T(2,128)S(1)} %copy-done.10, f32[128,128]{1,0:T(8,128)S(1)} %shard_map.141.gathered_ref, bf16[1024,128]{1,0:T(8,128)(2,1)S(1)} %copy-done, ...), custom_call_target="tpu_custom_call" | custom-call | flops 100000000 | bytes 1352192 | tf_op jit(solution)/shard_map/pallas_call | solution.py:21
  (1 shorter events, 0.0 us)
Async XLA Ops:
  2.6 23.5 %all-to-all-start = ((bf16[32,80,128]{2,1,0:T(8,128)(2,1)}), bf16[32,80,128]{2,1,0:T(8,128)(2,1)S(1)}, u32[]{:S(2)}, u32[]{:S(2)}) async-start(bf16[32,80,128]{2,1,0:T(8,128)(2,1)} %get-tuple-element.24), calls=%async_computation | async-start | bytes 1310720 | tf_op jit(solution)/shard_map/all_to_all | solution.py:271
  13.0 13.1 %copy-start.4 = (bf16[128,128]{1,0:T(8,128)(2,1)S(1)}, bf16[128,128]{1,0:T(8,128)(2,1)}, u32[]{:S(2)}) copy-start(bf16[128,128]{1,0:T(8,128)(2,1)} %get-tuple-element.25.refs_4_.base_ref) | copy-start | bytes 98308
  13.0 24.2 %copy-start.8 = (s32[2,96]{1,0:T(2,128)S(1)}, s32[2,96]{1,0:T(2,128)}, u32[]{:S(2)}) copy-start(s32[2,96]{1,0:T(2,128)} %refs_6_.1) | copy-start | bytes 2308
  13.0 24.2 %copy-start.9 = (s32[2,128]{1,0:T(2,128)S(1)}, s32[2,128]{1,0:T(2,128)}, u32[]{:S(2)}) copy-start(s32[2,128]{1,0:T(2,128)} %refs_7_.1) | copy-start | bytes 3076
  13.1 50.3 %copy-start.3 = (f32[1024,32]{0,1:T(8,128)S(1)}, f32[1024,32]{0,1:T(8,128)}, u32[]{:S(2)}) copy-start(f32[1024,32]{0,1:T(8,128)} %param.26) | copy-start | bytes 393220
  13.1 66.0 %copy-start.11 = (s32[128,64]{0,1:T(8,128)S(1)}, s32[128,64]{0,1:T(8,128)}, u32[]{:S(2)}) copy-start(s32[128,64]{0,1:T(8,128)} %param.17) | copy-start | bytes 98308
  26.1 0.8 copy-start.5
  26.8 0.8 copy-start.6
  37.3 0.9 %copy-start.2 = (f32[448,128]{1,0:T(8,128)S(1)}, f32[448,128]{1,0:T(8,128)}, u32[]{:S(2)}) copy-start(f32[448,128]{1,0:T(8,128)} %get-tuple-element.30.core_ref) | copy-start | bytes 688132
  38.6 24.8 %collective-permute-start = (bf16[208,128]{1,0:T(8,128)(2,1)S(1)}, bf16[208,128]{1,0:T(8,128)(2,1)S(1)}, u32[]{:S(2)}, u32[]{:S(2)}) collective-permute-start(bf16[208,128]{1,0:T(8,128)(2,1)S(1)} %get-tuple-element.31), channel_id=1, source_target_pairs={{0,4},{4,8},{8,12},{12,0},{1,5},{5,9},{9,13},{13,1},{2,6},{6,10},{... | collective-permute-start | bytes 159752 | tf_op jit(solution)/shard_map/ppermute | solution.py:267
  47.4 15.9 %collective-permute-start.1 = (bf16[208,128]{1,0:T(8,128)(2,1)S(1)}, bf16[208,128]{1,0:T(8,128)(2,1)S(1)}, u32[]{:S(2)}, u32[]{:S(2)}) collective-permute-start(bf16[208,128]{1,0:T(8,128)(2,1)S(1)} %get-tuple-element.32), channel_id=1, source_target_pairs={{4,0},{8,4},{12,8},{0,12},{5,1},{9,5},{13,9},{1,13},{6,2},{10,6},{... | collective-permute-start | bytes 159752 | tf_op jit(solution)/shard_map/ppermute | solution.py:267
  50.3 13.1 %collective-permute-start.2 = (bf16[16,128]{1,0:T(8,128)(2,1)S(1)}, bf16[16,128]{1,0:T(8,128)(2,1)S(1)}, u32[]{:S(2)}, u32[]{:S(2)}) collective-permute-start(bf16[16,128]{1,0:T(8,128)(2,1)S(1)} %get-tuple-element.33.refs_2_), channel_id=1, source_target_pairs={{0,8},{4,12},{8,0},{12,4},{1,9},{5,13},{9,1},{13,5},{2,10},{6,14},... | collective-permute-start | bytes 12296 | tf_op jit(solution)/shard_map/ppermute | solution.py:337
  64.7 19.6 %all-to-all-start.2 = ((bf16[32,80,128]{2,1,0:T(8,128)(2,1)}), bf16[32,80,128]{2,1,0:T(8,128)(2,1)S(1)}, u32[]{:S(2)}, u32[]{:S(2)}) async-start(bf16[32,80,128]{2,1,0:T(8,128)(2,1)} %get-tuple-element.35), calls=%async_computation.2 | async-start | bytes 1310720 | tf_op jit(solution)/shard_map/all_to_all | solution.py:271
  70.9 7.1 %collective-permute-start.3 = (bf16[128,128]{1,0:T(8,128)(2,1)S(1)}, bf16[128,128]{1,0:T(8,128)(2,1)S(1)}, u32[]{:S(2)}, u32[]{:S(2)}) collective-permute-start(bf16[128,128]{1,0:T(8,128)(2,1)S(1)} %get-tuple-element.39), channel_id=1, source_target_pairs={{0,1},{1,2},{2,3},{3,0},{4,5},{5,6},{6,7},{7,4},{8,9},{9,10},{10,1... | collective-permute-start | bytes 98312 | tf_op jit(solution)/shard_map/ppermute | solution.py:267
  73.4 5.6 %collective-permute-start.4 = (bf16[128,128]{1,0:T(8,128)(2,1)S(1)}, bf16[128,128]{1,0:T(8,128)(2,1)S(1)}, u32[]{:S(2)}, u32[]{:S(2)}) collective-permute-start(bf16[128,128]{1,0:T(8,128)(2,1)S(1)} %get-tuple-element.40), channel_id=1, source_target_pairs={{1,0},{2,1},{3,2},{0,3},{5,4},{6,5},{7,6},{4,7},{9,8},{10,9},{11,1... | collective-permute-start | bytes 98312 | tf_op jit(solution)/shard_map/ppermute | solution.py:267
  79.0 1.6 %copy-start.12 = (bf16[64,128,128]{2,1,0:T(8,128)(2,1)S(1)}, bf16[64,128,128]{2,1,0:T(8,128)(2,1)}, u32[]{:S(2)}) copy-start(bf16[64,128,128]{2,1,0:T(8,128)(2,1)} %get-tuple-element.37.radial_ref) | copy-start | bytes 6291460
  80.6 3.7 %copy-start = (bf16[1024,128]{1,0:T(8,128)(2,1)S(1)}, bf16[1024,128]{1,0:T(8,128)(2,1)}, u32[]{:S(2)}) copy-start(bf16[1024,128]{1,0:T(8,128)(2,1)} %get-tuple-element.41.cos_ref) | copy-start | bytes 786436
  80.6 3.7 %copy-start.1 = (bf16[1024,128]{1,0:T(8,128)(2,1)S(1)}, bf16[1024,128]{1,0:T(8,128)(2,1)}, u32[]{:S(2)}) copy-start(bf16[1024,128]{1,0:T(8,128)(2,1)} %get-tuple-element.42.sin_ref) | copy-start | bytes 786436
  80.6 3.7 %copy-start.7 = (bf16[32,128]{1,0:T(8,128)(2,1)S(1)}, bf16[32,128]{1,0:T(8,128)(2,1)}, u32[]{:S(2)}) copy-start(bf16[32,128]{1,0:T(8,128)(2,1)} %ewald_ref.1) | copy-start | bytes 24580
  80.6 3.7 %copy-start.10 = (s32[2,64]{1,0:T(2,128)S(1)}, s32[2,64]{1,0:T(2,128)}, u32[]{:S(2)}) copy-start(s32[2,64]{1,0:T(2,128)} %send_ref.1) | copy-start | bytes 1540

commit v4 on v3

--- a/solution.py
+++ b/solution.py
@@ -1,3 +1,4 @@
+import functools
 import math
 
 import jax
@@ -14,10 +15,11 @@
 mebi = 1024 * 1024
 
 
-def kernel_call(body, outs, operands, flops, limit, scratch=(), far=0):
+def kernel_call(body, outs, operands, flops, limit, scratch=(), far=0, moved=None):
     specs = [pl.BlockSpec(memory_space=pltpu.HBM)] * far
     specs += [pl.BlockSpec(memory_space=pltpu.VMEM)] * (len(operands) - far)
-    moved = sum(math.prod(v.shape) * v.dtype.itemsize for v in (*operands, *outs))
+    if moved is None:
+        moved = sum(math.prod(v.shape) * v.dtype.itemsize for v in (*operands, *outs))
     return pl.pallas_call(
         body,
         out_shape=tuple(outs),
@@ -83,31 +85,28 @@
     return cos_part, (left_sin * right_cos + left_cos * right_sin).reshape(shape)
 
 
-def opening_body(*refs):
-    far, (base_ref, blocks_ref, cos_ref, sin_ref), near, sems = refs[:6], refs[6:10], refs[10:16], refs[16]
-    feats_ref, one_ref, two_ref, send_ref, coords_ref, charge_ref = fetched(far, near, sems)
+def wave_tables(coords, total):
+    firsts = total // 64
+    along_first = unit_waves(coords[0:1], -(firsts // 2), firsts)
+    along_second = unit_waves(coords[1:2], -4, 8)
+    along_third = unit_waves(coords[2:3], 1, 8)
+    cos_part, sin_part = outer_waves(outer_waves(along_first, along_second), along_third)
+    return cos_part.astype(jnp.bfloat16), sin_part.astype(jnp.bfloat16)
+
+
+def opening_body(total, *refs):
+    far, (base_ref, blocks_ref) = refs[:6], refs[6:8]
+    feats_ref, one_ref, two_ref, send_ref, coords_ref, charge_ref = fetched(far, refs[8:14], refs[14])
     feats = feats_ref[...]
     raw = dot32(feats, one_ref[...])
     hidden = (raw / (1.0 + jnp.exp(-raw))).astype(jnp.bfloat16)
     base = dot32(hidden, two_ref[...]).astype(jnp.bfloat16)
     base_ref[...] = base
-    total, atoms = cos_ref.shape
     blocks, tall, width = blocks_ref.shape
     height = tall - send_ref.shape[1]
-    lower, upper = sides("gx")
-    blocks_ref[lower, height:] = picked(send_ref[...], 0, base)
-    blocks_ref[upper, height:] = picked(send_ref[...], 1, base)
-
-    firsts = total // 64
-    coords = coords_ref[...]
-    along_first = unit_waves(coords[0:1], -(firsts // 2), firsts)
-    along_second = unit_waves(coords[1:2], -4, 8)
-    along_third = unit_waves(coords[2:3], 1, 8)
-    cos_part, sin_part = outer_waves(outer_waves(along_first, along_second), along_third)
-    cos_table = cos_part.astype(jnp.bfloat16)
-    sin_table = sin_part.astype(jnp.bfloat16)
-    cos_ref[...] = cos_table
-    sin_ref[...] = sin_table
+    for side, peer in enumerate(sides("gx")):
+        blocks_ref[peer, height:] = picked(send_ref[...], side, base)
+    cos_table, sin_table = wave_tables(coords_ref[...], total)
     over_last = (((1,), (1,)), ((), ()))
     charge_t = lax.dot_general(charge_ref[...], feats, over_last, preferred_element_type=jnp.float32).astype(jnp.bfloat16)
     real = lax.dot_general(charge_t, cos_table, over_last, preferred_element_type=jnp.float32)
@@ -120,11 +119,11 @@
 
 
 def spread_body(*refs):
-    far, (base_ref, core_ref, low_ref, high_ref, radial_ref, basis_ref) = refs[:4], refs[4:10]
-    dist_ref, nbr_ref, count_ref, weight_ref = fetched(far, refs[10:14], refs[14])
+    far, (base_ref, core_ref, rim_ref, cos_ref, sin_ref, radial_ref, basis_ref) = refs[:5], refs[5:12]
+    dist_ref, nbr_ref, count_ref, weight_ref, coords_ref = fetched(far, refs[12:17], refs[17])
     slots, atoms = dist_ref.shape
     feat = base_ref.shape[1]
-    core, half = core_ref.shape[0], low_ref.shape[0]
+    core, rim = core_ref.shape[0], rim_ref.shape[0]
     distance = dist_ref[...]
     angle = (math.pi / cutoff) * distance
     turn = jnp.cos(angle)
@@ -140,7 +139,7 @@
             basis_ref[place, :] = term[row : row + 8]
         before, now = now, turn * now - before
     base = base_ref[...]
-    iota = lax.broadcasted_iota(jnp.int32, (core + 2 * half, atoms), 0)
+    iota = lax.broadcasted_iota(jnp.int32, (core + rim, atoms), 0)
     group_rows = slot_group * basis_rows
     shape = (group_rows, weight_ref.shape[0])
     down, along = (lax.broadcasted_iota(jnp.int32, shape, i) for i in range(2))
@@ -161,52 +160,63 @@
             pickers.append((iota == nbr_ref[slot : slot + 1, :]).astype(jnp.bfloat16))
     total = dot32(jnp.concatenate(pickers, axis=1), jnp.concatenate(outward, axis=0))
     core_ref[...] = total[:core]
-    low_ref[...] = total[core : core + half].astype(jnp.bfloat16)
-    high_ref[...] = total[core + half :].astype(jnp.bfloat16)
-
-
-def second_body(first_ref, base_ref, low_ref, high_ref, table_ref, blocks_ref):
-    height = blocks_ref.shape[1] - low_ref.shape[0]
-    lower, upper = sides("gx")
-    table_ref[...] = jnp.concatenate(
-        [base_ref[...], first_ref[lower, height:], first_ref[upper, height:]], axis=0
-    )
+    rim_ref[...] = total[core:].astype(jnp.bfloat16)
+    cos_ref[...], sin_ref[...] = wave_tables(coords_ref[...], cos_ref.shape[0])
+
+
+def second_body(first_ref, rim_ref, blocks_ref):
+    half = rim_ref.shape[0] // 2
+    height = blocks_ref.shape[1] - half
     total = jnp.sum(first_ref[:, :height].astype(jnp.float32), axis=0).astype(blocks_ref.dtype)
     for peer in range(blocks_ref.shape[0]):
         blocks_ref[peer, :height] = total
-    lower, upper = sides("gz")
-    blocks_ref[lower, height:] = low_ref[...]
-    blocks_ref[upper, height:] = high_ref[...]
-
-
-def third_body(
-    third_ref, table_ref, core_ref, send_y_ref, send_z_ref, keep_ref, low_ref, high_ref, share_ref
-):
-    height, half = share_ref.shape[0], send_y_ref.shape[1]
+    for side, peer in enumerate(sides("gz")):
+        blocks_ref[peer, height:] = rim_ref[side * half : (side + 1) * half]
+
+
+def pick_body(first_ref, base_ref, send_ref, table_ref, packets_ref):
+    height = first_ref.shape[1] - (table_ref.shape[0] - base_ref.shape[0]) // 2
+    lower, upper = sides("gx")
+    table = jnp.concatenate([base_ref[...], first_ref[lower, height:], first_ref[upper, height:]], axis=0)
+    table_ref[...] = table
+    for side in range(2):
+        packets_ref[side] = picked(send_ref[...], side, table)
+
+
+def third_body(third_ref, packets_ref, core_ref, send_z_ref, keep_ref, low_ref, high_ref, share_ref):
+    half = packets_ref.shape[1]
+    height = low_ref.shape[0] - 2 * half
     share = jnp.sum(third_ref[:, :height].astype(jnp.float32), axis=0).astype(share_ref.dtype)
-    share_ref[...] = share
+    share_ref[:height] = share
     below, above = sides("gz")
     spread = core_ref[...] + placed(
         send_z_ref[...], third_ref[below, height:], third_ref[above, height:], core_ref.shape[0]
     )
     keep = keep_ref.shape[0]
     keep_ref[...] = spread[:keep]
-    table = table_ref[...]
     for side, packet_ref in enumerate((low_ref, high_ref)):
         rows = slice(keep + side * half, keep + (side + 1) * half)
         packet_ref[:height] = share
-        packet_ref[height : height + half] = picked(send_y_ref[...], side, table)
+        packet_ref[height : height + half] = packets_ref[side]
         packet_ref[height + half :] = spread[rows].astype(jnp.bfloat16)
 
 
+def add_body(left_ref, right_ref, total_ref):
+    height = total_ref.shape[0]
+    total_ref[...] = left_ref[:height].astype(jnp.float32) + right_ref[:height].astype(jnp.float32)
+
+
+def relay_body(above_ref, relay_ref):
+    relay_ref[...] = above_ref[: relay_ref.shape[0]]
+
+
 def fourth_body(
-    below_ref, above_ref, share_ref, across_ref, table_ref, core_ref, send_y_ref, send_z_ref, kernel_ref,
-    longer_ref, keep_ref, low_ref, high_ref, blocks_ref, norm_factor,
+    below_ref, above_ref, share_ref, relay_ref, table_ref, core_ref, send_y_ref, send_z_ref, kernel_ref,
+    gathered_ref, keep_ref, low_ref, high_ref, blocks_ref, norm_factor,
 ):
     height, half = share_ref.shape[0], send_y_ref.shape[1]
     fresh, back = slice(height, height + half), slice(height + half, height + 2 * half)
     table = jnp.concatenate([table_ref[...], below_ref[fresh], above_ref[fresh]], axis=0)
-    longer_ref[...] = table
     low_ref[...] = picked(send_z_ref[...], 0, table)
     high_ref[...] = picked(send_z_ref[...], 1, table)
     spread = core_ref[...] + placed(send_y_ref[...], below_ref[back], above_ref[back], core_ref.shape[0])
@@ -220,7 +230,7 @@
     down, along = lax.div(here, across), lax.rem(here, across)
     weights = kernel_ref[:, pl.ds(pl.multiple_of(along * width, width), width)]
     weights = jnp.where(lax.rem(down, 2) == 0, weights[:height], weights[height:])
-    parts = (share_ref[...], across_ref[...], below_ref[:height], above_ref[:height])
+    parts = (share_ref[...], relay_ref[...], below_ref[:height], above_ref[:height])
     total = sum(part.astype(jnp.float32) for part in parts)
     factors = (total * weights * norm_factor).astype(blocks_ref.dtype)
     blocks_ref[:, :height] = jnp.broadcast_to(factors[None], (blocks, height, width))
@@ -229,16 +239,24 @@
     blocks_ref[upper, height:] = spread[keep + rim :].astype(jnp.bfloat16)
 
 
-def gather_body(nbr_ref, radial_ref, table_ref, below_ref, above_ref, gathered_ref):
+def gather_rows(first_row, table, nbr_ref, radial_ref):
     slots, atoms = nbr_ref.shape
-    table = jnp.concatenate([table_ref[...], below_ref[...], above_ref[...]], axis=0)
-    lanes = lax.broadcasted_iota(jnp.int32, (atoms, table.shape[0]), 1)
+    lanes = lax.broadcasted_iota(jnp.int32, (atoms, table.shape[0]), 1) + first_row
     partner = nbr_ref[...].T
-    total = jnp.zeros(gathered_ref.shape, jnp.float32)
+    total = jnp.zeros((atoms, table.shape[1]), jnp.float32)
     for slot in range(slots):
         picker = (partner[:, slot : slot + 1] == lanes).astype(jnp.bfloat16)
         total = total + dot32(picker, table) * radial_ref[slot].astype(jnp.float32)
-    gathered_ref[...] = total
+    return total
+
+
+def gather_first_body(nbr_ref, radial_ref, table_ref, order_ref, gathered_ref):
+    gathered_ref[...] = gather_rows(0, table_ref[...], nbr_ref, radial_ref)
+
+
+def gather_more_body(first_row, rows, nbr_ref, radial_ref, below_ref, above_ref, sofar_ref, gathered_ref):
+    table = jnp.concatenate([below_ref[rows], above_ref[rows]], axis=0)
+    gathered_ref[...] = sofar_ref[...] + gather_rows(first_row, table, nbr_ref, radial_ref)
 
 
 def update_body(first_ref, core_ref, send_ref, gathered_ref, cos_ref, sin_ref, ewald_ref, out_ref):
@@ -300,54 +318,65 @@
     tall = height + rim_x
 
     far = (feats, w_one, w_two, send_x, coords, w_charge.T)
-    base, blocks, cos_table, sin_table = kernel_call(
-        opening_body,
-        (
-            like((atoms, feat), half), like((count_x, tall, feat), half),
-            like((total, atoms), half), like((total, atoms), half),
-        ),
+    base, blocks = kernel_call(
+        functools.partial(opening_body, total),
+        (like((atoms, feat), half), like((count_x, tall, feat), half)),
         far, 10**8, 60, landing(far), far=len(far),
     )
     first = exchange(blocks, "gx")
 
-    far = (pair_dist.T, nbr_index.T, nbr_count[None, :], w_radial)
-    core, low, high, radial = kernel_call(
+    far = (pair_dist.T, nbr_index.T, nbr_count[None, :], w_radial, coords)
+    core, rim, cos_table, sin_table, radial = kernel_call(
         spread_body,
         (
-            like((with_y, feat), full), like((rim_z, feat), half), like((rim_z, feat), half),
-            like((slots, atoms, feat), half),
+            like((with_y, feat), full), like((2 * rim_z, feat), half), like((total, atoms), half),
+            like((total, atoms), half), like((slots, atoms, feat), half),
         ),
         (*far, base), 6 * 10**9, 60, (pltpu.VMEM((slots * basis_rows, atoms), full), *landing(far)), far=len(far),
     )
-    table, blocks = kernel_call(
-        second_body,
-        (like((with_x, feat), half), like((count_z, height + rim_z, feat), half)),
-        (first, base, low, high), 10**8, 8,
+    (blocks,) = kernel_call(
+        second_body, (like((count_z, height + rim_z, feat), half),), (first, rim), 10**8, 8
     )
     third = exchange(blocks, "gz")
+    table, packets = kernel_call(
+        pick_body, (like((with_x, feat), half), like((2, rim_y, feat), half)), (first, base, send_y), 2 * 10**9, 8
+    )
     core, low, high, share = kernel_call(
         third_body,
         (
             like((with_x, feat), full), like((height + 2 * rim_y, feat), half),
-            like((height + 2 * rim_y, feat), half), like((height, feat), half),
+            like((height + 2 * rim_y, feat), half), like((224, feat), half),
         ),
-        (third, table, core, send_y, send_z), 10**8, 8,
-    )
-    below, above = swap(low, high, "gy")
-    across = lax.ppermute(share, "gy", [(i, (i + 2) % count_y) for i in range(count_y)])
+        (third, packets, core, send_z), 10**8, 8,
+    )
+    early = lax.ppermute(share, "gy", [(2, 0)])
+    below_y, above_y = swap(low, high, "gy")
+    (partial,) = kernel_call(add_body, (like((height, feat), full),), (share, early), 10**11, 8)
+    (gathered,) = kernel_call(
+        gather_first_body, (like((atoms, feat), full),), (nbr_index.T, radial, table, partial), 10**3, 24, moved=10**3
+    )
+    (relay,) = kernel_call(
+        relay_body, (like((height, feat), half),), (above_y,), 10**6, 8
+    )
+    relay = lax.ppermute(relay, "gy", [(0, 3), (3, 2), (2, 1)])
     norm_factor = 1.0 / math.sqrt(atoms * count_x * count_y * count_z)
-    table, core, low, high, blocks = kernel_call(
+    core, low, high, blocks = kernel_call(
         lambda *refs: fourth_body(*refs, norm_factor),
         (
-            like((with_y, feat), half), like((atoms, feat), full), like((rim_z, feat), half),
-            like((rim_z, feat), half), like((count_x, tall, feat), half),
+            like((atoms, feat), full), like((rim_z, feat), half), like((rim_z, feat), half),
+            like((count_x, tall, feat), half),
         ),
-        (below, above, share, across, table, core, send_y, send_z, k_kernel.T), 10**8, 8,
-    )
-    below, above = swap(low, high, "gz")
+        (below_y, above_y, partial, relay, table, core, send_y, send_z, k_kernel.T, gathered), 10**8, 8,
+    )
+    below_z, above_z = swap(low, high, "gz")
     first = exchange(blocks, "gx")
     (gathered,) = kernel_call(
-        gather_body, (like((atoms, feat), full),), (nbr_index.T, radial, table, below, above), 6 * 10**9, 32
+        functools.partial(gather_more_body, with_x, slice(height, height + rim_y)), (like((atoms, feat), full),),
+        (nbr_index.T, radial, below_y, above_y, gathered), 2 * 10**9, 24,
+    )
+    (gathered,) = kernel_call(
+        functools.partial(gather_more_body, with_y, slice(0, rim_z)), (like((atoms, feat), full),),
+        (nbr_index.T, radial, below_z, above_z, gathered), 2 * 10**9, 24,
     )
     (update,) = kernel_call(
         update_body, (like((atoms, feat), half),),

time: 86.4 us -> 82 us (0.949)
  blocking collectives: 9.62 us -> 0 us
  waiting for transfers between devices: 10.3 us -> 14.4 us
  local copies, waits for them, and re-layouts: 4.09 us -> 0.9 us
  Pallas kernels: 15.5 us -> 17.8 us
  starting transfers between devices: 45.7 us -> 47.9 us
    all_to_all x1 -> x0, blocking collectives: 9.62 us -> none  [exchange(): return lax.all_to_all(blocks, axes, split_axis=0, concat_axis=0)]
    all_to_all x2 -> x3, waiting for transfers between devices: 6.47 us -> 13.9 us  [exchange(): return lax.all_to_all(blocks, axes, split_axis=0, concat_axis=0)]
    ppermute x2, starting transfers between devices: 7.45 us -> 14.1 us  [swap(): lax.ppermute(low, axis, backward)]
    ppermute x2, starting transfers between devices: 11.3 us -> 4.91 us  [swap(): lax.ppermute(high, axis, forward)]
    unnamed x26 -> x24, local copies, waits for them, and re-layouts: 4.09 us -> 0.9 us
    ppermute x1 -> x2, waiting for transfers between devices: 2.8 us -> 0.01 us  [the longest x1 0.01 us: on_device(): relay = lax.ppermute(relay, 'gy', [(0, 3), (3, 2), (2, 1)])]
    all_to_all x2 -> x3, starting transfers between devices: 16.7 us -> 19 us  [exchange(): return lax.all_to_all(blocks, axes, split_axis=0, concat_axis=0)]
    pallas_call x7 -> x12, Pallas kernels: 15.5 us -> 17.8 us  [kernel_call(): pl.pallas_call(body, out_shape=tuple(outs), in_specs=specs, out_specs=(pl...]
  transfers between devices with their start and end apart: 7 -> 9, of which waited for: 3 -> 4; matrix products, arithmetic and copies ran while one was open for 0% -> 0% of each run, Pallas kernels for 12% -> 15%
where the time goes in v4:
time: 82 us; the launch traced here: 81.3 us
  starting transfers between devices  47.9 us (58%)
  Pallas kernels  17.8 us (22%)
  waiting for transfers between devices  14.4 us (18%)
  local copies, waits for them, and re-layouts  0.9 us (1%)
    all_to_all x3, starting transfers between devices, exchange(): return lax.all_to_all(blocks, axes, split_axis=0, concat_axis=0)  19 us
    pallas_call x12, Pallas kernels, kernel_call(): pl.pallas_call(body, out_shape=tuple(outs), in_specs=specs, out_specs=(pl...  17.8 us
    ppermute x2, starting transfers between devices, swap(): lax.ppermute(low, axis, backward)  14.1 us
    all_to_all x3, waiting for transfers between devices, exchange(): return lax.all_to_all(blocks, axes, split_axis=0, concat_axis=0)  13.9 us
    ppermute x1, starting transfers between devices, on_device(): relay = lax.ppermute(relay, 'gy', [(0, 3), (3, 2), (2, 1)])  8.58 us
    ppermute x2, starting transfers between devices, swap(): lax.ppermute(high, axis, forward)  4.91 us
  transfers between devices with their start and end apart: 9, of which 4 were waited for; matrix products, arithmetic and copies ran while one was open for 0% of the time, Pallas kernels for 15%

profile of v4, /device:TPU:1, one launch (start us, length us, event | category | flops | bytes accessed | tf_op | source)
XLA Modules:
  0.0 81.3 jit_solution(12218233203850636036)
XLA Ops:
  0.0 2.5 %shard_map.136 = (bf16[128,128]{1,0:T(8,128)(2,1)}, bf16[32,80,128]{2,1,0:T(8,128)(2,1)}) custom-call(bf16[128,128]{1,0:T(8,128)(2,1)} %refs_0_.1, bf16[128,128]{1,0:T(8,128)(2,1)} %refs_1_.1, bf16[128,128]{1,0:T(8,128)(2,1)} %refs_2_.1, s32[2,64]{1,0:T(2,128)} %send_ref.3, f32[3,128]{1,0:T(4,128)} %refs_4_.3, bf16[32,128]{1,0:T(8,128)(2,1)} %bitcast.11), custom_call_target="tpu_custom_call" | custom-call | flops 100000000 | bytes 796672 | tf_op jit(solution)/shard_map/pallas_call | solution.py:23
  2.5 10.4 %all-to-all-start = ((bf16[32,80,128]{2,1,0:T(8,128)(2,1)}), bf16[32,80,128]{2,1,0:T(8,128)(2,1)S(1)}, u32[]{:S(2)}, u32[]{:S(2)}) async-start(bf16[32,80,128]{2,1,0:T(8,128)(2,1)} %get-tuple-element.22), calls=%async_computation | async-start | bytes 1310720 | tf_op jit(solution)/shard_map/all_to_all | solution.py:289
  12.9 0.0 copy-start.9
  13.0 0.0 copy-start.11
  13.0 7.0 %shard_map.137 = (f32[448,128]{1,0:T(8,128)}, bf16[256,128]{1,0:T(8,128)(2,1)}, bf16[1024,128]{1,0:T(8,128)(2,1)}, bf16[1024,128]{1,0:T(8,128)(2,1)}, bf16[64,128,128]{2,1,0:T(8,128)(2,1)}) custom-call(f32[64,128]{1,0:T(8,128)} %bitcast.10, s32[64,128]{1,0:T(8,128)} %bitcast.6, s32[1,128]{1,0:T(1,128)} %bitcast.12, bf16[20,128]{1,0:T(8,128)(2,1)} %refs_3_.3, ...), custom_call_target="tpu_custom_call" | custom-call | flops 6000000000 | bytes 3021824 | tf_op jit(solution)/shard_map/pallas_call | solution.py:23
  19.9 6.1 %all-to-all-done.first_ref = bf16[32,80,128]{2,1,0:T(8,128)(2,1)S(1)} async-done(((bf16[32,80,128]{2,1,0:T(8,128)(2,1)}), bf16[32,80,128]{2,1,0:T(8,128)(2,1)S(1)}, u32[]{:S(2)}, u32[]{:S(2)}) %all-to-all-start) | async-done | bytes 655392 | tf_op jit(solution)/shard_map/all_to_all | solution.py:289
  26.0 0.8 %copy-done.5 = bf16[256,128]{1,0:T(8,128)(2,1)S(1)} copy-done((bf16[256,128]{1,0:T(8,128)(2,1)S(1)}, bf16[256,128]{1,0:T(8,128)(2,1)}, u32[]{:S(2)}) %copy-start.5) | copy-done | bytes 65560
  26.8 0.7 shard_map.138
  27.5 3.7 %all-to-all-start.1 = ((bf16[4,144,128]{2,1,0:T(8,128)(2,1)}), bf16[4,144,128]{2,1,0:T(8,128)(2,1)S(1)}, u32[]{:S(2)}, u32[]{:S(2)}) async-start(bf16[4,144,128]{2,1,0:T(8,128)(2,1)} %shard_map.138), calls=%async_computation.1 | async-start | bytes 294912 | tf_op jit(solution)/shard_map/all_to_all | solution.py:289
  31.2 0.0 copy-done.9
  31.2 0.0 copy-done.11
  31.2 0.0 copy-start.8
  31.2 0.3 shard_map.139
  31.5 5.1 %all-to-all-done.1.third_ref = bf16[4,144,128]{2,1,0:T(8,128)(2,1)S(1)} async-done(((bf16[4,144,128]{2,1,0:T(8,128)(2,1)}), bf16[4,144,128]{2,1,0:T(8,128)(2,1)S(1)}, u32[]{:S(2)}, u32[]{:S(2)}) %all-to-all-start.1) | async-done | bytes 147488 | tf_op jit(solution)/shard_map/all_to_all | solution.py:289
  36.6 0.0 copy-done.3
  36.6 0.0 copy-done.8
  36.6 0.2 shard_map.140
  36.9 1.3 %collective-permute-start.2 = (bf16[224,128]{1,0:T(8,128)(2,1)S(1)}, bf16[224,128]{1,0:T(8,128)(2,1)S(1)}, u32[]{:S(2)}, u32[]{:S(2)}) collective-permute-start(bf16[224,128]{1,0:T(8,128)(2,1)S(1)} %get-tuple-element.29.left_ref), channel_id=1, source_target_pairs={{8,0},{9,1},{10,2},{11,3},{24,16},{25,17},{26,18},{27,19},{40,32},... | collective-permute-start | bytes 172040 | tf_op jit(solution)/shard_map/ppermute | solution.py:352
  38.2 10.0 %collective-permute-start.1 = (bf16[208,128]{1,0:T(8,128)(2,1)S(1)}, bf16[208,128]{1,0:T(8,128)(2,1)S(1)}, u32[]{:S(2)}, u32[]{:S(2)}) collective-permute-start(bf16[208,128]{1,0:T(8,128)(2,1)S(1)} %get-tuple-element.28), channel_id=1, source_target_pairs={{4,0},{8,4},{12,8},{0,12},{5,1},{9,5},{13,9},{1,13},{6,2},{10,6},{... | collective-permute-start | bytes 159752 | tf_op jit(solution)/shard_map/ppermute | solution.py:285
  48.2 1.9 %collective-permute-start = (bf16[208,128]{1,0:T(8,128)(2,1)S(1)}, bf16[208,128]{1,0:T(8,128)(2,1)S(1)}, u32[]{:S(2)}, u32[]{:S(2)}) collective-permute-start(bf16[208,128]{1,0:T(8,128)(2,1)S(1)} %get-tuple-element.27), channel_id=1, source_target_pairs={{0,4},{4,8},{8,12},{12,0},{1,5},{5,9},{9,13},{13,1},{2,6},{6,10},{... | collective-permute-start | bytes 159752 | tf_op jit(solution)/shard_map/ppermute | solution.py:285
  50.1 0.5 collective-permute-done.1.above_ref.refs_1_
  50.6 8.6 %collective-permute-start.3 = (bf16[16,128]{1,0:T(8,128)(2,1)S(1)}, bf16[16,128]{1,0:T(8,128)(2,1)S(1)}, u32[]{:S(2)}, u32[]{:S(2)}) collective-permute-start(bf16[16,128]{1,0:T(8,128)(2,1)S(1)} %shard_map.142), channel_id=1, source_target_pairs={{0,12},{12,8},{8,4},{1,13},{13,9},{9,5},{2,14},{14,10},{10,6},{3,1... | collective-permute-start | bytes 12296 | tf_op jit(solution)/shard_map/ppermute | solution.py:361
  59.2 0.0 collective-permute-done.2.right_ref
  59.2 0.0 copy-start.4
  59.2 0.0 copy-done
  59.3 0.0 copy-done.6
  59.3 1.6 %shard_map.143.refs_9_.sofar_ref = f32[128,128]{1,0:T(8,128)S(1)} custom-call(s32[64,128]{1,0:T(8,128)S(1)} %bitcast.7, bf16[64,128,128]{2,1,0:T(8,128)(2,1)S(1)} %copy-done, bf16[256,128]{1,0:T(8,128)(2,1)S(1)} %get-tuple-element.30.table_ref.refs_4_, f32[16,128]{1,0:T(8,128)S(1)} %shard_map.141.order_ref.refs_2_), custom_call_target="tpu_custom_call" | custom-call | flops 1000 | bytes 1000 | tf_op jit(solution)/shard_map/pallas_call | solution.py:23
  60.8 0.0 collective-permute-done.refs_0_.below_ref
  60.9 0.0 collective-permute-done.3.refs_3_
  60.9 0.0 copy-done.4
  60.9 1.3 %shard_map.144 = (f32[128,128]{1,0:T(8,128)S(1)}, bf16[128,128]{1,0:T(8,128)(2,1)S(1)}, bf16[128,128]{1,0:T(8,128)(2,1)S(1)}, bf16[32,80,128]{2,1,0:T(8,128)(2,1)}) custom-call(bf16[208,128]{1,0:T(8,128)(2,1)S(1)} %collective-permute-done.refs_0_.below_ref, bf16[208,128]{1,0:T(8,128)(2,1)S(1)} %collective-permute-done.1.above_ref.refs_1_, ...), custom_call_target="tpu_custom_call" | custom-call | flops 100000000 | bytes 1300224 | tf_op jit(solution)/shard_map/pallas_call | solution.py:23
  62.2 4.9 %all-to-all-start.2 = ((bf16[32,80,128]{2,1,0:T(8,128)(2,1)}), bf16[32,80,128]{2,1,0:T(8,128)(2,1)S(1)}, u32[]{:S(2)}, u32[]{:S(2)}) async-start(bf16[32,80,128]{2,1,0:T(8,128)(2,1)} %get-tuple-element.33), calls=%async_computation.2 | async-start | bytes 1310720 | tf_op jit(solution)/shard_map/all_to_all | solution.py:289
  67.1 3.0 %collective-permute-start.4 = (bf16[128,128]{1,0:T(8,128)(2,1)S(1)}, bf16[128,128]{1,0:T(8,128)(2,1)S(1)}, u32[]{:S(2)}, u32[]{:S(2)}) collective-permute-start(bf16[128,128]{1,0:T(8,128)(2,1)S(1)} %get-tuple-element.35), channel_id=1, source_target_pairs={{0,1},{1,2},{2,3},{3,0},{4,5},{5,6},{6,7},{7,4},{8,9},{9,10},{10,1... | collective-permute-start | bytes 98312 | tf_op jit(solution)/shard_map/ppermute | solution.py:285
  70.1 4.1 %collective-permute-start.5 = (bf16[128,128]{1,0:T(8,128)(2,1)S(1)}, bf16[128,128]{1,0:T(8,128)(2,1)S(1)}, u32[]{:S(2)}, u32[]{:S(2)}) collective-permute-start(bf16[128,128]{1,0:T(8,128)(2,1)S(1)} %get-tuple-element.36), channel_id=1, source_target_pairs={{1,0},{2,1},{3,2},{0,3},{5,4},{6,5},{7,6},{4,7},{9,8},{10,9},{11,1... | collective-permute-start | bytes 98312 | tf_op jit(solution)/shard_map/ppermute | solution.py:285
  74.2 1.6 %shard_map.145.sofar_ref = f32[128,128]{1,0:T(8,128)S(1)} custom-call(s32[64,128]{1,0:T(8,128)S(1)} %bitcast.8, bf16[64,128,128]{2,1,0:T(8,128)(2,1)S(1)} %copy-done, bf16[208,128]{1,0:T(8,128)(2,1)S(1)} %collective-permute-done.refs_0_.below_ref, bf16[208,128]{1,0:T(8,128)(2,1)S(1)} %collective-permute-done.1.above_ref.refs_1_, ...), custom_call_target="tpu_custom_call" | custom-call | flops 2000000000 | bytes 2367488 | tf_op jit(solution)/shard_map/pallas_call | solution.py:23
  75.8 0.0 copy-start.1
  75.8 0.0 copy-start.2
  75.8 0.0 copy-start.7
  75.8 0.0 copy-start.10
  75.8 0.0 collective-permute-done.4.below_ref
  75.9 0.0 collective-permute-done.5.above_ref
  75.9 1.6 %shard_map.146.gathered_ref = f32[128,128]{1,0:T(8,128)S(1)} custom-call(s32[64,128]{1,0:T(8,128)S(1)} %bitcast.9, bf16[64,128,128]{2,1,0:T(8,128)(2,1)S(1)} %copy-done, bf16[128,128]{1,0:T(8,128)(2,1)S(1)} %collective-permute-done.4.below_ref, bf16[128,128]{1,0:T(8,128)(2,1)S(1)} %collective-permute-done.5.above_ref, f32[128,128]{1,0:T(8,128)S(1)} %shard_map.145.sofar_ref), custom_call_target="tpu_custom_call" | custom-call | flops 2000000000 | bytes 2326528 | tf_op jit(solution)/shard_map/pallas_call | solution.py:23
  77.4 2.7 %all-to-all-done.2.first_ref = bf16[32,80,128]{2,1,0:T(8,128)(2,1)S(1)} async-done(((bf16[32,80,128]{2,1,0:T(8,128)(2,1)}), bf16[32,80,128]{2,1,0:T(8,128)(2,1)S(1)}, u32[]{:S(2)}, u32[]{:S(2)}) %all-to-all-start.2) | async-done | bytes 655392 | tf_op jit(solution)/shard_map/all_to_all | solution.py:289
  80.2 0.0 copy-done.1
  80.2 0.0 copy-done.2
  80.2 0.0 copy-done.7
  80.2 0.0 copy-done.10
  80.2 1.1 %shard_map.147 = bf16[128,128]{1,0:T(8,128)(2,1)} custom-call(bf16[32,80,128]{2,1,0:T(8,128)(2,1)S(1)} %all-to-all-done.2.first_ref, f32[128,128]{1,0:T(8,128)S(1)} %get-tuple-element.34.core_ref, s32[2,64]{1,0:T(2,128)S(1)} %copy-done.10, f32[128,128]{1,0:T(8,128)S(1)} %shard_map.146.gathered_ref, bf16[1024,128]{1,0:T(8,128)(2,1)S(1)} %copy-done.1, ...), custom_call_target="tpu_custom_call" | custom-call | flops 100000000 | bytes 1352192 | tf_op jit(solution)/shard_map/pallas_call | solution.py:23
  (6 shorter events, 0.0 us)
Async XLA Ops:
  2.5 23.5 %all-to-all-start = ((bf16[32,80,128]{2,1,0:T(8,128)(2,1)}), bf16[32,80,128]{2,1,0:T(8,128)(2,1)S(1)}, u32[]{:S(2)}, u32[]{:S(2)}) async-start(bf16[32,80,128]{2,1,0:T(8,128)(2,1)} %get-tuple-element.22), calls=%async_computation | async-start | bytes 1310720 | tf_op jit(solution)/shard_map/all_to_all | solution.py:289
  12.9 18.2 %copy-start.9 = (s32[2,96]{1,0:T(2,128)S(1)}, s32[2,96]{1,0:T(2,128)}, u32[]{:S(2)}) copy-start(s32[2,96]{1,0:T(2,128)} %refs_6_.1) | copy-start | bytes 2308
  13.0 18.2 %copy-start.11 = (bf16[128,128]{1,0:T(8,128)(2,1)S(1)}, bf16[128,128]{1,0:T(8,128)(2,1)}, u32[]{:S(2)}) copy-start(bf16[128,128]{1,0:T(8,128)(2,1)} %get-tuple-element.23.refs_5_.base_ref) | copy-start | bytes 98308
  26.0 0.8 %copy-start.5 = (bf16[256,128]{1,0:T(8,128)(2,1)S(1)}, bf16[256,128]{1,0:T(8,128)(2,1)}, u32[]{:S(2)}) copy-start(bf16[256,128]{1,0:T(8,128)(2,1)} %get-tuple-element.24.rim_ref) | copy-start | bytes 196612
  27.5 9.1 %all-to-all-start.1 = ((bf16[4,144,128]{2,1,0:T(8,128)(2,1)}), bf16[4,144,128]{2,1,0:T(8,128)(2,1)S(1)}, u32[]{:S(2)}, u32[]{:S(2)}) async-start(bf16[4,144,128]{2,1,0:T(8,128)(2,1)} %shard_map.138), calls=%async_computation.1 | async-start | bytes 294912 | tf_op jit(solution)/shard_map/all_to_all | solution.py:289
  31.2 5.5 %copy-start.3 = (f32[448,128]{1,0:T(8,128)S(1)}, f32[448,128]{1,0:T(8,128)}, u32[]{:S(2)}) copy-start(f32[448,128]{1,0:T(8,128)} %get-tuple-element.26.core_ref) | copy-start | bytes 688132
  31.2 5.5 %copy-start.8 = (s32[2,128]{1,0:T(2,128)S(1)}, s32[2,128]{1,0:T(2,128)}, u32[]{:S(2)}) copy-start(s32[2,128]{1,0:T(2,128)} %refs_7_.1) | copy-start | bytes 3076
  36.9 22.3 %collective-permute-start.2 = (bf16[224,128]{1,0:T(8,128)(2,1)S(1)}, bf16[224,128]{1,0:T(8,128)(2,1)S(1)}, u32[]{:S(2)}, u32[]{:S(2)}) collective-permute-start(bf16[224,128]{1,0:T(8,128)(2,1)S(1)} %get-tuple-element.29.left_ref), channel_id=1, source_target_pairs={{8,0},{9,1},{10,2},{11,3},{24,16},{25,17},{26,18},{27,19},{40,32},... | collective-permute-start | bytes 172040 | tf_op jit(solution)/shard_map/ppermute | solution.py:352
  38.2 12.4 %collective-permute-start.1 = (bf16[208,128]{1,0:T(8,128)(2,1)S(1)}, bf16[208,128]{1,0:T(8,128)(2,1)S(1)}, u32[]{:S(2)}, u32[]{:S(2)}) collective-permute-start(bf16[208,128]{1,0:T(8,128)(2,1)S(1)} %get-tuple-element.28), channel_id=1, source_target_pairs={{4,0},{8,4},{12,8},{0,12},{5,1},{9,5},{13,9},{1,13},{6,2},{10,6},{... | collective-permute-start | bytes 159752 | tf_op jit(solution)/shard_map/ppermute | solution.py:285
  48.2 12.7 %collective-permute-start = (bf16[208,128]{1,0:T(8,128)(2,1)S(1)}, bf16[208,128]{1,0:T(8,128)(2,1)S(1)}, u32[]{:S(2)}, u32[]{:S(2)}) collective-permute-start(bf16[208,128]{1,0:T(8,128)(2,1)S(1)} %get-tuple-element.27), channel_id=1, source_target_pairs={{0,4},{4,8},{8,12},{12,0},{1,5},{5,9},{9,13},{13,1},{2,6},{6,10},{... | collective-permute-start | bytes 159752 | tf_op jit(solution)/shard_map/ppermute | solution.py:285
  50.6 8.6 %copy-start = (bf16[64,128,128]{2,1,0:T(8,128)(2,1)S(1)}, bf16[64,128,128]{2,1,0:T(8,128)(2,1)}, u32[]{:S(2)}) copy-start(bf16[64,128,128]{2,1,0:T(8,128)(2,1)} %get-tuple-element.32.radial_ref) | copy-start | bytes 6291460
  50.6 8.6 %copy-start.6 = (s32[128,64]{0,1:T(8,128)S(1)}, s32[128,64]{0,1:T(8,128)}, u32[]{:S(2)}) copy-start(s32[128,64]{0,1:T(8,128)} %param.17) | copy-start | bytes 98308
  50.6 10.2 %collective-permute-start.3 = (bf16[16,128]{1,0:T(8,128)(2,1)S(1)}, bf16[16,128]{1,0:T(8,128)(2,1)S(1)}, u32[]{:S(2)}, u32[]{:S(2)}) collective-permute-start(bf16[16,128]{1,0:T(8,128)(2,1)S(1)} %shard_map.142), channel_id=1, source_target_pairs={{0,12},{12,8},{8,4},{1,13},{13,9},{9,5},{2,14},{14,10},{10,6},{3,1... | collective-permute-start | bytes 12296 | tf_op jit(solution)/shard_map/ppermute | solution.py:361
  59.2 1.6 %copy-start.4 = (f32[1024,32]{0,1:T(8,128)S(1)}, f32[1024,32]{0,1:T(8,128)}, u32[]{:S(2)}) copy-start(f32[1024,32]{0,1:T(8,128)} %param.26) | copy-start | bytes 393220
  62.2 18.0 %all-to-all-start.2 = ((bf16[32,80,128]{2,1,0:T(8,128)(2,1)}), bf16[32,80,128]{2,1,0:T(8,128)(2,1)S(1)}, u32[]{:S(2)}, u32[]{:S(2)}) async-start(bf16[32,80,128]{2,1,0:T(8,128)(2,1)} %get-tuple-element.33), calls=%async_computation.2 | async-start | bytes 1310720 | tf_op jit(solution)/shard_map/all_to_all | solution.py:289
  67.1 8.7 %collective-permute-start.4 = (bf16[128,128]{1,0:T(8,128)(2,1)S(1)}, bf16[128,128]{1,0:T(8,128)(2,1)S(1)}, u32[]{:S(2)}, u32[]{:S(2)}) collective-permute-start(bf16[128,128]{1,0:T(8,128)(2,1)S(1)} %get-tuple-element.35), channel_id=1, source_target_pairs={{0,1},{1,2},{2,3},{3,0},{4,5},{5,6},{6,7},{7,4},{8,9},{9,10},{10,1... | collective-permute-start | bytes 98312 | tf_op jit(solution)/shard_map/ppermute | solution.py:285
  70.1 5.7 %collective-permute-start.5 = (bf16[128,128]{1,0:T(8,128)(2,1)S(1)}, bf16[128,128]{1,0:T(8,128)(2,1)S(1)}, u32[]{:S(2)}, u32[]{:S(2)}) collective-permute-start(bf16[128,128]{1,0:T(8,128)(2,1)S(1)} %get-tuple-element.36), channel_id=1, source_target_pairs={{1,0},{2,1},{3,2},{0,3},{5,4},{6,5},{7,6},{4,7},{9,8},{10,9},{11,1... | collective-permute-start | bytes 98312 | tf_op jit(solution)/shard_map/ppermute | solution.py:285
  75.8 4.4 %copy-start.1 = (bf16[1024,128]{1,0:T(8,128)(2,1)S(1)}, bf16[1024,128]{1,0:T(8,128)(2,1)}, u32[]{:S(2)}) copy-start(bf16[1024,128]{1,0:T(8,128)(2,1)} %get-tuple-element.37.cos_ref) | copy-start | bytes 786436
  75.8 4.4 %copy-start.2 = (bf16[1024,128]{1,0:T(8,128)(2,1)S(1)}, bf16[1024,128]{1,0:T(8,128)(2,1)}, u32[]{:S(2)}) copy-start(bf16[1024,128]{1,0:T(8,128)(2,1)} %get-tuple-element.38.sin_ref) | copy-start | bytes 786436
  75.8 4.4 %copy-start.7 = (bf16[32,128]{1,0:T(8,128)(2,1)S(1)}, bf16[32,128]{1,0:T(8,128)(2,1)}, u32[]{:S(2)}) copy-start(bf16[32,128]{1,0:T(8,128)(2,1)} %ewald_ref.1) | copy-start | bytes 24580
  75.8 4.4 %copy-start.10 = (s32[2,64]{1,0:T(2,128)S(1)}, s32[2,64]{1,0:T(2,128)}, u32[]{:S(2)}) copy-start(s32[2,64]{1,0:T(2,128)} %send_ref.3) | copy-start | bytes 1540

commit v5 on v4

--- a/solution.py
+++ b/solution.py
@@ -187,7 +187,7 @@
     half = packets_ref.shape[1]
     height = low_ref.shape[0] - 2 * half
     share = jnp.sum(third_ref[:, :height].astype(jnp.float32), axis=0).astype(share_ref.dtype)
-    share_ref[:height] = share
+    share_ref[...] = share
     below, above = sides("gz")
     spread = core_ref[...] + placed(
         send_z_ref[...], third_ref[below, height:], third_ref[above, height:], core_ref.shape[0]
@@ -199,11 +199,6 @@
         packet_ref[:height] = share
         packet_ref[height : height + half] = packets_ref[side]
         packet_ref[height + half :] = spread[rows].astype(jnp.bfloat16)
-
-
-def add_body(left_ref, right_ref, total_ref):
-    height = total_ref.shape[0]
-    total_ref[...] = left_ref[:height].astype(jnp.float32) + right_ref[:height].astype(jnp.float32)
 
 
 def relay_body(above_ref, relay_ref):
@@ -250,7 +245,7 @@
     return total
 
 
-def gather_first_body(nbr_ref, radial_ref, table_ref, order_ref, gathered_ref):
+def gather_first_body(nbr_ref, radial_ref, table_ref, gathered_ref):
     gathered_ref[...] = gather_rows(0, table_ref[...], nbr_ref, radial_ref)
 
 
@@ -345,20 +340,18 @@
         third_body,
         (
             like((with_x, feat), full), like((height + 2 * rim_y, feat), half),
-            like((height + 2 * rim_y, feat), half), like((224, feat), half),
+            like((height + 2 * rim_y, feat), half), like((height, feat), half),
         ),
         (third, packets, core, send_z), 10**8, 8,
     )
-    early = lax.ppermute(share, "gy", [(2, 0)])
     below_y, above_y = swap(low, high, "gy")
-    (partial,) = kernel_call(add_body, (like((height, feat), full),), (share, early), 10**11, 8)
     (gathered,) = kernel_call(
-        gather_first_body, (like((atoms, feat), full),), (nbr_index.T, radial, table, partial), 10**3, 24, moved=10**3
+        gather_first_body, (like((atoms, feat), full),), (nbr_index.T, radial, table), 10**3, 24, moved=10**3
     )
     (relay,) = kernel_call(
-        relay_body, (like((height, feat), half),), (above_y,), 10**6, 8
-    )
-    relay = lax.ppermute(relay, "gy", [(0, 3), (3, 2), (2, 1)])
+        relay_body, (like((height, feat), half),), (below_y,), 10**6, 8
+    )
+    relay = lax.ppermute(relay, "gy", [(i, (i + 1) % count_y) for i in range(count_y)])
     norm_factor = 1.0 / math.sqrt(atoms * count_x * count_y * count_z)
     core, low, high, blocks = kernel_call(
         lambda *refs: fourth_body(*refs, norm_factor),
@@ -366,7 +359,7 @@
             like((atoms, feat), full), like((rim_z, feat), half), like((rim_z, feat), half),
             like((count_x, tall, feat), half),
         ),
-        (below_y, above_y, partial, relay, table, core, send_y, send_z, k_kernel.T, gathered), 10**8, 8,
+        (below_y, above_y, share, relay, table, core, send_y, send_z, k_kernel.T, gathered), 10**8, 8,
     )
     below_z, above_z = swap(low, high, "gz")
     first = exchange(blocks, "gx")

time: 82 us -> 81.2 us (level)
    ppermute x2, starting transfers between devices: 4.91 us -> 12.9 us  [swap(): lax.ppermute(high, axis, forward)]
    ppermute x2, starting transfers between devices: 14.1 us -> 6.7 us  [swap(): lax.ppermute(low, axis, backward)]
    ppermute x2 -> x1, starting transfers between devices: 9.87 us -> 7.47 us  [on_device(): lax.ppermute(relay, 'gy', [(i, (i + 1) % count_y) for i in range(count_y)])]
    all_to_all x3, starting transfers between devices: 19 us -> 20.5 us  [exchange(): return lax.all_to_all(blocks, axes, split_axis=0, concat_axis=0)]
    pallas_call x12 -> x11, Pallas kernels: 17.8 us -> 17.8 us  [kernel_call(): pl.pallas_call(body, out_shape=tuple(outs), in_specs=specs, out_specs=(pl...]
  transfers between devices with their start and end apart: 9 -> 8, of which waited for: 4 -> 4; matrix products, arithmetic and copies ran while one was open for 0% -> 0% of each run, Pallas kernels for 15% -> 15%
where the time goes in v5:
time: 81.2 us; the launch traced here: 80.4 us
  starting transfers between devices  47.5 us (58%)
  Pallas kernels  17.8 us (22%)
  waiting for transfers between devices  13.9 us (17%)
  local copies, waits for them, and re-layouts  0.9 us (1%)
    all_to_all x3, starting transfers between devices, exchange(): return lax.all_to_all(blocks, axes, split_axis=0, concat_axis=0)  20.5 us
    pallas_call x11, Pallas kernels, kernel_call(): pl.pallas_call(body, out_shape=tuple(outs), in_specs=specs, out_specs=(pl...  17.8 us
    all_to_all x3, waiting for transfers between devices, exchange(): return lax.all_to_all(blocks, axes, split_axis=0, concat_axis=0)  13.6 us
    ppermute x2, starting transfers between devices, swap(): lax.ppermute(high, axis, forward)  12.9 us
    ppermute x1, starting transfers between devices, on_device(): lax.ppermute(relay, 'gy', [(i, (i + 1) % count_y) for i in range(count_y)])  7.47 us
    ppermute x2, starting transfers between devices, swap(): lax.ppermute(low, axis, backward)  6.7 us
  transfers between devices with their start and end apart: 8, of which 4 were waited for; matrix products, arithmetic and copies ran while one was open for 0% of the time, Pallas kernels for 15%

profile of v5, /device:TPU:1, one launch (start us, length us, event | category | flops | bytes accessed | tf_op | source)
XLA Modules:
  0.0 80.4 jit_solution(12354624811332238296)
XLA Ops:
  0.0 2.5 %shard_map.136 = (bf16[128,128]{1,0:T(8,128)(2,1)}, bf16[32,80,128]{2,1,0:T(8,128)(2,1)}) custom-call(bf16[128,128]{1,0:T(8,128)(2,1)} %refs_0_.1, bf16[128,128]{1,0:T(8,128)(2,1)} %refs_1_.1, bf16[128,128]{1,0:T(8,128)(2,1)} %refs_2_.1, s32[2,64]{1,0:T(2,128)} %send_ref.3, f32[3,128]{1,0:T(4,128)} %refs_4_.3, bf16[32,128]{1,0:T(8,128)(2,1)} %bitcast.11), custom_call_target="tpu_custom_call" | custom-call | flops 100000000 | bytes 796672 | tf_op jit(solution)/shard_map/pallas_call | solution.py:23
  2.5 10.4 %all-to-all-start = ((bf16[32,80,128]{2,1,0:T(8,128)(2,1)}), bf16[32,80,128]{2,1,0:T(8,128)(2,1)S(1)}, u32[]{:S(2)}, u32[]{:S(2)}) async-start(bf16[32,80,128]{2,1,0:T(8,128)(2,1)} %get-tuple-element.22), calls=%async_computation | async-start | bytes 1310720 | tf_op jit(solution)/shard_map/all_to_all | solution.py:284
  13.0 0.0 copy-start.9
  13.0 0.0 copy-start.11
  13.0 7.0 %shard_map.137 = (f32[448,128]{1,0:T(8,128)}, bf16[256,128]{1,0:T(8,128)(2,1)}, bf16[1024,128]{1,0:T(8,128)(2,1)}, bf16[1024,128]{1,0:T(8,128)(2,1)}, bf16[64,128,128]{2,1,0:T(8,128)(2,1)}) custom-call(f32[64,128]{1,0:T(8,128)} %bitcast.10, s32[64,128]{1,0:T(8,128)} %bitcast.6, s32[1,128]{1,0:T(1,128)} %bitcast.12, bf16[20,128]{1,0:T(8,128)(2,1)} %refs_3_.3, ...), custom_call_target="tpu_custom_call" | custom-call | flops 6000000000 | bytes 3021824 | tf_op jit(solution)/shard_map/pallas_call | solution.py:23
  19.9 6.1 %all-to-all-done.first_ref = bf16[32,80,128]{2,1,0:T(8,128)(2,1)S(1)} async-done(((bf16[32,80,128]{2,1,0:T(8,128)(2,1)}), bf16[32,80,128]{2,1,0:T(8,128)(2,1)S(1)}, u32[]{:S(2)}, u32[]{:S(2)}) %all-to-all-start) | async-done | bytes 655392 | tf_op jit(solution)/shard_map/all_to_all | solution.py:284
  26.0 0.8 %copy-done.5 = bf16[256,128]{1,0:T(8,128)(2,1)S(1)} copy-done((bf16[256,128]{1,0:T(8,128)(2,1)S(1)}, bf16[256,128]{1,0:T(8,128)(2,1)}, u32[]{:S(2)}) %copy-start.5) | copy-done | bytes 65560
  26.8 0.7 shard_map.138
  27.5 3.7 %all-to-all-start.1 = ((bf16[4,144,128]{2,1,0:T(8,128)(2,1)}), bf16[4,144,128]{2,1,0:T(8,128)(2,1)S(1)}, u32[]{:S(2)}, u32[]{:S(2)}) async-start(bf16[4,144,128]{2,1,0:T(8,128)(2,1)} %shard_map.138), calls=%async_computation.1 | async-start | bytes 294912 | tf_op jit(solution)/shard_map/all_to_all | solution.py:284
  31.2 0.0 copy-done.9
  31.2 0.0 copy-done.11
  31.2 0.0 copy-start.8
  31.2 0.0 copy-start
  31.2 0.0 copy-start.6
  31.2 0.3 shard_map.139
  31.6 0.0 copy-start.4
  31.6 5.1 %all-to-all-done.1.third_ref = bf16[4,144,128]{2,1,0:T(8,128)(2,1)S(1)} async-done(((bf16[4,144,128]{2,1,0:T(8,128)(2,1)}), bf16[4,144,128]{2,1,0:T(8,128)(2,1)S(1)}, u32[]{:S(2)}, u32[]{:S(2)}) %all-to-all-start.1) | async-done | bytes 147488 | tf_op jit(solution)/shard_map/all_to_all | solution.py:284
  36.6 0.0 copy-done.3
  36.6 0.0 copy-done.8
  36.7 0.2 shard_map.140
  36.9 8.8 %collective-permute-start = (bf16[208,128]{1,0:T(8,128)(2,1)S(1)}, bf16[208,128]{1,0:T(8,128)(2,1)S(1)}, u32[]{:S(2)}, u32[]{:S(2)}) collective-permute-start(bf16[208,128]{1,0:T(8,128)(2,1)S(1)} %get-tuple-element.27), channel_id=1, source_target_pairs={{0,4},{4,8},{8,12},{12,0},{1,5},{5,9},{9,13},{13,1},{2,6},{6,10},{... | collective-permute-start | bytes 159752 | tf_op jit(solution)/shard_map/ppermute | solution.py:280
  45.7 3.7 %collective-permute-start.1 = (bf16[208,128]{1,0:T(8,128)(2,1)S(1)}, bf16[208,128]{1,0:T(8,128)(2,1)S(1)}, u32[]{:S(2)}, u32[]{:S(2)}) collective-permute-start(bf16[208,128]{1,0:T(8,128)(2,1)S(1)} %get-tuple-element.28), channel_id=1, source_target_pairs={{4,0},{8,4},{12,8},{0,12},{5,1},{9,5},{13,9},{1,13},{6,2},{10,6},{... | collective-permute-start | bytes 159752 | tf_op jit(solution)/shard_map/ppermute | solution.py:280
  49.4 0.0 collective-permute-done.above_ref.refs_0_.below_ref
  49.4 7.5 %collective-permute-start.2 = (bf16[16,128]{1,0:T(8,128)(2,1)S(1)}, bf16[16,128]{1,0:T(8,128)(2,1)S(1)}, u32[]{:S(2)}, u32[]{:S(2)}) collective-permute-start(bf16[16,128]{1,0:T(8,128)(2,1)S(1)} %shard_map.141), channel_id=1, source_target_pairs={{0,4},{4,8},{8,12},{12,0},{1,5},{5,9},{9,13},{13,1},{2,6},{6,10},{... | collective-permute-start | bytes 12296 | tf_op jit(solution)/shard_map/ppermute | solution.py:354
  56.9 0.0 copy-done
  56.9 0.0 copy-done.6
  56.9 1.6 %shard_map.142.refs_9_.sofar_ref = f32[128,128]{1,0:T(8,128)S(1)} custom-call(s32[64,128]{1,0:T(8,128)S(1)} %bitcast.7, bf16[64,128,128]{2,1,0:T(8,128)(2,1)S(1)} %copy-done, bf16[256,128]{1,0:T(8,128)(2,1)S(1)} %get-tuple-element.30.table_ref.refs_4_), custom_call_target="tpu_custom_call" | custom-call | flops 1000 | bytes 1000 | tf_op jit(solution)/shard_map/pallas_call | solution.py:23
  58.5 0.0 collective-permute-done.1.refs_1_.above_ref
  58.5 0.0 collective-permute-done.2.refs_3_
  58.5 0.0 copy-done.4
  58.6 1.3 %shard_map.143 = (f32[128,128]{1,0:T(8,128)S(1)}, bf16[128,128]{1,0:T(8,128)(2,1)S(1)}, bf16[128,128]{1,0:T(8,128)(2,1)S(1)}, bf16[32,80,128]{2,1,0:T(8,128)(2,1)}) custom-call(bf16[208,128]{1,0:T(8,128)(2,1)S(1)} %collective-permute-done.above_ref.refs_0_.below_ref, bf16[208,128]{1,0:T(8,128)(2,1)S(1)} %collective-permute-done.1.refs_1_.above_ref, ...), custom_call_target="tpu_custom_call" | custom-call | flops 100000000 | bytes 1296128 | tf_op jit(solution)/shard_map/pallas_call | solution.py:23
  59.9 6.4 %all-to-all-start.2 = ((bf16[32,80,128]{2,1,0:T(8,128)(2,1)}), bf16[32,80,128]{2,1,0:T(8,128)(2,1)S(1)}, u32[]{:S(2)}, u32[]{:S(2)}) async-start(bf16[32,80,128]{2,1,0:T(8,128)(2,1)} %get-tuple-element.33), calls=%async_computation.2 | async-start | bytes 1310720 | tf_op jit(solution)/shard_map/all_to_all | solution.py:284
  66.3 4.1 %collective-permute-start.3 = (bf16[128,128]{1,0:T(8,128)(2,1)S(1)}, bf16[128,128]{1,0:T(8,128)(2,1)S(1)}, u32[]{:S(2)}, u32[]{:S(2)}) collective-permute-start(bf16[128,128]{1,0:T(8,128)(2,1)S(1)} %get-tuple-element.35), channel_id=1, source_target_pairs={{0,1},{1,2},{2,3},{3,0},{4,5},{5,6},{6,7},{7,4},{8,9},{9,10},{10,1... | collective-permute-start | bytes 98312 | tf_op jit(solution)/shard_map/ppermute | solution.py:280
  70.3 3.0 %collective-permute-start.4 = (bf16[128,128]{1,0:T(8,128)(2,1)S(1)}, bf16[128,128]{1,0:T(8,128)(2,1)S(1)}, u32[]{:S(2)}, u32[]{:S(2)}) collective-permute-start(bf16[128,128]{1,0:T(8,128)(2,1)S(1)} %get-tuple-element.36), channel_id=1, source_target_pairs={{1,0},{2,1},{3,2},{0,3},{5,4},{6,5},{7,6},{4,7},{9,8},{10,9},{11,1... | collective-permute-start | bytes 98312 | tf_op jit(solution)/shard_map/ppermute | solution.py:280
  73.4 1.6 %shard_map.144.sofar_ref = f32[128,128]{1,0:T(8,128)S(1)} custom-call(s32[64,128]{1,0:T(8,128)S(1)} %bitcast.8, bf16[64,128,128]{2,1,0:T(8,128)(2,1)S(1)} %copy-done, bf16[208,128]{1,0:T(8,128)(2,1)S(1)} %collective-permute-done.above_ref.refs_0_.below_ref, bf16[208,128]{1,0:T(8,128)(2,1)S(1)} %collective-permute-done.1.refs_1_.above_ref, ...), custom_call_target="tpu_custom_call" | custom-call | flops 2000000000 | bytes 2367488 | tf_op jit(solution)/shard_map/pallas_call | solution.py:23
  74.9 0.0 copy-start.1
  74.9 0.0 copy-start.2
  75.0 0.0 copy-start.7
  75.0 0.0 copy-start.10
  75.0 0.0 collective-permute-done.3.below_ref
  75.0 0.3 collective-permute-done.4.above_ref
  75.3 1.6 %shard_map.145.gathered_ref = f32[128,128]{1,0:T(8,128)S(1)} custom-call(s32[64,128]{1,0:T(8,128)S(1)} %bitcast.9, bf16[64,128,128]{2,1,0:T(8,128)(2,1)S(1)} %copy-done, bf16[128,128]{1,0:T(8,128)(2,1)S(1)} %collective-permute-done.3.below_ref, bf16[128,128]{1,0:T(8,128)(2,1)S(1)} %collective-permute-done.4.above_ref, f32[128,128]{1,0:T(8,128)S(1)} %shard_map.144.sofar_ref), custom_call_target="tpu_custom_call" | custom-call | flops 2000000000 | bytes 2326528 | tf_op jit(solution)/shard_map/pallas_call | solution.py:23
  76.9 2.4 %all-to-all-done.2.first_ref = bf16[32,80,128]{2,1,0:T(8,128)(2,1)S(1)} async-done(((bf16[32,80,128]{2,1,0:T(8,128)(2,1)}), bf16[32,80,128]{2,1,0:T(8,128)(2,1)S(1)}, u32[]{:S(2)}, u32[]{:S(2)}) %all-to-all-start.2) | async-done | bytes 655392 | tf_op jit(solution)/shard_map/all_to_all | solution.py:284
  79.3 0.0 copy-done.1
  79.3 0.0 copy-done.2
  79.3 0.0 copy-done.7
  79.3 0.0 copy-done.10
  79.3 1.1 %shard_map.146 = bf16[128,128]{1,0:T(8,128)(2,1)} custom-call(bf16[32,80,128]{2,1,0:T(8,128)(2,1)S(1)} %all-to-all-done.2.first_ref, f32[128,128]{1,0:T(8,128)S(1)} %get-tuple-element.34.core_ref, s32[2,64]{1,0:T(2,128)S(1)} %copy-done.10, f32[128,128]{1,0:T(8,128)S(1)} %shard_map.145.gathered_ref, bf16[1024,128]{1,0:T(8,128)(2,1)S(1)} %copy-done.1, ...), custom_call_target="tpu_custom_call" | custom-call | flops 100000000 | bytes 1352192 | tf_op jit(solution)/shard_map/pallas_call | solution.py:23
  (3 shorter events, 0.0 us)
Async XLA Ops:
  2.5 23.5 %all-to-all-start = ((bf16[32,80,128]{2,1,0:T(8,128)(2,1)}), bf16[32,80,128]{2,1,0:T(8,128)(2,1)S(1)}, u32[]{:S(2)}, u32[]{:S(2)}) async-start(bf16[32,80,128]{2,1,0:T(8,128)(2,1)} %get-tuple-element.22), calls=%async_computation | async-start | bytes 1310720 | tf_op jit(solution)/shard_map/all_to_all | solution.py:284
  13.0 18.2 %copy-start.9 = (s32[2,96]{1,0:T(2,128)S(1)}, s32[2,96]{1,0:T(2,128)}, u32[]{:S(2)}) copy-start(s32[2,96]{1,0:T(2,128)} %refs_6_.1) | copy-start | bytes 2308
  13.0 18.2 %copy-start.11 = (bf16[128,128]{1,0:T(8,128)(2,1)S(1)}, bf16[128,128]{1,0:T(8,128)(2,1)}, u32[]{:S(2)}) copy-start(bf16[128,128]{1,0:T(8,128)(2,1)} %get-tuple-element.23.refs_5_.base_ref) | copy-start | bytes 98308
  26.0 0.8 %copy-start.5 = (bf16[256,128]{1,0:T(8,128)(2,1)S(1)}, bf16[256,128]{1,0:T(8,128)(2,1)}, u32[]{:S(2)}) copy-start(bf16[256,128]{1,0:T(8,128)(2,1)} %get-tuple-element.24.rim_ref) | copy-start | bytes 196612
  27.5 9.1 %all-to-all-start.1 = ((bf16[4,144,128]{2,1,0:T(8,128)(2,1)}), bf16[4,144,128]{2,1,0:T(8,128)(2,1)S(1)}, u32[]{:S(2)}, u32[]{:S(2)}) async-start(bf16[4,144,128]{2,1,0:T(8,128)(2,1)} %shard_map.138), calls=%async_computation.1 | async-start | bytes 294912 | tf_op jit(solution)/shard_map/all_to_all | solution.py:284
  31.2 5.5 %copy-start.3 = (f32[448,128]{1,0:T(8,128)S(1)}, f32[448,128]{1,0:T(8,128)}, u32[]{:S(2)}) copy-start(f32[448,128]{1,0:T(8,128)} %get-tuple-element.26.core_ref) | copy-start | bytes 688132
  31.2 5.5 %copy-start.8 = (s32[2,128]{1,0:T(2,128)S(1)}, s32[2,128]{1,0:T(2,128)}, u32[]{:S(2)}) copy-start(s32[2,128]{1,0:T(2,128)} %refs_7_.1) | copy-start | bytes 3076
  31.2 25.7 %copy-start = (bf16[64,128,128]{2,1,0:T(8,128)(2,1)S(1)}, bf16[64,128,128]{2,1,0:T(8,128)(2,1)}, u32[]{:S(2)}) copy-start(bf16[64,128,128]{2,1,0:T(8,128)(2,1)} %get-tuple-element.32.radial_ref) | copy-start | bytes 6291460
  31.2 25.7 %copy-start.6 = (s32[128,64]{0,1:T(8,128)S(1)}, s32[128,64]{0,1:T(8,128)}, u32[]{:S(2)}) copy-start(s32[128,64]{0,1:T(8,128)} %param.17) | copy-start | bytes 98308
  31.6 27.0 %copy-start.4 = (f32[1024,32]{0,1:T(8,128)S(1)}, f32[1024,32]{0,1:T(8,128)}, u32[]{:S(2)}) copy-start(f32[1024,32]{0,1:T(8,128)} %param.26) | copy-start | bytes 393220
  36.9 12.5 %collective-permute-start = (bf16[208,128]{1,0:T(8,128)(2,1)S(1)}, bf16[208,128]{1,0:T(8,128)(2,1)S(1)}, u32[]{:S(2)}, u32[]{:S(2)}) collective-permute-start(bf16[208,128]{1,0:T(8,128)(2,1)S(1)} %get-tuple-element.27), channel_id=1, source_target_pairs={{0,4},{4,8},{8,12},{12,0},{1,5},{5,9},{9,13},{13,1},{2,6},{6,10},{... | collective-permute-start | bytes 159752 | tf_op jit(solution)/shard_map/ppermute | solution.py:280
  45.7 12.8 %collective-permute-start.1 = (bf16[208,128]{1,0:T(8,128)(2,1)S(1)}, bf16[208,128]{1,0:T(8,128)(2,1)S(1)}, u32[]{:S(2)}, u32[]{:S(2)}) collective-permute-start(bf16[208,128]{1,0:T(8,128)(2,1)S(1)} %get-tuple-element.28), channel_id=1, source_target_pairs={{4,0},{8,4},{12,8},{0,12},{5,1},{9,5},{13,9},{1,13},{6,2},{10,6},{... | collective-permute-start | bytes 159752 | tf_op jit(solution)/shard_map/ppermute | solution.py:280
  49.4 9.1 %collective-permute-start.2 = (bf16[16,128]{1,0:T(8,128)(2,1)S(1)}, bf16[16,128]{1,0:T(8,128)(2,1)S(1)}, u32[]{:S(2)}, u32[]{:S(2)}) collective-permute-start(bf16[16,128]{1,0:T(8,128)(2,1)S(1)} %shard_map.141), channel_id=1, source_target_pairs={{0,4},{4,8},{8,12},{12,0},{1,5},{5,9},{9,13},{13,1},{2,6},{6,10},{... | collective-permute-start | bytes 12296 | tf_op jit(solution)/shard_map/ppermute | solution.py:354
  59.9 19.4 %all-to-all-start.2 = ((bf16[32,80,128]{2,1,0:T(8,128)(2,1)}), bf16[32,80,128]{2,1,0:T(8,128)(2,1)S(1)}, u32[]{:S(2)}, u32[]{:S(2)}) async-start(bf16[32,80,128]{2,1,0:T(8,128)(2,1)} %get-tuple-element.33), calls=%async_computation.2 | async-start | bytes 1310720 | tf_op jit(solution)/shard_map/all_to_all | solution.py:284
  66.3 8.7 %collective-permute-start.3 = (bf16[128,128]{1,0:T(8,128)(2,1)S(1)}, bf16[128,128]{1,0:T(8,128)(2,1)S(1)}, u32[]{:S(2)}, u32[]{:S(2)}) collective-permute-start(bf16[128,128]{1,0:T(8,128)(2,1)S(1)} %get-tuple-element.35), channel_id=1, source_target_pairs={{0,1},{1,2},{2,3},{3,0},{4,5},{5,6},{6,7},{7,4},{8,9},{9,10},{10,1... | collective-permute-start | bytes 98312 | tf_op jit(solution)/shard_map/ppermute | solution.py:280
  70.3 5.0 %collective-permute-start.4 = (bf16[128,128]{1,0:T(8,128)(2,1)S(1)}, bf16[128,128]{1,0:T(8,128)(2,1)S(1)}, u32[]{:S(2)}, u32[]{:S(2)}) collective-permute-start(bf16[128,128]{1,0:T(8,128)(2,1)S(1)} %get-tuple-element.36), channel_id=1, source_target_pairs={{1,0},{2,1},{3,2},{0,3},{5,4},{6,5},{7,6},{4,7},{9,8},{10,9},{11,1... | collective-permute-start | bytes 98312 | tf_op jit(solution)/shard_map/ppermute | solution.py:280
  74.9 4.4 %copy-start.1 = (bf16[1024,128]{1,0:T(8,128)(2,1)S(1)}, bf16[1024,128]{1,0:T(8,128)(2,1)}, u32[]{:S(2)}) copy-start(bf16[1024,128]{1,0:T(8,128)(2,1)} %get-tuple-element.37.cos_ref) | copy-start | bytes 786436
  74.9 4.4 %copy-start.2 = (bf16[1024,128]{1,0:T(8,128)(2,1)S(1)}, bf16[1024,128]{1,0:T(8,128)(2,1)}, u32[]{:S(2)}) copy-start(bf16[1024,128]{1,0:T(8,128)(2,1)} %get-tuple-element.38.sin_ref) | copy-start | bytes 786436
  75.0 4.4 %copy-start.7 = (bf16[32,128]{1,0:T(8,128)(2,1)S(1)}, bf16[32,128]{1,0:T(8,128)(2,1)}, u32[]{:S(2)}) copy-start(bf16[32,128]{1,0:T(8,128)(2,1)} %ewald_ref.1) | copy-start | bytes 24580
  75.0 4.4 %copy-start.10 = (s32[2,64]{1,0:T(2,128)S(1)}, s32[2,64]{1,0:T(2,128)}, u32[]{:S(2)}) copy-start(s32[2,64]{1,0:T(2,128)} %send_ref.3) | copy-start | bytes 1540

commit v6 on v5

--- a/solution.py
+++ b/solution.py
@@ -164,6 +164,10 @@
     cos_ref[...], sin_ref[...] = wave_tables(coords_ref[...], cos_ref.shape[0])
 
 
+def stage_body(source_ref, staged_ref):
+    staged_ref[...] = source_ref[...]
+
+
 def second_body(first_ref, rim_ref, blocks_ref):
     half = rim_ref.shape[0] // 2
     height = blocks_ref.shape[1] - half
@@ -205,15 +209,18 @@
     relay_ref[...] = above_ref[: relay_ref.shape[0]]
 
 
+def rim_body(fresh, below_ref, above_ref, table_ref, send_ref, order_ref, low_ref, high_ref):
+    table = jnp.concatenate([table_ref[...], below_ref[fresh], above_ref[fresh]], axis=0)
+    low_ref[...] = picked(send_ref[...], 0, table)
+    high_ref[...] = picked(send_ref[...], 1, table)
+
+
 def fourth_body(
-    below_ref, above_ref, share_ref, relay_ref, table_ref, core_ref, send_y_ref, send_z_ref, kernel_ref,
-    gathered_ref, keep_ref, low_ref, high_ref, blocks_ref, norm_factor,
+    below_ref, above_ref, share_ref, relay_ref, core_ref, send_y_ref, kernel_ref,
+    gathered_ref, keep_ref, blocks_ref, norm_factor,
 ):
     height, half = share_ref.shape[0], send_y_ref.shape[1]
-    fresh, back = slice(height, height + half), slice(height + half, height + 2 * half)
-    table = jnp.concatenate([table_ref[...], below_ref[fresh], above_ref[fresh]], axis=0)
-    low_ref[...] = picked(send_z_ref[...], 0, table)
-    high_ref[...] = picked(send_z_ref[...], 1, table)
+    back = slice(height + half, height + 2 * half)
     spread = core_ref[...] + placed(send_y_ref[...], below_ref[back], above_ref[back], core_ref.shape[0])
     keep = keep_ref.shape[0]
     keep_ref[...] = spread[:keep]
@@ -329,6 +336,7 @@
         ),
         (*far, base), 6 * 10**9, 60, (pltpu.VMEM((slots * basis_rows, atoms), full), *landing(far)), far=len(far),
     )
+    (rim,) = kernel_call(stage_body, (like(rim.shape, half),), (rim,), 10**6, 8)
     (blocks,) = kernel_call(
         second_body, (like((count_z, height + rim_z, feat), half),), (first, rim), 10**8, 8
     )
@@ -353,13 +361,16 @@
     )
     relay = lax.ppermute(relay, "gy", [(i, (i + 1) % count_y) for i in range(count_y)])
     norm_factor = 1.0 / math.sqrt(atoms * count_x * count_y * count_z)
-    core, low, high, blocks = kernel_call(
+    core, blocks = kernel_call(
         lambda *refs: fourth_body(*refs, norm_factor),
         (
-            like((atoms, feat), full), like((rim_z, feat), half), like((rim_z, feat), half),
-            like((count_x, tall, feat), half),
+            like((atoms, feat), full), like((count_x, tall, feat), half),
         ),
-        (below_y, above_y, share, relay, table, core, send_y, send_z, k_kernel.T, gathered), 10**8, 8,
+        (below_y, above_y, share, relay, core, send_y, k_kernel.T, gathered), 10**8, 8,
+    )
+    low, high = kernel_call(
+        functools.partial(rim_body, slice(height, height + rim_y)), (like((rim_z, feat), half),) * 2,
+        (below_y, above_y, table, send_z, core), 10**8, 8
     )
     below_z, above_z = swap(low, high, "gz")
     first = exchange(blocks, "gx")

time: 81.2 us -> 80 us (0.985)
  waiting for transfers between devices: 13.9 us -> 12.6 us
    all_to_all x3, waiting for transfers between devices: 13.6 us -> 12.3 us  [exchange(): return lax.all_to_all(blocks, axes, split_axis=0, concat_axis=0)]
    pallas_call x11 -> x13, Pallas kernels: 17.8 us -> 17.9 us  [kernel_call(): pl.pallas_call(body, out_shape=tuple(outs), in_specs=specs, out_specs=(pl...]
  transfers between devices with their start and end apart: 8 -> 8, of which waited for: 4 -> 4; matrix products, arithmetic and copies ran while one was open for 0% -> 0% of each run, Pallas kernels for 15% -> 16%
where the time goes in v6:
time: 80 us; the launch traced here: 79.2 us
  starting transfers between devices  47.5 us (59%)
  Pallas kernels  17.9 us (22%)
  waiting for transfers between devices  12.6 us (16%)
  local copies, waits for them, and re-layouts  0.89 us (1%)
    all_to_all x3, starting transfers between devices, exchange(): return lax.all_to_all(blocks, axes, split_axis=0, concat_axis=0)  20.5 us
    pallas_call x13, Pallas kernels, kernel_call(): pl.pallas_call(body, out_shape=tuple(outs), in_specs=specs, out_specs=(pl...  17.9 us
    ppermute x2, starting transfers between devices, swap(): lax.ppermute(high, axis, forward)  12.9 us
    all_to_all x3, waiting for transfers between devices, exchange(): return lax.all_to_all(blocks, axes, split_axis=0, concat_axis=0)  12.3 us
    ppermute x1, starting transfers between devices, on_device(): lax.ppermute(relay, 'gy', [(i, (i + 1) % count_y) for i in range(count_y)])  7.47 us
    ppermute x2, starting transfers between devices, swap(): lax.ppermute(low, axis, backward)  6.7 us
  transfers between devices with their start and end apart: 8, of which 4 were waited for; matrix products, arithmetic and copies ran while one was open for 0% of the time, Pallas kernels for 16%

profile of v6, /device:TPU:1, one launch (start us, length us, event | category | flops | bytes accessed | tf_op | source)
XLA Modules:
  0.0 79.2 jit_solution(17677284524581006895)
XLA Ops:
  0.0 2.5 %shard_map.136 = (bf16[128,128]{1,0:T(8,128)(2,1)}, bf16[32,80,128]{2,1,0:T(8,128)(2,1)}) custom-call(bf16[128,128]{1,0:T(8,128)(2,1)} %refs_0_.1, bf16[128,128]{1,0:T(8,128)(2,1)} %refs_1_.1, bf16[128,128]{1,0:T(8,128)(2,1)} %refs_2_.1, s32[2,64]{1,0:T(2,128)} %send_ref.5, f32[3,128]{1,0:T(4,128)} %refs_4_.3, bf16[32,128]{1,0:T(8,128)(2,1)} %bitcast.11), custom_call_target="tpu_custom_call" | custom-call | flops 100000000 | bytes 796672 | tf_op jit(solution)/shard_map/pallas_call | solution.py:23
  2.5 10.4 %all-to-all-start = ((bf16[32,80,128]{2,1,0:T(8,128)(2,1)}), bf16[32,80,128]{2,1,0:T(8,128)(2,1)S(1)}, u32[]{:S(2)}, u32[]{:S(2)}) async-start(bf16[32,80,128]{2,1,0:T(8,128)(2,1)} %get-tuple-element.22), calls=%async_computation | async-start | bytes 1310720 | tf_op jit(solution)/shard_map/all_to_all | solution.py:291
  12.9 0.0 copy-start.8
  13.0 0.0 copy-start.11
  13.0 7.0 %shard_map.137 = (f32[448,128]{1,0:T(8,128)}, bf16[256,128]{1,0:T(8,128)(2,1)}, bf16[1024,128]{1,0:T(8,128)(2,1)}, bf16[1024,128]{1,0:T(8,128)(2,1)}, bf16[64,128,128]{2,1,0:T(8,128)(2,1)}) custom-call(f32[64,128]{1,0:T(8,128)} %bitcast.10, s32[64,128]{1,0:T(8,128)} %bitcast.6, s32[1,128]{1,0:T(1,128)} %bitcast.12, bf16[20,128]{1,0:T(8,128)(2,1)} %refs_3_.3, ...), custom_call_target="tpu_custom_call" | custom-call | flops 6000000000 | bytes 3021824 | tf_op jit(solution)/shard_map/pallas_call | solution.py:23
  19.9 0.0 copy-start.5
  19.9 0.8 %copy-done.5 = bf16[256,128]{1,0:T(8,128)(2,1)S(1)} copy-done((bf16[256,128]{1,0:T(8,128)(2,1)S(1)}, bf16[256,128]{1,0:T(8,128)(2,1)}, u32[]{:S(2)}) %copy-start.5) | copy-done | bytes 65560
  20.8 5.2 %all-to-all-done.first_ref = bf16[32,80,128]{2,1,0:T(8,128)(2,1)S(1)} async-done(((bf16[32,80,128]{2,1,0:T(8,128)(2,1)}), bf16[32,80,128]{2,1,0:T(8,128)(2,1)S(1)}, u32[]{:S(2)}, u32[]{:S(2)}) %all-to-all-start) | async-done | bytes 655392 | tf_op jit(solution)/shard_map/all_to_all | solution.py:291
  26.0 0.7 shard_map.139
  26.7 3.7 %all-to-all-start.1 = ((bf16[4,144,128]{2,1,0:T(8,128)(2,1)}), bf16[4,144,128]{2,1,0:T(8,128)(2,1)S(1)}, u32[]{:S(2)}, u32[]{:S(2)}) async-start(bf16[4,144,128]{2,1,0:T(8,128)(2,1)} %shard_map.139), calls=%async_computation.1 | async-start | bytes 294912 | tf_op jit(solution)/shard_map/all_to_all | solution.py:291
  30.3 0.0 copy-done.8
  30.3 0.0 copy-done.11
  30.4 0.0 copy-start.9
  30.4 0.0 copy-start
  30.4 0.0 copy-start.6
  30.4 0.3 shard_map.140
  30.7 0.0 copy-start.4
  30.7 5.1 %all-to-all-done.1.third_ref = bf16[4,144,128]{2,1,0:T(8,128)(2,1)S(1)} async-done(((bf16[4,144,128]{2,1,0:T(8,128)(2,1)}), bf16[4,144,128]{2,1,0:T(8,128)(2,1)S(1)}, u32[]{:S(2)}, u32[]{:S(2)}) %all-to-all-start.1) | async-done | bytes 147488 | tf_op jit(solution)/shard_map/all_to_all | solution.py:291
  35.8 0.0 copy-done.3
  35.8 0.0 copy-done.9
  35.8 0.2 shard_map.141
  36.1 8.8 %collective-permute-start = (bf16[208,128]{1,0:T(8,128)(2,1)S(1)}, bf16[208,128]{1,0:T(8,128)(2,1)S(1)}, u32[]{:S(2)}, u32[]{:S(2)}) collective-permute-start(bf16[208,128]{1,0:T(8,128)(2,1)S(1)} %get-tuple-element.27), channel_id=1, source_target_pairs={{0,4},{4,8},{8,12},{12,0},{1,5},{5,9},{9,13},{13,1},{2,6},{6,10},{... | collective-permute-start | bytes 159752 | tf_op jit(solution)/shard_map/ppermute | solution.py:287
  44.9 3.7 %collective-permute-start.1 = (bf16[208,128]{1,0:T(8,128)(2,1)S(1)}, bf16[208,128]{1,0:T(8,128)(2,1)S(1)}, u32[]{:S(2)}, u32[]{:S(2)}) collective-permute-start(bf16[208,128]{1,0:T(8,128)(2,1)S(1)} %get-tuple-element.28), channel_id=1, source_target_pairs={{4,0},{8,4},{12,8},{0,12},{5,1},{9,5},{13,9},{1,13},{6,2},{10,6},{... | collective-permute-start | bytes 159752 | tf_op jit(solution)/shard_map/ppermute | solution.py:287
  48.6 0.0 collective-permute-done.above_ref.refs_0_.below_ref
  48.6 7.5 %collective-permute-start.2 = (bf16[16,128]{1,0:T(8,128)(2,1)S(1)}, bf16[16,128]{1,0:T(8,128)(2,1)S(1)}, u32[]{:S(2)}, u32[]{:S(2)}) collective-permute-start(bf16[16,128]{1,0:T(8,128)(2,1)S(1)} %shard_map.142), channel_id=1, source_target_pairs={{0,4},{4,8},{8,12},{12,0},{1,5},{5,9},{9,13},{13,1},{2,6},{6,10},{... | collective-permute-start | bytes 12296 | tf_op jit(solution)/shard_map/ppermute | solution.py:362
  56.1 0.0 copy-done
  56.1 0.0 copy-done.6
  56.1 1.6 %shard_map.143.refs_7_.sofar_ref = f32[128,128]{1,0:T(8,128)S(1)} custom-call(s32[64,128]{1,0:T(8,128)S(1)} %bitcast.7, bf16[64,128,128]{2,1,0:T(8,128)(2,1)S(1)} %copy-done, bf16[256,128]{1,0:T(8,128)(2,1)S(1)} %get-tuple-element.32.table_ref), custom_call_target="tpu_custom_call" | custom-call | flops 1000 | bytes 1000 | tf_op jit(solution)/shard_map/pallas_call | solution.py:23
  57.7 0.0 collective-permute-done.1.refs_1_.above_ref
  57.7 0.0 collective-permute-done.2.refs_3_
  57.7 0.0 copy-done.4
  57.7 1.0 %shard_map.144 = (f32[128,128]{1,0:T(8,128)S(1)}, bf16[32,80,128]{2,1,0:T(8,128)(2,1)}) custom-call(bf16[208,128]{1,0:T(8,128)(2,1)S(1)} %collective-permute-done.above_ref.refs_0_.below_ref, bf16[208,128]{1,0:T(8,128)(2,1)S(1)} %collective-permute-done.1.refs_1_.above_ref, bf16[16,128]{1,0:T(8,128)(2,1)S(1)} %get-tuple-element.29.refs_2_, ...), custom_call_target="tpu_custom_call" | custom-call | flops 100000000 | bytes 1164032 | tf_op jit(solution)/shard_map/pallas_call | solution.py:23
  58.7 6.4 %all-to-all-start.2 = ((bf16[32,80,128]{2,1,0:T(8,128)(2,1)}), bf16[32,80,128]{2,1,0:T(8,128)(2,1)S(1)}, u32[]{:S(2)}, u32[]{:S(2)}) async-start(bf16[32,80,128]{2,1,0:T(8,128)(2,1)} %get-tuple-element.33), calls=%async_computation.2 | async-start | bytes 1310720 | tf_op jit(solution)/shard_map/all_to_all | solution.py:291
  65.1 0.4 shard_map.145
  65.5 4.1 %collective-permute-start.3 = (bf16[128,128]{1,0:T(8,128)(2,1)S(1)}, bf16[128,128]{1,0:T(8,128)(2,1)S(1)}, u32[]{:S(2)}, u32[]{:S(2)}) collective-permute-start(bf16[128,128]{1,0:T(8,128)(2,1)S(1)} %get-tuple-element.35), channel_id=1, source_target_pairs={{0,1},{1,2},{2,3},{3,0},{4,5},{5,6},{6,7},{7,4},{8,9},{9,10},{10,1... | collective-permute-start | bytes 98312 | tf_op jit(solution)/shard_map/ppermute | solution.py:287
  69.6 3.0 %collective-permute-start.4 = (bf16[128,128]{1,0:T(8,128)(2,1)S(1)}, bf16[128,128]{1,0:T(8,128)(2,1)S(1)}, u32[]{:S(2)}, u32[]{:S(2)}) collective-permute-start(bf16[128,128]{1,0:T(8,128)(2,1)S(1)} %get-tuple-element.36), channel_id=1, source_target_pairs={{1,0},{2,1},{3,2},{0,3},{5,4},{6,5},{7,6},{4,7},{9,8},{10,9},{11,1... | collective-permute-start | bytes 98312 | tf_op jit(solution)/shard_map/ppermute | solution.py:287
  72.6 1.6 %shard_map.146.sofar_ref = f32[128,128]{1,0:T(8,128)S(1)} custom-call(s32[64,128]{1,0:T(8,128)S(1)} %bitcast.8, bf16[64,128,128]{2,1,0:T(8,128)(2,1)S(1)} %copy-done, bf16[208,128]{1,0:T(8,128)(2,1)S(1)} %collective-permute-done.above_ref.refs_0_.below_ref, bf16[208,128]{1,0:T(8,128)(2,1)S(1)} %collective-permute-done.1.refs_1_.above_ref, ...), custom_call_target="tpu_custom_call" | custom-call | flops 2000000000 | bytes 2367488 | tf_op jit(solution)/shard_map/pallas_call | solution.py:23
  74.2 0.0 copy-start.1
  74.2 0.0 copy-start.2
  74.2 0.0 copy-start.7
  74.2 0.0 copy-start.10
  74.3 0.0 collective-permute-done.3.below_ref
  74.3 0.3 collective-permute-done.4.above_ref
  74.6 1.6 %shard_map.147.gathered_ref = f32[128,128]{1,0:T(8,128)S(1)} custom-call(s32[64,128]{1,0:T(8,128)S(1)} %bitcast.9, bf16[64,128,128]{2,1,0:T(8,128)(2,1)S(1)} %copy-done, bf16[128,128]{1,0:T(8,128)(2,1)S(1)} %collective-permute-done.3.below_ref, bf16[128,128]{1,0:T(8,128)(2,1)S(1)} %collective-permute-done.4.above_ref, f32[128,128]{1,0:T(8,128)S(1)} %shard_map.146.sofar_ref), custom_call_target="tpu_custom_call" | custom-call | flops 2000000000 | bytes 2326528 | tf_op jit(solution)/shard_map/pallas_call | solution.py:23
  76.1 2.0 %all-to-all-done.2.first_ref = bf16[32,80,128]{2,1,0:T(8,128)(2,1)S(1)} async-done(((bf16[32,80,128]{2,1,0:T(8,128)(2,1)}), bf16[32,80,128]{2,1,0:T(8,128)(2,1)S(1)}, u32[]{:S(2)}, u32[]{:S(2)}) %all-to-all-start.2) | async-done | bytes 655392 | tf_op jit(solution)/shard_map/all_to_all | solution.py:291
  78.2 0.0 copy-done.1
  78.2 0.0 copy-done.7
  78.2 1.1 %shard_map.148 = bf16[128,128]{1,0:T(8,128)(2,1)} custom-call(bf16[32,80,128]{2,1,0:T(8,128)(2,1)S(1)} %all-to-all-done.2.first_ref, f32[128,128]{1,0:T(8,128)S(1)} %get-tuple-element.34.order_ref.core_ref, s32[2,64]{1,0:T(2,128)S(1)} %copy-done.10, f32[128,128]{1,0:T(8,128)S(1)} %shard_map.147.gathered_ref, bf16[1024,128]{1,0:T(8,128)(2,1)S(1)} %copy-done.1, ...), custom_call_target="tpu_custom_call" | custom-call | flops 100000000 | bytes 1352192 | tf_op jit(solution)/shard_map/pallas_call | solution.py:23
  (5 shorter events, 0.0 us)
Async XLA Ops:
  2.5 23.5 %all-to-all-start = ((bf16[32,80,128]{2,1,0:T(8,128)(2,1)}), bf16[32,80,128]{2,1,0:T(8,128)(2,1)S(1)}, u32[]{:S(2)}, u32[]{:S(2)}) async-start(bf16[32,80,128]{2,1,0:T(8,128)(2,1)} %get-tuple-element.22), calls=%async_computation | async-start | bytes 1310720 | tf_op jit(solution)/shard_map/all_to_all | solution.py:291
  12.9 17.4 %copy-start.8 = (s32[2,96]{1,0:T(2,128)S(1)}, s32[2,96]{1,0:T(2,128)}, u32[]{:S(2)}) copy-start(s32[2,96]{1,0:T(2,128)} %refs_5_.1) | copy-start | bytes 2308
  13.0 17.4 %copy-start.11 = (bf16[128,128]{1,0:T(8,128)(2,1)S(1)}, bf16[128,128]{1,0:T(8,128)(2,1)}, u32[]{:S(2)}) copy-start(bf16[128,128]{1,0:T(8,128)(2,1)} %get-tuple-element.23.refs_5_.base_ref) | copy-start | bytes 98308
  19.9 0.8 %copy-start.5 = (bf16[256,128]{1,0:T(8,128)(2,1)S(1)}, bf16[256,128]{1,0:T(8,128)(2,1)}, u32[]{:S(2)}) copy-start(bf16[256,128]{1,0:T(8,128)(2,1)} %get-tuple-element.24.source_ref) | copy-start | bytes 196612
  26.7 9.1 %all-to-all-start.1 = ((bf16[4,144,128]{2,1,0:T(8,128)(2,1)}), bf16[4,144,128]{2,1,0:T(8,128)(2,1)S(1)}, u32[]{:S(2)}, u32[]{:S(2)}) async-start(bf16[4,144,128]{2,1,0:T(8,128)(2,1)} %shard_map.139), calls=%async_computation.1 | async-start | bytes 294912 | tf_op jit(solution)/shard_map/all_to_all | solution.py:291
  30.3 5.5 %copy-start.3 = (f32[448,128]{1,0:T(8,128)S(1)}, f32[448,128]{1,0:T(8,128)}, u32[]{:S(2)}) copy-start(f32[448,128]{1,0:T(8,128)} %get-tuple-element.26.core_ref) | copy-start | bytes 688132
  30.4 5.5 %copy-start.9 = (s32[2,128]{1,0:T(2,128)S(1)}, s32[2,128]{1,0:T(2,128)}, u32[]{:S(2)}) copy-start(s32[2,128]{1,0:T(2,128)} %send_ref.4) | copy-start | bytes 3076
  30.4 25.7 %copy-start = (bf16[64,128,128]{2,1,0:T(8,128)(2,1)S(1)}, bf16[64,128,128]{2,1,0:T(8,128)(2,1)}, u32[]{:S(2)}) copy-start(bf16[64,128,128]{2,1,0:T(8,128)(2,1)} %get-tuple-element.31.radial_ref) | copy-start | bytes 6291460
  30.4 25.7 %copy-start.6 = (s32[128,64]{0,1:T(8,128)S(1)}, s32[128,64]{0,1:T(8,128)}, u32[]{:S(2)}) copy-start(s32[128,64]{0,1:T(8,128)} %param.17) | copy-start | bytes 98308
  30.7 27.0 %copy-start.4 = (f32[1024,32]{0,1:T(8,128)S(1)}, f32[1024,32]{0,1:T(8,128)}, u32[]{:S(2)}) copy-start(f32[1024,32]{0,1:T(8,128)} %param.26) | copy-start | bytes 393220
  36.1 12.5 %collective-permute-start = (bf16[208,128]{1,0:T(8,128)(2,1)S(1)}, bf16[208,128]{1,0:T(8,128)(2,1)S(1)}, u32[]{:S(2)}, u32[]{:S(2)}) collective-permute-start(bf16[208,128]{1,0:T(8,128)(2,1)S(1)} %get-tuple-element.27), channel_id=1, source_target_pairs={{0,4},{4,8},{8,12},{12,0},{1,5},{5,9},{9,13},{13,1},{2,6},{6,10},{... | collective-permute-start | bytes 159752 | tf_op jit(solution)/shard_map/ppermute | solution.py:287
  44.9 12.8 %collective-permute-start.1 = (bf16[208,128]{1,0:T(8,128)(2,1)S(1)}, bf16[208,128]{1,0:T(8,128)(2,1)S(1)}, u32[]{:S(2)}, u32[]{:S(2)}) collective-permute-start(bf16[208,128]{1,0:T(8,128)(2,1)S(1)} %get-tuple-element.28), channel_id=1, source_target_pairs={{4,0},{8,4},{12,8},{0,12},{5,1},{9,5},{13,9},{1,13},{6,2},{10,6},{... | collective-permute-start | bytes 159752 | tf_op jit(solution)/shard_map/ppermute | solution.py:287
  48.6 9.1 %collective-permute-start.2 = (bf16[16,128]{1,0:T(8,128)(2,1)S(1)}, bf16[16,128]{1,0:T(8,128)(2,1)S(1)}, u32[]{:S(2)}, u32[]{:S(2)}) collective-permute-start(bf16[16,128]{1,0:T(8,128)(2,1)S(1)} %shard_map.142), channel_id=1, source_target_pairs={{0,4},{4,8},{8,12},{12,0},{1,5},{5,9},{9,13},{13,1},{2,6},{6,10},{... | collective-permute-start | bytes 12296 | tf_op jit(solution)/shard_map/ppermute | solution.py:362
  58.7 19.4 %all-to-all-start.2 = ((bf16[32,80,128]{2,1,0:T(8,128)(2,1)}), bf16[32,80,128]{2,1,0:T(8,128)(2,1)S(1)}, u32[]{:S(2)}, u32[]{:S(2)}) async-start(bf16[32,80,128]{2,1,0:T(8,128)(2,1)} %get-tuple-element.33), calls=%async_computation.2 | async-start | bytes 1310720 | tf_op jit(solution)/shard_map/all_to_all | solution.py:291
  65.5 8.7 %collective-permute-start.3 = (bf16[128,128]{1,0:T(8,128)(2,1)S(1)}, bf16[128,128]{1,0:T(8,128)(2,1)S(1)}, u32[]{:S(2)}, u32[]{:S(2)}) collective-permute-start(bf16[128,128]{1,0:T(8,128)(2,1)S(1)} %get-tuple-element.35), channel_id=1, source_target_pairs={{0,1},{1,2},{2,3},{3,0},{4,5},{5,6},{6,7},{7,4},{8,9},{9,10},{10,1... | collective-permute-start | bytes 98312 | tf_op jit(solution)/shard_map/ppermute | solution.py:287
  69.6 5.0 %collective-permute-start.4 = (bf16[128,128]{1,0:T(8,128)(2,1)S(1)}, bf16[128,128]{1,0:T(8,128)(2,1)S(1)}, u32[]{:S(2)}, u32[]{:S(2)}) collective-permute-start(bf16[128,128]{1,0:T(8,128)(2,1)S(1)} %get-tuple-element.36), channel_id=1, source_target_pairs={{1,0},{2,1},{3,2},{0,3},{5,4},{6,5},{7,6},{4,7},{9,8},{10,9},{11,1... | collective-permute-start | bytes 98312 | tf_op jit(solution)/shard_map/ppermute | solution.py:287
  74.2 4.0 %copy-start.1 = (bf16[1024,128]{1,0:T(8,128)(2,1)S(1)}, bf16[1024,128]{1,0:T(8,128)(2,1)}, u32[]{:S(2)}) copy-start(bf16[1024,128]{1,0:T(8,128)(2,1)} %get-tuple-element.37.cos_ref) | copy-start | bytes 786436
  74.2 3.9 %copy-start.2 = (bf16[1024,128]{1,0:T(8,128)(2,1)S(1)}, bf16[1024,128]{1,0:T(8,128)(2,1)}, u32[]{:S(2)}) copy-start(bf16[1024,128]{1,0:T(8,128)(2,1)} %get-tuple-element.38.sin_ref) | copy-start | bytes 786436
  74.2 3.9 %copy-start.7 = (bf16[32,128]{1,0:T(8,128)(2,1)S(1)}, bf16[32,128]{1,0:T(8,128)(2,1)}, u32[]{:S(2)}) copy-start(bf16[32,128]{1,0:T(8,128)(2,1)} %ewald_ref.1) | copy-start | bytes 24580
  74.2 3.9 %copy-start.10 = (s32[2,64]{1,0:T(2,128)S(1)}, s32[2,64]{1,0:T(2,128)}, u32[]{:S(2)}) copy-start(s32[2,64]{1,0:T(2,128)} %send_ref.5) | copy-start | bytes 1540

commit v7 on v6

--- a/solution.py
+++ b/solution.py
@@ -187,7 +187,7 @@
         packets_ref[side] = picked(send_ref[...], side, table)
 
 
-def third_body(third_ref, packets_ref, core_ref, send_z_ref, keep_ref, low_ref, high_ref, share_ref):
+def third_body(third_ref, packets_ref, core_ref, send_z_ref, gathered_ref, keep_ref, low_ref, high_ref, share_ref):
     half = packets_ref.shape[1]
     height = low_ref.shape[0] - 2 * half
     share = jnp.sum(third_ref[:, :height].astype(jnp.float32), axis=0).astype(share_ref.dtype)
@@ -217,7 +217,7 @@
 
 def fourth_body(
     below_ref, above_ref, share_ref, relay_ref, core_ref, send_y_ref, kernel_ref,
-    gathered_ref, keep_ref, blocks_ref, norm_factor,
+    keep_ref, blocks_ref, norm_factor,
 ):
     height, half = share_ref.shape[0], send_y_ref.shape[1]
     back = slice(height + half, height + 2 * half)
@@ -344,18 +344,18 @@
     table, packets = kernel_call(
         pick_body, (like((with_x, feat), half), like((2, rim_y, feat), half)), (first, base, send_y), 2 * 10**9, 8
     )
+    (gathered,) = kernel_call(
+        gather_first_body, (like((atoms, feat), full),), (nbr_index.T, radial, table), 10**3, 24, moved=10**3
+    )
     core, low, high, share = kernel_call(
         third_body,
         (
             like((with_x, feat), full), like((height + 2 * rim_y, feat), half),
             like((height + 2 * rim_y, feat), half), like((height, feat), half),
         ),
-        (third, packets, core, send_z), 10**8, 8,
+        (third, packets, core, send_z, gathered), 10**8, 8,
     )
     below_y, above_y = swap(low, high, "gy")
-    (gathered,) = kernel_call(
-        gather_first_body, (like((atoms, feat), full),), (nbr_index.T, radial, table), 10**3, 24, moved=10**3
-    )
     (relay,) = kernel_call(
         relay_body, (like((height, feat), half),), (below_y,), 10**6, 8
     )
@@ -366,7 +366,7 @@
         (
             like((atoms, feat), full), like((count_x, tall, feat), half),
         ),
-        (below_y, above_y, share, relay, core, send_y, k_kernel.T, gathered), 10**8, 8,
+        (below_y, above_y, share, relay, core, send_y, k_kernel.T), 10**8, 8,
     )
     low, high = kernel_call(
         functools.partial(rim_body, slice(height, height + rim_y)), (like((rim_z, feat), half),) * 2,

time: 80 us -> 80 us (level)
  waiting for transfers between devices: 12.6 us -> 10.6 us
  local copies, waits for them, and re-layouts: 0.89 us -> 2.09 us
  starting transfers between devices: 47.5 us -> 48.4 us
    all_to_all x3, waiting for transfers between devices: 12.3 us -> 9.51 us  [exchange(): return lax.all_to_all(blocks, axes, split_axis=0, concat_axis=0)]
    unnamed x24, local copies, waits for them, and re-layouts: 0.89 us -> 2.09 us
    all_to_all x3, starting transfers between devices: 20.5 us -> 21.3 us  [exchange(): return lax.all_to_all(blocks, axes, split_axis=0, concat_axis=0)]
  transfers between devices with their start and end apart: 8 -> 8, of which waited for: 4 -> 5; matrix products, arithmetic and copies ran while one was open for 0% -> 0% of each run, Pallas kernels for 16% -> 16%
where the time goes in v7:
time: 80 us; the launch traced here: 79.2 us
  starting transfers between devices  48.4 us (60%)
  Pallas kernels  17.9 us (22%)
  waiting for transfers between devices  10.6 us (13%)
  local copies, waits for them, and re-layouts  2.09 us (3%)
    all_to_all x3, starting transfers between devices, exchange(): return lax.all_to_all(blocks, axes, split_axis=0, concat_axis=0)  21.3 us
    pallas_call x13, Pallas kernels, kernel_call(): pl.pallas_call(body, out_shape=tuple(outs), in_specs=specs, out_specs=(pl...  17.9 us
    ppermute x2, starting transfers between devices, swap(): lax.ppermute(high, axis, forward)  12.9 us
    all_to_all x3, waiting for transfers between devices, exchange(): return lax.all_to_all(blocks, axes, split_axis=0, concat_axis=0)  9.51 us
    ppermute x1, starting transfers between devices, on_device(): lax.ppermute(relay, 'gy', [(i, (i + 1) % count_y) for i in range(count_y)])  7.47 us
    ppermute x2, starting transfers between devices, swap(): lax.ppermute(low, axis, backward)  6.7 us
    unnamed x24, local copies, waits for them, and re-layouts  2.09 us
  transfers between devices with their start and end apart: 8, of which 5 were waited for; matrix products, arithmetic and copies ran while one was open for 0% of the time, Pallas kernels for 16%

profile of v7, /device:TPU:1, one launch (start us, length us, event | category | flops | bytes accessed | tf_op | source)
XLA Modules:
  0.0 79.2 jit_solution(9942890241968489014)
XLA Ops:
  0.0 2.5 %shard_map.136 = (bf16[128,128]{1,0:T(8,128)(2,1)}, bf16[32,80,128]{2,1,0:T(8,128)(2,1)}) custom-call(bf16[128,128]{1,0:T(8,128)(2,1)} %refs_0_.1, bf16[128,128]{1,0:T(8,128)(2,1)} %refs_1_.1, bf16[128,128]{1,0:T(8,128)(2,1)} %refs_2_.1, s32[2,64]{1,0:T(2,128)} %send_ref.5, f32[3,128]{1,0:T(4,128)} %refs_4_.3, bf16[32,128]{1,0:T(8,128)(2,1)} %bitcast.11), custom_call_target="tpu_custom_call" | custom-call | flops 100000000 | bytes 796672 | tf_op jit(solution)/shard_map/pallas_call | solution.py:23
  2.5 10.4 %all-to-all-start = ((bf16[32,80,128]{2,1,0:T(8,128)(2,1)}), bf16[32,80,128]{2,1,0:T(8,128)(2,1)S(1)}, u32[]{:S(2)}, u32[]{:S(2)}) async-start(bf16[32,80,128]{2,1,0:T(8,128)(2,1)} %get-tuple-element.22), calls=%async_computation | async-start | bytes 1310720 | tf_op jit(solution)/shard_map/all_to_all | solution.py:291
  12.9 0.0 copy-start.8
  13.0 0.0 copy-start.11
  13.0 7.0 %shard_map.137 = (f32[448,128]{1,0:T(8,128)}, bf16[256,128]{1,0:T(8,128)(2,1)}, bf16[1024,128]{1,0:T(8,128)(2,1)}, bf16[1024,128]{1,0:T(8,128)(2,1)}, bf16[64,128,128]{2,1,0:T(8,128)(2,1)}) custom-call(f32[64,128]{1,0:T(8,128)} %bitcast.10, s32[64,128]{1,0:T(8,128)} %bitcast.6, s32[1,128]{1,0:T(1,128)} %bitcast.12, bf16[20,128]{1,0:T(8,128)(2,1)} %refs_3_.3, ...), custom_call_target="tpu_custom_call" | custom-call | flops 6000000000 | bytes 3021824 | tf_op jit(solution)/shard_map/pallas_call | solution.py:23
  19.9 0.0 copy-start.5
  19.9 0.8 %copy-done.5 = bf16[256,128]{1,0:T(8,128)(2,1)S(1)} copy-done((bf16[256,128]{1,0:T(8,128)(2,1)S(1)}, bf16[256,128]{1,0:T(8,128)(2,1)}, u32[]{:S(2)}) %copy-start.5) | copy-done | bytes 65560
  20.8 5.2 %all-to-all-done.first_ref = bf16[32,80,128]{2,1,0:T(8,128)(2,1)S(1)} async-done(((bf16[32,80,128]{2,1,0:T(8,128)(2,1)}), bf16[32,80,128]{2,1,0:T(8,128)(2,1)S(1)}, u32[]{:S(2)}, u32[]{:S(2)}) %all-to-all-start) | async-done | bytes 655392 | tf_op jit(solution)/shard_map/all_to_all | solution.py:291
  26.0 0.7 shard_map.139
  26.7 3.7 %all-to-all-start.1 = ((bf16[4,144,128]{2,1,0:T(8,128)(2,1)}), bf16[4,144,128]{2,1,0:T(8,128)(2,1)S(1)}, u32[]{:S(2)}, u32[]{:S(2)}) async-start(bf16[4,144,128]{2,1,0:T(8,128)(2,1)} %shard_map.139), calls=%async_computation.1 | async-start | bytes 294912 | tf_op jit(solution)/shard_map/all_to_all | solution.py:291
  30.3 0.0 copy-done.8
  30.3 0.0 copy-done.11
  30.4 0.0 copy-start.6
  30.4 0.3 shard_map.140
  30.7 0.0 copy-start.3
  30.7 0.0 copy-start.9
  30.7 0.0 copy-start.4
  30.7 1.2 %copy-done = bf16[64,128,128]{2,1,0:T(8,128)(2,1)S(1)} copy-done((bf16[64,128,128]{2,1,0:T(8,128)(2,1)S(1)}, bf16[64,128,128]{2,1,0:T(8,128)(2,1)}, u32[]{:S(2)}) %copy-start) | copy-done | bytes 2097176
  31.9 0.0 copy-done.6
  31.9 1.6 %shard_map.141.gathered_ref.sofar_ref = f32[128,128]{1,0:T(8,128)S(1)} custom-call(s32[64,128]{1,0:T(8,128)S(1)} %bitcast.7, bf16[64,128,128]{2,1,0:T(8,128)(2,1)S(1)} %copy-done, bf16[256,128]{1,0:T(8,128)(2,1)S(1)} %get-tuple-element.28.table_ref), custom_call_target="tpu_custom_call" | custom-call | flops 1000 | bytes 1000 | tf_op jit(solution)/shard_map/pallas_call | solution.py:23
  33.5 2.3 %all-to-all-done.1.third_ref = bf16[4,144,128]{2,1,0:T(8,128)(2,1)S(1)} async-done(((bf16[4,144,128]{2,1,0:T(8,128)(2,1)}), bf16[4,144,128]{2,1,0:T(8,128)(2,1)S(1)}, u32[]{:S(2)}, u32[]{:S(2)}) %all-to-all-start.1) | async-done | bytes 147488 | tf_op jit(solution)/shard_map/all_to_all | solution.py:291
  35.8 0.0 copy-done.3
  35.8 0.0 copy-done.9
  35.8 0.2 shard_map.142
  36.1 8.8 %collective-permute-start = (bf16[208,128]{1,0:T(8,128)(2,1)S(1)}, bf16[208,128]{1,0:T(8,128)(2,1)S(1)}, u32[]{:S(2)}, u32[]{:S(2)}) collective-permute-start(bf16[208,128]{1,0:T(8,128)(2,1)S(1)} %get-tuple-element.29), channel_id=1, source_target_pairs={{0,4},{4,8},{8,12},{12,0},{1,5},{5,9},{9,13},{13,1},{2,6},{6,10},{... | collective-permute-start | bytes 159752 | tf_op jit(solution)/shard_map/ppermute | solution.py:287
  44.9 3.7 %collective-permute-start.1 = (bf16[208,128]{1,0:T(8,128)(2,1)S(1)}, bf16[208,128]{1,0:T(8,128)(2,1)S(1)}, u32[]{:S(2)}, u32[]{:S(2)}) collective-permute-start(bf16[208,128]{1,0:T(8,128)(2,1)S(1)} %get-tuple-element.30), channel_id=1, source_target_pairs={{4,0},{8,4},{12,8},{0,12},{5,1},{9,5},{13,9},{1,13},{6,2},{10,6},{... | collective-permute-start | bytes 159752 | tf_op jit(solution)/shard_map/ppermute | solution.py:287
  48.6 0.0 collective-permute-done.above_ref.refs_0_.below_ref
  48.6 7.5 %collective-permute-start.2 = (bf16[16,128]{1,0:T(8,128)(2,1)S(1)}, bf16[16,128]{1,0:T(8,128)(2,1)S(1)}, u32[]{:S(2)}, u32[]{:S(2)}) collective-permute-start(bf16[16,128]{1,0:T(8,128)(2,1)S(1)} %shard_map.143), channel_id=1, source_target_pairs={{0,4},{4,8},{8,12},{12,0},{1,5},{5,9},{9,13},{13,1},{2,6},{6,10},{... | collective-permute-start | bytes 12296 | tf_op jit(solution)/shard_map/ppermute | solution.py:362
  56.1 0.0 collective-permute-done.1.refs_1_.above_ref
  56.1 0.8 collective-permute-done.2.refs_3_
  56.9 0.0 copy-done.4
  56.9 1.0 %shard_map.144 = (f32[128,128]{1,0:T(8,128)S(1)}, bf16[32,80,128]{2,1,0:T(8,128)(2,1)}) custom-call(bf16[208,128]{1,0:T(8,128)(2,1)S(1)} %collective-permute-done.above_ref.refs_0_.below_ref, bf16[208,128]{1,0:T(8,128)(2,1)S(1)} %collective-permute-done.1.refs_1_.above_ref, bf16[16,128]{1,0:T(8,128)(2,1)S(1)} %get-tuple-element.31.refs_2_, ...), custom_call_target="tpu_custom_call" | custom-call | flops 100000000 | bytes 1098496 | tf_op jit(solution)/shard_map/pallas_call | solution.py:23
  57.9 7.2 %all-to-all-start.2 = ((bf16[32,80,128]{2,1,0:T(8,128)(2,1)}), bf16[32,80,128]{2,1,0:T(8,128)(2,1)S(1)}, u32[]{:S(2)}, u32[]{:S(2)}) async-start(bf16[32,80,128]{2,1,0:T(8,128)(2,1)} %get-tuple-element.33), calls=%async_computation.2 | async-start | bytes 1310720 | tf_op jit(solution)/shard_map/all_to_all | solution.py:291
  65.1 0.4 shard_map.145
  65.5 4.1 %collective-permute-start.3 = (bf16[128,128]{1,0:T(8,128)(2,1)S(1)}, bf16[128,128]{1,0:T(8,128)(2,1)S(1)}, u32[]{:S(2)}, u32[]{:S(2)}) collective-permute-start(bf16[128,128]{1,0:T(8,128)(2,1)S(1)} %get-tuple-element.35), channel_id=1, source_target_pairs={{0,1},{1,2},{2,3},{3,0},{4,5},{5,6},{6,7},{7,4},{8,9},{9,10},{10,1... | collective-permute-start | bytes 98312 | tf_op jit(solution)/shard_map/ppermute | solution.py:287
  69.6 3.0 %collective-permute-start.4 = (bf16[128,128]{1,0:T(8,128)(2,1)S(1)}, bf16[128,128]{1,0:T(8,128)(2,1)S(1)}, u32[]{:S(2)}, u32[]{:S(2)}) collective-permute-start(bf16[128,128]{1,0:T(8,128)(2,1)S(1)} %get-tuple-element.36), channel_id=1, source_target_pairs={{1,0},{2,1},{3,2},{0,3},{5,4},{6,5},{7,6},{4,7},{9,8},{10,9},{11,1... | collective-permute-start | bytes 98312 | tf_op jit(solution)/shard_map/ppermute | solution.py:287
  72.6 1.6 %shard_map.146.sofar_ref = f32[128,128]{1,0:T(8,128)S(1)} custom-call(s32[64,128]{1,0:T(8,128)S(1)} %bitcast.8, bf16[64,128,128]{2,1,0:T(8,128)(2,1)S(1)} %copy-done, bf16[208,128]{1,0:T(8,128)(2,1)S(1)} %collective-permute-done.above_ref.refs_0_.below_ref, bf16[208,128]{1,0:T(8,128)(2,1)S(1)} %collective-permute-done.1.refs_1_.above_ref, ...), custom_call_target="tpu_custom_call" | custom-call | flops 2000000000 | bytes 2367488 | tf_op jit(solution)/shard_map/pallas_call | solution.py:23
  74.2 0.0 copy-start.1
  74.2 0.0 copy-start.2
  74.2 0.0 copy-start.7
  74.3 0.0 copy-start.10
  74.3 0.0 collective-permute-done.3.below_ref
  74.3 0.3 collective-permute-done.4.above_ref
  74.6 1.6 %shard_map.147.gathered_ref = f32[128,128]{1,0:T(8,128)S(1)} custom-call(s32[64,128]{1,0:T(8,128)S(1)} %bitcast.9, bf16[64,128,128]{2,1,0:T(8,128)(2,1)S(1)} %copy-done, bf16[128,128]{1,0:T(8,128)(2,1)S(1)} %collective-permute-done.3.below_ref, bf16[128,128]{1,0:T(8,128)(2,1)S(1)} %collective-permute-done.4.above_ref, f32[128,128]{1,0:T(8,128)S(1)} %shard_map.146.sofar_ref), custom_call_target="tpu_custom_call" | custom-call | flops 2000000000 | bytes 2326528 | tf_op jit(solution)/shard_map/pallas_call | solution.py:23
  76.1 2.0 %all-to-all-done.2.first_ref = bf16[32,80,128]{2,1,0:T(8,128)(2,1)S(1)} async-done(((bf16[32,80,128]{2,1,0:T(8,128)(2,1)}), bf16[32,80,128]{2,1,0:T(8,128)(2,1)S(1)}, u32[]{:S(2)}, u32[]{:S(2)}) %all-to-all-start.2) | async-done | bytes 655392 | tf_op jit(solution)/shard_map/all_to_all | solution.py:291
  78.2 0.0 copy-done.1
  78.2 0.0 copy-done.2
  78.2 1.1 %shard_map.148 = bf16[128,128]{1,0:T(8,128)(2,1)} custom-call(bf16[32,80,128]{2,1,0:T(8,128)(2,1)S(1)} %all-to-all-done.2.first_ref, f32[128,128]{1,0:T(8,128)S(1)} %get-tuple-element.34.order_ref.core_ref, s32[2,64]{1,0:T(2,128)S(1)} %copy-done.10, f32[128,128]{1,0:T(8,128)S(1)} %shard_map.147.gathered_ref, bf16[1024,128]{1,0:T(8,128)(2,1)S(1)} %copy-done.1, ...), custom_call_target="tpu_custom_call" | custom-call | flops 100000000 | bytes 1352192 | tf_op jit(solution)/shard_map/pallas_call | solution.py:23
  (5 shorter events, 0.0 us)
Async XLA Ops:
  2.5 23.5 %all-to-all-start = ((bf16[32,80,128]{2,1,0:T(8,128)(2,1)}), bf16[32,80,128]{2,1,0:T(8,128)(2,1)S(1)}, u32[]{:S(2)}, u32[]{:S(2)}) async-start(bf16[32,80,128]{2,1,0:T(8,128)(2,1)} %get-tuple-element.22), calls=%async_computation | async-start | bytes 1310720 | tf_op jit(solution)/shard_map/all_to_all | solution.py:291
  12.9 17.4 %copy-start.8 = (s32[2,96]{1,0:T(2,128)S(1)}, s32[2,96]{1,0:T(2,128)}, u32[]{:S(2)}) copy-start(s32[2,96]{1,0:T(2,128)} %refs_5_.1) | copy-start | bytes 2308
  13.0 17.4 %copy-start.11 = (bf16[128,128]{1,0:T(8,128)(2,1)S(1)}, bf16[128,128]{1,0:T(8,128)(2,1)}, u32[]{:S(2)}) copy-start(bf16[128,128]{1,0:T(8,128)(2,1)} %get-tuple-element.23.refs_5_.base_ref) | copy-start | bytes 98308
  19.9 0.8 %copy-start.5 = (bf16[256,128]{1,0:T(8,128)(2,1)S(1)}, bf16[256,128]{1,0:T(8,128)(2,1)}, u32[]{:S(2)}) copy-start(bf16[256,128]{1,0:T(8,128)(2,1)} %get-tuple-element.24.source_ref) | copy-start | bytes 196612
  26.7 9.1 %all-to-all-start.1 = ((bf16[4,144,128]{2,1,0:T(8,128)(2,1)}), bf16[4,144,128]{2,1,0:T(8,128)(2,1)S(1)}, u32[]{:S(2)}, u32[]{:S(2)}) async-start(bf16[4,144,128]{2,1,0:T(8,128)(2,1)} %shard_map.139), calls=%async_computation.1 | async-start | bytes 294912 | tf_op jit(solution)/shard_map/all_to_all | solution.py:291
  30.3 1.6 %copy-start = (bf16[64,128,128]{2,1,0:T(8,128)(2,1)S(1)}, bf16[64,128,128]{2,1,0:T(8,128)(2,1)}, u32[]{:S(2)}) copy-start(bf16[64,128,128]{2,1,0:T(8,128)(2,1)} %get-tuple-element.27.radial_ref) | copy-start | bytes 6291460
  30.4 1.6 %copy-start.6 = (s32[128,64]{0,1:T(8,128)S(1)}, s32[128,64]{0,1:T(8,128)}, u32[]{:S(2)}) copy-start(s32[128,64]{0,1:T(8,128)} %param.17) | copy-start | bytes 98308
  30.7 5.1 %copy-start.3 = (f32[448,128]{1,0:T(8,128)S(1)}, f32[448,128]{1,0:T(8,128)}, u32[]{:S(2)}) copy-start(f32[448,128]{1,0:T(8,128)} %get-tuple-element.26.core_ref) | copy-start | bytes 688132
  30.7 5.1 %copy-start.9 = (s32[2,128]{1,0:T(2,128)S(1)}, s32[2,128]{1,0:T(2,128)}, u32[]{:S(2)}) copy-start(s32[2,128]{1,0:T(2,128)} %send_ref.4) | copy-start | bytes 3076
  30.7 26.1 %copy-start.4 = (f32[1024,32]{0,1:T(8,128)S(1)}, f32[1024,32]{0,1:T(8,128)}, u32[]{:S(2)}) copy-start(f32[1024,32]{0,1:T(8,128)} %param.26) | copy-start | bytes 393220
  36.1 12.5 %collective-permute-start = (bf16[208,128]{1,0:T(8,128)(2,1)S(1)}, bf16[208,128]{1,0:T(8,128)(2,1)S(1)}, u32[]{:S(2)}, u32[]{:S(2)}) collective-permute-start(bf16[208,128]{1,0:T(8,128)(2,1)S(1)} %get-tuple-element.29), channel_id=1, source_target_pairs={{0,4},{4,8},{8,12},{12,0},{1,5},{5,9},{9,13},{13,1},{2,6},{6,10},{... | collective-permute-start | bytes 159752 | tf_op jit(solution)/shard_map/ppermute | solution.py:287
  44.9 11.2 %collective-permute-start.1 = (bf16[208,128]{1,0:T(8,128)(2,1)S(1)}, bf16[208,128]{1,0:T(8,128)(2,1)S(1)}, u32[]{:S(2)}, u32[]{:S(2)}) collective-permute-start(bf16[208,128]{1,0:T(8,128)(2,1)S(1)} %get-tuple-element.30), channel_id=1, source_target_pairs={{4,0},{8,4},{12,8},{0,12},{5,1},{9,5},{13,9},{1,13},{6,2},{10,6},{... | collective-permute-start | bytes 159752 | tf_op jit(solution)/shard_map/ppermute | solution.py:287
  48.6 8.3 %collective-permute-start.2 = (bf16[16,128]{1,0:T(8,128)(2,1)S(1)}, bf16[16,128]{1,0:T(8,128)(2,1)S(1)}, u32[]{:S(2)}, u32[]{:S(2)}) collective-permute-start(bf16[16,128]{1,0:T(8,128)(2,1)S(1)} %shard_map.143), channel_id=1, source_target_pairs={{0,4},{4,8},{8,12},{12,0},{1,5},{5,9},{9,13},{13,1},{2,6},{6,10},{... | collective-permute-start | bytes 12296 | tf_op jit(solution)/shard_map/ppermute | solution.py:362
  57.9 20.3 %all-to-all-start.2 = ((bf16[32,80,128]{2,1,0:T(8,128)(2,1)}), bf16[32,80,128]{2,1,0:T(8,128)(2,1)S(1)}, u32[]{:S(2)}, u32[]{:S(2)}) async-start(bf16[32,80,128]{2,1,0:T(8,128)(2,1)} %get-tuple-element.33), calls=%async_computation.2 | async-start | bytes 1310720 | tf_op jit(solution)/shard_map/all_to_all | solution.py:291
  65.5 8.7 %collective-permute-start.3 = (bf16[128,128]{1,0:T(8,128)(2,1)S(1)}, bf16[128,128]{1,0:T(8,128)(2,1)S(1)}, u32[]{:S(2)}, u32[]{:S(2)}) collective-permute-start(bf16[128,128]{1,0:T(8,128)(2,1)S(1)} %get-tuple-element.35), channel_id=1, source_target_pairs={{0,1},{1,2},{2,3},{3,0},{4,5},{5,6},{6,7},{7,4},{8,9},{9,10},{10,1... | collective-permute-start | bytes 98312 | tf_op jit(solution)/shard_map/ppermute | solution.py:287
  69.6 5.0 %collective-permute-start.4 = (bf16[128,128]{1,0:T(8,128)(2,1)S(1)}, bf16[128,128]{1,0:T(8,128)(2,1)S(1)}, u32[]{:S(2)}, u32[]{:S(2)}) collective-permute-start(bf16[128,128]{1,0:T(8,128)(2,1)S(1)} %get-tuple-element.36), channel_id=1, source_target_pairs={{1,0},{2,1},{3,2},{0,3},{5,4},{6,5},{7,6},{4,7},{9,8},{10,9},{11,1... | collective-permute-start | bytes 98312 | tf_op jit(solution)/shard_map/ppermute | solution.py:287
  74.2 4.0 %copy-start.1 = (bf16[1024,128]{1,0:T(8,128)(2,1)S(1)}, bf16[1024,128]{1,0:T(8,128)(2,1)}, u32[]{:S(2)}) copy-start(bf16[1024,128]{1,0:T(8,128)(2,1)} %get-tuple-element.37.cos_ref) | copy-start | bytes 786436
  74.2 3.9 %copy-start.2 = (bf16[1024,128]{1,0:T(8,128)(2,1)S(1)}, bf16[1024,128]{1,0:T(8,128)(2,1)}, u32[]{:S(2)}) copy-start(bf16[1024,128]{1,0:T(8,128)(2,1)} %get-tuple-element.38.sin_ref) | copy-start | bytes 786436
  74.2 3.9 %copy-start.7 = (bf16[32,128]{1,0:T(8,128)(2,1)S(1)}, bf16[32,128]{1,0:T(8,128)(2,1)}, u32[]{:S(2)}) copy-start(bf16[32,128]{1,0:T(8,128)(2,1)} %ewald_ref.1) | copy-start | bytes 24580
  74.3 3.9 %copy-start.10 = (s32[2,64]{1,0:T(2,128)S(1)}, s32[2,64]{1,0:T(2,128)}, u32[]{:S(2)}) copy-start(s32[2,64]{1,0:T(2,128)} %send_ref.5) | copy-start | bytes 1540
